TPU v7x, 32 devices: a whole 2x2x4 slice. The times are simulated.
32 devices in a mesh: grp: 2 (over y), row: 8 (over z, x), key: 2 (over core).
Axes of the slice: x: 2, y: 2, z: 4, core: 2. Of those that a mesh axis runs over, the one named last changes fastest.
Arguments:
- query: bfloat16 [32, 768, 128], P(('grp', 'row'), 'key'), parts along dimension 0, may hold values from -8 to 8
- keys: bfloat16 [32, 768, 128], P(('grp', 'row'), 'key'), parts along dimension 0, may hold values from -8 to 8
- values: bfloat16 [32, 768, 128], P(('grp', 'row'), 'key'), parts along dimension 0, may hold values from -6 to 6
- gate_logits: bfloat16 [32, 768, 128], P(('grp', 'row'), 'key'), parts along dimension 0, may hold values from -8 to 8
- pair_bias: bfloat16 [4, 1536, 768], P(None, ('grp', 'row'), 'key'), parts along dimension 1, may hold values from -6 to 6
- key_mask: int32 [1536], P(('grp', 'key')), parts along dimension 0, may hold values 0 or 1
- grad_out: bfloat16 [32, 768, 128], P(('grp', 'row'), 'key'), parts along dimension 0, may hold values from -6 to 6
Outputs:
- grad_query: bfloat16 [32, 768, 128], P(('grp', 'row'), 'key'), parts along dimension 0
- grad_keys: bfloat16 [32, 768, 128], P(('grp', 'row'), 'key'), parts along dimension 0
- grad_values: bfloat16 [32, 768, 128], P(('grp', 'row'), 'key'), parts along dimension 0
- grad_gate: bfloat16 [32, 768, 128], P(('grp', 'row'), 'key'), parts along dimension 0
- grad_bias: float32 [4, 1536, 768], P(None, ('grp', 'row'), 'key'), parts along dimension 1
There are 2 independent parts, one for each index of `grp`. A program takes and returns all parts, laid end to end along the dimension named above; each array names one. Nothing has to cross between parts.
All inputs are finite; a program needn't handle non-finite values. No bound on the sum of `key_mask` on one device may be relied on, other than what follows from the above.
Results may differ from a plain program's by a relative error of at most 0.024.
Values may be sent and summed in bfloat16 or wider, within the bound.
No kernel may reach another device: no remote copies, remote signals or barrier semaphores. Data moves between devices by JAX's collectives and lax.ppermute only.
A program may use at most 64 MiB of HBM per device.

v0:
```python
import functools
import math

import jax
import jax.numpy as jnp
from jax import lax
from jax.experimental import pallas as pl
from jax.experimental.pallas import tpu as pltpu
from jax.sharding import PartitionSpec as P

PAIR = 2
NEAR_PARTS = 2
ROWS_AT_ONCE = 16
VMEM = pltpu.VMEM
PARAMS = pltpu.CompilerParams(vmem_limit_bytes=32 * 1024 * 1024)
PRE_PARAMS = pltpu.CompilerParams(vmem_limit_bytes=60 * 1024 * 1024)


def places():
    near = lax.axis_index("near") * PAIR + lax.axis_index("side")
    return lax.axis_index("far") * PAIR * PAIR + near, near, lax.axis_index("key")


def fetch(pairs, sems):
    copies = [pltpu.make_async_copy(ref, buffer, sems.at[i]) for i, (ref, buffer) in enumerate(pairs)]
    for copy in copies:
        copy.start()
    for copy in copies:
        copy.wait()


def slab_kernel(bias, *slabs):
    near = places()[1]
    for s in range(4):
        slabs[s][...] = bias[near ^ s]


def make_slabs(bias):
    return pl.pallas_call(
        slab_kernel,
        out_shape=[jax.ShapeDtypeStruct(bias.shape[1:], jnp.bfloat16)] * 4,
        compiler_params=PARAMS,
        name="bias_by_head",
    )(bias)


def pack_kernel(*refs):
    inputs, packs, kept, buffers, (sems, held) = refs[:5], refs[5:8], refs[8:10], refs[10:15], refs[15:]
    fetch(list(zip(inputs, buffers)), sems)
    query, keys, values, gate, cot = buffers
    rows = query.shape[0]
    size = query.shape[2] // 4
    _, near, core = places()
    for r in range(rows):
        upstream = (cot[r].astype(jnp.float32) * jax.nn.sigmoid(gate[r].astype(jnp.float32))).astype(jnp.bfloat16)
        whole = [query[r], keys[r], values[r], upstream]
        for head in range(4):
            held[head, r] = jnp.concatenate([one[:, head * size : (head + 1) * size] for one in whole], axis=1)
    for i in range(2):
        for s in range(1, 4):
            packs[s - 1][i] = held[near ^ s, core ^ i]
        kept[i][...] = held[near, core ^ i]


def make_packs(*inputs):
    one = inputs[0]
    return pl.pallas_call(
        pack_kernel,
        in_specs=[pl.BlockSpec(memory_space=pl.ANY)] * 5,
        out_shape=[jax.ShapeDtypeStruct(one.shape, jnp.bfloat16)] * 3
        + [jax.ShapeDtypeStruct(one.shape[1:], jnp.bfloat16)] * 2,
        scratch_shapes=[VMEM(one.shape, jnp.bfloat16)] * 5
        + [pltpu.SemaphoreType.DMA((5,)), VMEM((4,) + one.shape, jnp.bfloat16)],
        compiler_params=PRE_PARAMS,
        name="pack",
    )(*inputs)


NT = (((1,), (1,)), ((), ()))


def dot(a, b, dims=(((1,), (0,)), ((), ()))):
    return lax.dot_general(a, b, dims, preferred_element_type=jnp.float32)


def main_kernel(scaling, size, start, relative, begun, ended, opened, closed, split, *refs):
    packs, swapped, (mine, other), refs = refs[:2], refs[2:4], refs[4:6], refs[6:]
    earlier, refs = refs[: 4 if begun else 0], refs[4 if begun else 0 :]
    before, refs = refs[: 1 if opened else 0], refs[1 if opened else 0 :]
    d_bias, refs = refs[: 2 if closed else 1], refs[2 if closed else 1 :]
    results, refs = refs[: 2 + split if ended else 4], refs[2 + split if ended else 4 :]
    q_all, d_all, k_of, v_of, dk_t, dv_t, att_all, dq_all, bias_wide, q_now, d_now, s_now, p_now, low_now, d_low_now, bias_sum = refs
    step = pl.program_id(0)
    chip, _, core = places()
    parts, (half, _) = len(packs), packs[0].shape
    blocks, own, _ = mine.shape
    lanes = parts * size

    def side(i):
        return pl.ds(pl.multiple_of((core ^ i) * half, half), half)

    @pl.when(step == 0)
    def _():
        lane = lax.broadcasted_iota(jnp.int32, (half, lanes), 1) // size
        for i in range(2):
            here = [(swapped if i else packs)[p][...] for p in range(parts)]
            q, k, v, d = [
                jnp.concatenate([one[:, j * size : (j + 1) * size] for one in here], axis=1) for j in range(4)
            ]
            q_all[side(i)], d_all[side(i)] = q, d
            rows = slice(i * half, (i + 1) * half)
            for r in range(parts):
                k_of[r, rows] = jnp.where(lane == r, k, 0)
                v_of[r, rows] = jnp.where(lane == r, v, 0)
        for i, ref in enumerate((att_all, dq_all, dk_t, dv_t)):
            ref[...] = earlier[i][...] if begun else jnp.zeros_like(ref)

    def strip(i):
        at = start + step * blocks + i
        at = chip ^ at if relative else at
        return pl.ds(pl.multiple_of(at * own, own), own)

    for i in range(blocks):
        rows = slice(i * own, (i + 1) * own)
        bias_wide[rows, :half] = mine[i].astype(jnp.float32)
        bias_wide[rows, half:] = other[i].astype(jnp.float32)
        q_now[rows], d_now[rows] = q_all[strip(i)], d_all[strip(i)]
    q, d = q_now[...], d_now[...]
    q_t = q.astype(jnp.float32).T.astype(jnp.bfloat16)
    d_t = d.astype(jnp.float32).T.astype(jnp.bfloat16)

    def scores(r):
        s_now[r % 2] = dot(q, k_of[r], NT)
        p_now[r % 2] = dot(d, v_of[r], NT)

    att_sum, dq_sum = None, None
    scores(0)
    for r in range(parts):
        if r + 1 < parts:
            scores(r + 1)
        for at in range(0, blocks * own, ROWS_AT_ONCE):
            rows = slice(at, at + ROWS_AT_ONCE)
            logits = s_now[r % 2, rows] * scaling + bias_wide[rows]
            expo = jnp.exp(logits - jnp.max(logits, axis=-1, keepdims=True))
            probs = expo * (1.0 / jnp.sum(expo, axis=-1, keepdims=True))
            d_probs = p_now[r % 2, rows]
            inner = jnp.sum(probs * d_probs, axis=-1, keepdims=True)
            d_logits = probs * (d_probs - inner)
            low_now[r % 2, rows] = probs.astype(jnp.bfloat16)
            d_low_now[r % 2, rows] = d_logits.astype(jnp.bfloat16)
            if r:
                d_logits = bias_sum[rows] + d_logits
            elif opened:
                d_logits = before[0][rows] + d_logits
            bias_sum[rows] = d_logits
        low, d_low = low_now[r % 2], d_low_now[r % 2]
        att, dq = dot(low, v_of[r]), dot(d_low, k_of[r])
        cut = slice(r * size, (r + 1) * size)
        dk_t[cut] += dot(q_t[cut], d_low)
        dv_t[cut] += dot(d_t[cut], low)
        att_sum = att if r == 0 else att_sum + att
        dq_sum = dq if r == 0 else dq_sum + dq
    att_low, dq_low = att_sum.astype(jnp.bfloat16), (dq_sum * scaling).astype(jnp.bfloat16)
    for i in range(blocks):
        rows = slice(i * own, (i + 1) * own)
        att_all[strip(i)], dq_all[strip(i)] = att_low[rows], dq_low[rows]
        if closed:
            d_bias[0][i] = bias_sum[rows, :half].astype(jnp.bfloat16)
            d_bias[1][i] = bias_sum[rows, half:].astype(jnp.bfloat16)
    if not closed:
        d_bias[0][...] = bias_sum[...]

    @pl.when(step == pl.num_programs(0) - 1)
    def _():
        if not ended:
            for ref, value in zip(results, (att_all, dq_all, dk_t, dv_t)):
                ref[...] = value[...]
            return
        dk = (dk_t[...] * scaling).T.astype(jnp.bfloat16)
        dv = dv_t[...].T.astype(jnp.bfloat16)
        for i in range(2):
            rows = slice(i * half, (i + 1) * half)
            whole = [att_all[side(i)], dq_all[side(i)], dk[rows], dv[rows]]
            for p in range(parts):
                pack = jnp.concatenate([one[:, p * size : (p + 1) * size] for one in whole], axis=1)
                if split and p == 0:
                    results[i][...] = pack
                else:
                    results[p + split][i] = pack


def fixed(value):
    return pl.BlockSpec(value.shape, lambda i: (0,) * len(value.shape))


def main(packs, swapped, mine, other, earlier, before, scaling, size, start, relative, ended, closed, split):
    parts, (half, width) = len(packs), swapped[0].shape
    strips, own, _ = mine.shape
    blocks, lanes = 4, parts * size
    key_count = queries = 2 * half
    rows = jax.ShapeDtypeStruct((queries, lanes), jnp.bfloat16)
    turned = jax.ShapeDtypeStruct((lanes, key_count), jnp.float32)
    wide = jax.ShapeDtypeStruct((strips * own, key_count), jnp.float32)
    strip = pl.BlockSpec((blocks, own, half), lambda i: (i, 0, 0))
    wide_strip = pl.BlockSpec((blocks * own, key_count), lambda i: (i, 0))
    now = VMEM((blocks * own, lanes), jnp.bfloat16)
    results = [rows, rows, turned, turned]
    if ended:
        ours = [jax.ShapeDtypeStruct((half, width), jnp.bfloat16)] * 2
        results = [jax.ShapeDtypeStruct((2, half, width), jnp.bfloat16)] * (parts - split)
        results = ours * split + results
    d_bias = [mine, other] if closed else [wide]
    return pl.pallas_call(
        functools.partial(main_kernel, scaling, size, start, relative, bool(earlier), ended, bool(before), closed, split),
        grid=(strips // blocks,),
        in_specs=[fixed(one) for one in [*packs, *swapped]]
        + [strip, strip]
        + [fixed(one) for one in earlier]
        + [wide_strip] * len(before),
        out_specs=([strip] * 2 if closed else [wide_strip]) + [fixed(one) for one in results],
        out_shape=[jax.ShapeDtypeStruct(one.shape, one.dtype) for one in d_bias + results],
        scratch_shapes=[
            VMEM(rows.shape, jnp.bfloat16),
            VMEM(rows.shape, jnp.bfloat16),
            VMEM((parts, key_count, lanes), jnp.bfloat16),
            VMEM((parts, key_count, lanes), jnp.bfloat16),
            VMEM(turned.shape, jnp.float32),
            VMEM(turned.shape, jnp.float32),
            VMEM(rows.shape, jnp.bfloat16),
            VMEM(rows.shape, jnp.bfloat16),
            VMEM((blocks * own, key_count), jnp.float32),
            now,
            now,
            VMEM((2, blocks * own, key_count), jnp.float32),
            VMEM((2, blocks * own, key_count), jnp.float32),
            VMEM((2, blocks * own, key_count), jnp.bfloat16),
            VMEM((2, blocks * own, key_count), jnp.bfloat16),
            VMEM((blocks * own, key_count), jnp.float32),
        ],
        compiler_params=PARAMS,
        cost_estimate=pl.CostEstimate(flops=1, bytes_accessed=1, transcendentals=0),
        name="attention",
    )(*packs, *swapped, mine, other, *earlier, *before)


def post_kernel(gate, cot, packs, swapped, d_query, d_keys, d_values, d_gate, held):
    rows, half, channels = gate.shape
    size = channels // 4
    _, near, core = places()
    for s in range(4):
        held[near ^ s, core] = packs[s]
        held[near ^ s, 1 - core] = swapped[s]
    for r in range(rows):
        full = []
        for j in range(4):
            full.append(jnp.concatenate([held[h, r, :, j * size : (j + 1) * size] for h in range(4)], axis=1))
        d_query[r], d_keys[r], d_values[r] = full[1], full[2], full[3]
        sig = jax.nn.sigmoid(gate[r].astype(jnp.float32))
        d_gate[r] = (cot[r].astype(jnp.float32) * full[0].astype(jnp.float32) * sig * (1.0 - sig)).astype(jnp.bfloat16)


def post(gate, cot, packs, swapped):
    return pl.pallas_call(
        post_kernel,
        out_shape=[jax.ShapeDtypeStruct(gate.shape, jnp.bfloat16)] * 4,
        scratch_shapes=[VMEM((4,) + gate.shape, jnp.bfloat16)],
        compiler_params=PARAMS,
        name="unpack",
    )(gate, cot, packs, swapped)


def bias_kernel(*refs):
    near = places()[1]
    for s in range(4):
        refs[4][near ^ s] = refs[s][...].astype(jnp.float32)


def bias_out(pieces):
    return pl.pallas_call(
        bias_kernel,
        out_shape=jax.ShapeDtypeStruct((4,) + pieces[0].shape, jnp.float32),
        compiler_params=PARAMS,
        name="bias_grad",
    )(*pieces)


def shards(query, keys, values, gate_logits, pair_bias, key_mask, grad_out):
    rows, half, channels = query.shape
    heads, own, _ = pair_bias.shape
    size = channels // heads
    scaling = 1.0 / math.sqrt(size)
    far, cores = lax.axis_size("far"), lax.axis_size("key")
    chips = far * PAIR * PAIR
    assert PAIR * PAIR == heads == 4 and rows == cores == 2
    relative = own % 16 == 0
    chip = places()[0]

    def swap(value, axes, s, count):
        return lax.ppermute(value, axes, [(i, i ^ s) for i in range(count)]) if s else value

    def near_swap(value, s):
        return swap(value, ("near", "side"), s, 4)

    def far_swap(value, s):
        return swap(value, "far", s, far)

    def other_core(value):
        return swap(value, "key", 1, 2)

    def wide(value):
        return value.astype(jnp.float32)

    slabs = make_slabs(pair_bias)
    strips = jnp.stack([near_swap(slabs[s], s) for s in range(4)])
    strips = jnp.where(key_mask == 1, strips, jnp.bfloat16(-1000000000.0))
    groups = [far_swap(strips, f) for f in range(far)]
    *packs, kept, spare = make_packs(query, keys, values, gate_logits, grad_out)
    packs = [near_swap(packs[s], s + 1) for s in range(3)]
    starts = [f * 4 for f in range(far)]
    if not relative:
        starts, groups = [0], [jnp.concatenate(groups)[chip ^ jnp.arange(chips)].reshape(8, -1, half)]
    others = [jnp.concatenate([other_core(part) for part in jnp.split(groups[0], NEAR_PARTS)])] + [None] * (len(starts) - 1)
    orders = [list(range(len(starts))), list(range(len(starts)))[::-1]]
    before, sums, returned = [[]] * len(starts), [None] * len(starts), []
    for a, order in enumerate(orders):
        ours = [packs[0]] if a == 0 else packs[1:]
        if a:
            ours = list(lax.optimization_barrier((*ours, before[0][0]))[:2])
        swapped = [other_core(pack[1]) for pack in ours]
        ours = [pack[0] for pack in ours]
        if a == 0:
            spare = lax.optimization_barrier((spare, ours[0]))[0]
            ours, swapped = [kept] + ours, [other_core(spare)] + swapped
        earlier = []
        for g in order:
            if others[g] is None:
                groups[g] = lax.optimization_barrier((groups[g], before[0][0]))[0]
                others[g] = other_core(groups[g])
            mine, closed, ended = groups[g], a == len(orders) - 1, g == order[-1]
            if closed and g != order[0]:
                mine, last = lax.optimization_barrier((mine, sums[order[order.index(g) - 1]]))
                sums[order[order.index(g) - 1]] = last
            out = main(
                ours, swapped, mine, others[g], earlier, before[g], scaling, size, starts[g], relative, ended, closed, 1 - a
            )
            if not closed:
                before[g], earlier = out[:1], out[1:]
                continue
            d_mine, d_other, *earlier = out
            d_mine = wide(d_mine)
            if ended and relative:
                for f in range(1, far):
                    d_mine = d_mine + wide(far_swap(sums[f], f))
                d_mine = lax.optimization_barrier(d_mine)
            sums[g] = (d_mine + wide(other_core(d_other))).astype(jnp.bfloat16)
        if a == 0:
            stay, pass_on, *earlier = earlier
        returned += [near_swap(value, len(returned) + i + 1) for i, value in enumerate(earlier)]
    d_sum = sums[0]
    if not relative:
        d_sum = d_sum.reshape(chips, own, half)[chip ^ jnp.arange(chips)]
        total = wide(d_sum[:4])
        for f in range(1, far):
            total = total + wide(far_swap(d_sum[4 * f : 4 * f + 4], f))
        d_sum = total.astype(jnp.bfloat16)
    pieces = [near_swap(d_sum[s], s) for s in range(4)]
    returned = lax.optimization_barrier((*returned, *pieces))[:3]
    swapped = other_core(jnp.stack([pass_on] + [pack[1] for pack in returned]))
    packs = jnp.stack([stay] + [pack[0] for pack in returned])
    return (*post(gate_logits, grad_out, packs, swapped), bias_out(pieces))


def solution(mesh):
    groups, rows, cores = mesh.devices.shape
    devices = mesh.devices.reshape(groups, rows // PAIR**2, PAIR, PAIR, cores)
    mesh = jax.sharding.Mesh(devices, ("grp", "far", "near", "side", "key"))
    split = ("grp", "far", "near", "side")
    tokens = P(split, "key", None)
    pair = P(None, split, "key")
    in_specs = (tokens, tokens, tokens, tokens, pair, P(("grp", "key")), tokens)
    out_specs = (tokens, tokens, tokens, tokens, pair)
    return jax.shard_map(shards, mesh=mesh, in_specs=in_specs, out_specs=out_specs, check_vma=False)
```

profile of v0, /device:TPU:0, one launch (start us, length us, event | category | flops | bytes accessed | tf_op | source)
XLA Modules:
  0.0 66.9 jit_solution(16900973083571129550)
XLA Ops:
  0.6 1.0 %copy-done.3 = bf16[4,96,384]{2,1,0:T(8,128)(2,1)S(1)} copy-done((bf16[4,96,384]{2,1,0:T(8,128)(2,1)S(1)}, bf16[4,96,384]{2,1,0:T(8,128)(2,1)}, u32[]{:S(2)}) %copy-start.3) | copy-done | bytes 294936
  1.6 3.0 %collective-permute-start.3 = (bf16[96,384]{1,0:T(8,128)(2,1)S(1)}, bf16[96,384]{1,0:T(8,128)(2,1)S(1)}, u32[]{:S(2)}, u32[]{:S(2)}) collective-permute-start(bf16[96,384]{1,0:T(8,128)(2,1)S(1)} %get-tuple-element.51), channel_id=1, source_target_pairs={{0,2},{2,0},{4,6},{6,4},{1,3},{3,1},{5,7},{7,5},{8,10},{10,8},{12,... | collective-permute-start | bytes 221192 | tf_op jit(solution)/shard_map/ppermute | solution.py:299
  4.6 1.6 %collective-permute-start.4 = (bf16[96,384]{1,0:T(8,128)(2,1)S(1)}, bf16[96,384]{1,0:T(8,128)(2,1)S(1)}, u32[]{:S(2)}, u32[]{:S(2)}) collective-permute-start(bf16[96,384]{1,0:T(8,128)(2,1)S(1)} %get-tuple-element.52), channel_id=1, source_target_pairs={{0,4},{2,6},{4,0},{6,2},{1,5},{3,7},{5,1},{7,3},{8,12},{10,14},{12... | collective-permute-start | bytes 221192 | tf_op jit(solution)/shard_map/ppermute | solution.py:299
  6.2 2.9 %pack.1 = (bf16[2,384,128]{2,1,0:T(8,128)(2,1)}, bf16[2,384,128]{2,1,0:T(8,128)(2,1)}, bf16[2,384,128]{2,1,0:T(8,128)(2,1)}, bf16[384,128]{1,0:T(8,128)(2,1)}, bf16[384,128]{1,0:T(8,128)(2,1)}) custom-call(bf16[2,384,128]{2,1,0:T(8,128)(2,1)} %refs_0_.1, bf16[2,384,128]{2,1,0:T(8,128)(2,1)} %refs_1_.1, bf16[2,384,128]{2,1,0:T(8,128)(2,1)} %refs_2_.1, ...), custom_call_target="tpu_custom_call" | custom-call | tf_op jit(solution)/shard_map/pack/pallas_call | solution.py:67
  9.1 2.0 %collective-permute-start = (bf16[2,384,128]{2,1,0:T(8,128)(2,1)}, bf16[2,384,128]{2,1,0:T(8,128)(2,1)S(1)}, u32[]{:S(2)}, u32[]{:S(2)}) collective-permute-start(bf16[2,384,128]{2,1,0:T(8,128)(2,1)} %get-tuple-element.47), channel_id=1, source_target_pairs={{0,2},{2,0},{4,6},{6,4},{1,3},{3,1},{5,7},{7,5},{8,10},{10,8},{12,... | collective-permute-start | bytes 589832 | tf_op jit(solution)/shard_map/ppermute | solution.py:299
  11.1 1.6 %collective-permute-start.11 = (bf16[2,384,128]{2,1,0:T(8,128)(2,1)}, bf16[2,384,128]{2,1,0:T(8,128)(2,1)S(1)}, u32[]{:S(2)}, u32[]{:S(2)}) collective-permute-start(bf16[2,384,128]{2,1,0:T(8,128)(2,1)} %get-tuple-element.62), channel_id=1, source_target_pairs={{0,4},{2,6},{4,0},{6,2},{1,5},{3,7},{5,1},{7,3},{8,12},{10,14},{12... | collective-permute-start | bytes 589832 | tf_op jit(solution)/shard_map/ppermute | solution.py:299
  12.9 3.0 %collective-permute-start.6 = (bf16[4,96,384]{2,1,0:T(8,128)(2,1)S(1)}, bf16[4,96,384]{2,1,0:T(8,128)(2,1)S(1)}, u32[]{:S(2)}, u32[]{:S(2)}) collective-permute-start(bf16[4,96,384]{2,1,0:T(8,128)(2,1)S(1)} %maximum_select_fusion.refs_4_), channel_id=1, source_target_pairs={{0,8},{8,0},{1,9},{9,1},{2,10},{10,2},{3,11},{11,3},{4,12},{12,4},... | collective-permute-start | bytes 884744 | tf_op jit(solution)/shard_map/ppermute | solution.py:299
  16.5 1.1 %collective-permute-done.7 = bf16[2,96,384]{2,1,0:T(8,128)(2,1)S(1)} collective-permute-done((bf16[2,96,384]{2,1,0:T(8,128)(2,1)S(1)}, bf16[2,96,384]{2,1,0:T(8,128)(2,1)S(1)}, u32[]{:S(2)}, u32[]{:S(2)}) %collective-permute-start.7) | collective-permute-done | bytes 147488 | tf_op jit(solution)/shard_map/ppermute | solution.py:299
  18.2 0.7 collective-permute-done.1.refs_2_
  18.9 0.4 collective-permute-done.2.refs_3_
  19.3 2.7 %attention.4 = (f32[384,768]{1,0:T(8,128)S(1)}, bf16[768,64]{1,0:T(8,128)(2,1)S(1)}, bf16[768,64]{1,0:T(8,128)(2,1)S(1)}, f32[64,768]{1,0:T(8,128)S(1)}, f32[64,768]{1,0:T(8,128)S(1)}) custom-call(bf16[384,128]{1,0:T(8,128)(2,1)S(1)} %copy-done.2, bf16[384,128]{1,0:T(8,128)(2,1)S(1)} %get-tuple-element.104.refs_1_, ...), custom_call_target="tpu_custom_call" | custom-call | flops 1 | bytes 1 | tf_op jit(solution)/shard_map/attention/pallas_call | solution.py:213
  22.0 3.2 %collective-permute-done.11 = bf16[2,384,128]{2,1,0:T(8,128)(2,1)S(1)} collective-permute-done((bf16[2,384,128]{2,1,0:T(8,128)(2,1)}, bf16[2,384,128]{2,1,0:T(8,128)(2,1)S(1)}, u32[]{:S(2)}, u32[]{:S(2)}) %collective-permute-start.11) | collective-permute-done | bytes 196640 | tf_op jit(solution)/shard_map/ppermute | solution.py:299
  25.2 1.9 %collective-permute-done.12 = bf16[2,384,128]{2,1,0:T(8,128)(2,1)S(1)} collective-permute-done((bf16[2,384,128]{2,1,0:T(8,128)(2,1)}, bf16[2,384,128]{2,1,0:T(8,128)(2,1)S(1)}, u32[]{:S(2)}, u32[]{:S(2)}) %collective-permute-start.12) | collective-permute-done | bytes 196640 | tf_op jit(solution)/shard_map/ppermute | solution.py:299
  27.3 0.5 collective-permute-start.9
  28.0 1.0 %collective-permute-done.9.refs_5_ = bf16[4,96,384]{2,1,0:T(8,128)(2,1)S(1)} collective-permute-done((bf16[4,96,384]{2,1,0:T(8,128)(2,1)S(1)}, bf16[4,96,384]{2,1,0:T(8,128)(2,1)S(1)}, u32[]{:S(2)}, u32[]{:S(2)}) %collective-permute-start.9) | collective-permute-done | bytes 294944 | tf_op jit(solution)/shard_map/ppermute | solution.py:299
  29.0 2.8 %attention.5 = (f32[384,768]{1,0:T(8,128)S(1)}, bf16[384,128]{1,0:T(8,128)(2,1)S(1)}, bf16[384,128]{1,0:T(8,128)(2,1)S(1)}, bf16[2,384,128]{2,1,0:T(8,128)(2,1)S(1)}) custom-call(bf16[384,128]{1,0:T(8,128)(2,1)S(1)} %copy-done.2, bf16[384,128]{1,0:T(8,128)(2,1)S(1)} %get-tuple-element.104.refs_1_, bf16[384,128]{1,0:T(8,128)(2,1)S(1)} %collective-permute-done.1.refs_2_, ...), custom_call_target="tpu_custom_call" | custom-call | flops 1 | bytes 1 | tf_op jit(solution)/shard_map/attention/pallas_call | solution.py:213
  31.9 2.8 %attention.6 = (bf16[4,96,384]{2,1,0:T(8,128)(2,1)S(1)}, bf16[4,96,384]{2,1,0:T(8,128)(2,1)S(1)}, bf16[768,64]{1,0:T(8,128)(2,1)S(1)}, bf16[768,64]{1,0:T(8,128)...) custom-call(bf16[384,128]{1,0:T(8,128)(2,1)S(1)} %get-tuple-element.102.refs_0_, ...), custom_call_target="tpu_custom_call" | custom-call | flops 1 | bytes 1 | tf_op jit(solution)/shard_map/attention/pallas_call | solution.py:213
  34.6 0.4 collective-permute-start.15
  35.1 1.2 %collective-permute-done.15 = bf16[4,96,384]{2,1,0:T(8,128)(2,1)S(1)} collective-permute-done((bf16[4,96,384]{2,1,0:T(8,128)(2,1)S(1)}, bf16[4,96,384]{2,1,0:T(8,128)(2,1)S(1)}, u32[]{:S(2)}, u32[]{:S(2)}) %collective-permute-start.15) | collective-permute-done | bytes 294944 | tf_op jit(solution)/shard_map/ppermute | solution.py:299
  36.4 2.6 %collective-permute-start.18 = (bf16[4,96,384]{2,1,0:T(8,128)(2,1)S(1)}, bf16[4,96,384]{2,1,0:T(8,128)(2,1)S(1)}, u32[]{:S(2)}, u32[]{:S(2)}) collective-permute-start(bf16[4,96,384]{2,1,0:T(8,128)(2,1)S(1)} %add_convert_fusion.1), channel_id=1, source_target_pairs={{0,8},{8,0},{1,9},{9,1},{2,10},{10,2},{3,11},{11,3},{4,12},{12,4},... | collective-permute-start | bytes 884744 | tf_op jit(solution)/shard_map/ppermute | solution.py:299
  38.9 3.1 %attention.7 = (bf16[4,96,384]{2,1,0:T(8,128)(2,1)S(1)}, bf16[4,96,384]{2,1,0:T(8,128)(2,1)S(1)}, bf16[2,384,128]{2,1,0:T(8,128)(2,1)S(1)}, bf16[2,384,128]{2,1,0:T(8,128)(2,1)S(1)}) custom-call(bf16[384,128]{1,0:T(8,128)(2,1)S(1)} %get-tuple-element.102.refs_0_, bf16[384,128]{1,0:T(8,128)(2,1)S(1)} %get-tuple-element.100.refs_1_, ...), custom_call_target="tpu_custom_call" | custom-call | flops 1 | bytes 1 | tf_op jit(solution)/shard_map/attention/pallas_call | solution.py:213
  42.1 0.6 collective-permute-start.10
  42.7 2.8 %collective-permute-start.16 = (bf16[2,384,128]{2,1,0:T(8,128)(2,1)S(1)}, bf16[2,384,128]{2,1,0:T(8,128)(2,1)S(1)}, u32[]{:S(2)}, u32[]{:S(2)}) collective-permute-start(bf16[2,384,128]{2,1,0:T(8,128)(2,1)S(1)} %get-tuple-element.74), channel_id=1, source_target_pairs={{0,4},{2,6},{4,0},{6,2},{1,5},{3,7},{5,1},{7,3},{8,12},{10,14},{12... | collective-permute-start | bytes 589832 | tf_op jit(solution)/shard_map/ppermute | solution.py:299
  45.7 7.4 %collective-permute-done.18 = bf16[4,96,384]{2,1,0:T(8,128)(2,1)S(1)} collective-permute-done((bf16[4,96,384]{2,1,0:T(8,128)(2,1)S(1)}, bf16[4,96,384]{2,1,0:T(8,128)(2,1)S(1)}, u32[]{:S(2)}, u32[]{:S(2)}) %collective-permute-start.18) | collective-permute-done | bytes 294944 | tf_op jit(solution)/shard_map/ppermute | solution.py:299
  53.6 2.8 %collective-permute-start.21 = (bf16[96,384]{1,0:T(8,128)(2,1)S(1)}, bf16[96,384]{1,0:T(8,128)(2,1)S(1)}, u32[]{:S(2)}, u32[]{:S(2)}) collective-permute-start(bf16[96,384]{1,0:T(8,128)(2,1)S(1)} %get-tuple-element.88), channel_id=1, source_target_pairs={{0,4},{2,6},{4,0},{6,2},{1,5},{3,7},{5,1},{7,3},{8,12},{10,14},{12... | collective-permute-start | bytes 221192 | tf_op jit(solution)/shard_map/ppermute | solution.py:299
  56.4 0.4 collective-permute-start.20
  56.8 4.3 %collective-permute-done.17 = bf16[2,384,128]{2,1,0:T(8,128)(2,1)S(1)} collective-permute-done((bf16[2,384,128]{2,1,0:T(8,128)(2,1)S(1)}, bf16[2,384,128]{2,1,0:T(8,128)(2,1)S(1)}, u32[]{:S(2)}, u32[]{:S(2)}) %collective-permute-start.17) | collective-permute-done | bytes 196640 | tf_op jit(solution)/shard_map/ppermute | solution.py:299
  61.1 1.5 %collective-permute-done.22.refs_3_ = bf16[96,384]{1,0:T(8,128)(2,1)S(1)} collective-permute-done((bf16[96,384]{1,0:T(8,128)(2,1)S(1)}, bf16[96,384]{1,0:T(8,128)(2,1)S(1)}, u32[]{:S(2)}, u32[]{:S(2)}) %collective-permute-start.22) | collective-permute-done | bytes 73760 | tf_op jit(solution)/shard_map/ppermute | solution.py:299
  62.7 0.8 %collective-permute-done.20.refs_1_ = bf16[96,384]{1,0:T(8,128)(2,1)S(1)} collective-permute-done((bf16[96,384]{1,0:T(8,128)(2,1)S(1)}, bf16[96,384]{1,0:T(8,128)(2,1)S(1)}, u32[]{:S(2)}, u32[]{:S(2)}) %collective-permute-start.20) | collective-permute-done | bytes 73760 | tf_op jit(solution)/shard_map/ppermute | solution.py:299
  63.7 0.9 %bias_grad.1 = f32[4,96,384]{2,1,0:T(8,128)} custom-call(bf16[96,384]{1,0:T(8,128)(2,1)S(1)} %get-tuple-element.90.refs_0_, bf16[96,384]{1,0:T(8,128)(2,1)S(1)} %collective-permute-done.20.refs_1_, bf16[96,384]{1,0:T(8,128)(2,1)S(1)} %collective-permute-done.21.refs_2_, bf16[96,384]{1,0:T(8,128)(2,1)S(1)} %collective-permute-done.22.refs_3_), custom_call_target="tpu_custom_call" | custom-call | tf_op jit(solution)/shard_map/bias_grad/pallas_call | solution.py:279
  64.6 0.8 %collective-permute-done.23.swapped = bf16[4,384,128]{2,1,0:T(8,128)(2,1)S(1)} collective-permute-done((bf16[4,384,128]{2,1,0:T(8,128)(2,1)S(1)}, bf16[4,384,128]{2,1,0:T(8,128)(2,1)S(1)}, u32[]{:S(2)}, u32[]{:S(2)}) %collective-permute-start.23) | collective-permute-done | bytes 393248 | tf_op jit(solution)/shard_map/ppermute | solution.py:299
  65.4 1.5 %unpack.1 = (bf16[2,384,128]{2,1,0:T(8,128)(2,1)}, bf16[2,384,128]{2,1,0:T(8,128)(2,1)}, bf16[2,384,128]{2,1,0:T(8,128)(2,1)}, bf16[2,384,128]{2,1,0:T(8,128)(2,1)}) custom-call(bf16[2,384,128]{2,1,0:T(8,128)(2,1)S(1)} %copy-done, bf16[2,384,128]{2,1,0:T(8,128)(2,1)S(1)} %copy-done.1, bf16[4,384,128]{2,1,0:T(8,128)(2,1)S(1)} %pad_maximum_fusion.packs, ...), custom_call_target="tpu_custom_call" | custom-call | tf_op jit(solution)/shard_map/unpack/pallas_call | solution.py:263
  (52 shorter events, 2.8 us)
Async XLA Ops:
  0.6 1.0 %copy-start.3 = (bf16[4,96,384]{2,1,0:T(8,128)(2,1)S(1)}, bf16[4,96,384]{2,1,0:T(8,128)(2,1)}, u32[]{:S(2)}) copy-start(bf16[4,96,384]{2,1,0:T(8,128)(2,1)} %bias.1) | copy-start | bytes 884740
  1.6 11.1 %copy-start.4 = (s32[384]{0:T(512)S(1)}, s32[384]{0:T(512)}, u32[]{:S(2)}) copy-start(s32[384]{0:T(512)} %param.12) | copy-start | bytes 4612
  1.6 11.1 %collective-permute-start.3 = (bf16[96,384]{1,0:T(8,128)(2,1)S(1)}, bf16[96,384]{1,0:T(8,128)(2,1)S(1)}, u32[]{:S(2)}, u32[]{:S(2)}) collective-permute-start(bf16[96,384]{1,0:T(8,128)(2,1)S(1)} %get-tuple-element.51), channel_id=1, source_target_pairs={{0,2},{2,0},{4,6},{6,4},{1,3},{3,1},{5,7},{7,5},{8,10},{10,8},{12,... | collective-permute-start | bytes 221192 | tf_op jit(solution)/shard_map/ppermute | solution.py:299
  4.6 8.1 %collective-permute-start.4 = (bf16[96,384]{1,0:T(8,128)(2,1)S(1)}, bf16[96,384]{1,0:T(8,128)(2,1)S(1)}, u32[]{:S(2)}, u32[]{:S(2)}) collective-permute-start(bf16[96,384]{1,0:T(8,128)(2,1)S(1)} %get-tuple-element.52), channel_id=1, source_target_pairs={{0,4},{2,6},{4,0},{6,2},{1,5},{3,7},{5,1},{7,3},{8,12},{10,14},{12... | collective-permute-start | bytes 221192 | tf_op jit(solution)/shard_map/ppermute | solution.py:299
  6.2 6.6 %collective-permute-start.5 = (bf16[96,384]{1,0:T(8,128)(2,1)S(1)}, bf16[96,384]{1,0:T(8,128)(2,1)S(1)}, u32[]{:S(2)}, u32[]{:S(2)}) collective-permute-start(bf16[96,384]{1,0:T(8,128)(2,1)S(1)} %get-tuple-element.53), channel_id=1, source_target_pairs={{0,6},{2,4},{4,2},{6,0},{1,7},{3,5},{5,3},{7,1},{8,14},{10,12},{12... | collective-permute-start | bytes 221192 | tf_op jit(solution)/shard_map/ppermute | solution.py:299
  9.1 8.5 %copy-start.5 = (bf16[384,128]{1,0:T(8,128)(2,1)S(1)}, bf16[384,128]{1,0:T(8,128)(2,1)}, u32[]{:S(2)}) copy-start(bf16[384,128]{1,0:T(8,128)(2,1)} %get-tuple-element.49) | copy-start | bytes 294916
  9.1 10.2 %copy-start.2 = (bf16[384,128]{1,0:T(8,128)(2,1)S(1)}, bf16[384,128]{1,0:T(8,128)(2,1)}, u32[]{:S(2)}) copy-start(bf16[384,128]{1,0:T(8,128)(2,1)} %get-tuple-element.46.refs_0_) | copy-start | bytes 294916
  9.1 7.1 %collective-permute-start = (bf16[2,384,128]{2,1,0:T(8,128)(2,1)}, bf16[2,384,128]{2,1,0:T(8,128)(2,1)S(1)}, u32[]{:S(2)}, u32[]{:S(2)}) collective-permute-start(bf16[2,384,128]{2,1,0:T(8,128)(2,1)} %get-tuple-element.47), channel_id=1, source_target_pairs={{0,2},{2,0},{4,6},{6,4},{1,3},{3,1},{5,7},{7,5},{8,10},{10,8},{12,... | collective-permute-start | bytes 589832 | tf_op jit(solution)/shard_map/ppermute | solution.py:299
  11.1 14.2 %collective-permute-start.11 = (bf16[2,384,128]{2,1,0:T(8,128)(2,1)}, bf16[2,384,128]{2,1,0:T(8,128)(2,1)S(1)}, u32[]{:S(2)}, u32[]{:S(2)}) collective-permute-start(bf16[2,384,128]{2,1,0:T(8,128)(2,1)} %get-tuple-element.62), channel_id=1, source_target_pairs={{0,4},{2,6},{4,0},{6,2},{1,5},{3,7},{5,1},{7,3},{8,12},{10,14},{12... | collective-permute-start | bytes 589832 | tf_op jit(solution)/shard_map/ppermute | solution.py:299
  12.7 14.5 %collective-permute-start.12 = (bf16[2,384,128]{2,1,0:T(8,128)(2,1)}, bf16[2,384,128]{2,1,0:T(8,128)(2,1)S(1)}, u32[]{:S(2)}, u32[]{:S(2)}) collective-permute-start(bf16[2,384,128]{2,1,0:T(8,128)(2,1)} %get-tuple-element.63), channel_id=1, source_target_pairs={{0,6},{2,4},{4,2},{6,0},{1,7},{3,5},{5,3},{7,1},{8,14},{10,12},{12... | collective-permute-start | bytes 589832 | tf_op jit(solution)/shard_map/ppermute | solution.py:299
  12.9 14.4 %collective-permute-start.6 = (bf16[4,96,384]{2,1,0:T(8,128)(2,1)S(1)}, bf16[4,96,384]{2,1,0:T(8,128)(2,1)S(1)}, u32[]{:S(2)}, u32[]{:S(2)}) collective-permute-start(bf16[4,96,384]{2,1,0:T(8,128)(2,1)S(1)} %maximum_select_fusion.refs_4_), channel_id=1, source_target_pairs={{0,8},{8,0},{1,9},{9,1},{2,10},{10,2},{3,11},{11,3},{4,12},{12,4},... | collective-permute-start | bytes 884744 | tf_op jit(solution)/shard_map/ppermute | solution.py:299
  15.9 2.0 %collective-permute-start.8 = (bf16[2,96,384]{2,1,0:T(8,128)(2,1)S(1)}, bf16[2,96,384]{2,1,0:T(8,128)(2,1)S(1)}, u32[]{:S(2)}, u32[]{:S(2)}) collective-permute-start(bf16[2,96,384]{2,1,0:T(8,128)(2,1)S(1)} %get-tuple-element.91), channel_id=1, source_target_pairs={{0,1},{1,0},{2,3},{3,2},{4,5},{5,4},{6,7},{7,6},{8,9},{9,8},{10,11... | collective-permute-start | bytes 442376 | tf_op jit(solution)/shard_map/ppermute | solution.py:299
  16.2 1.4 %collective-permute-start.7 = (bf16[2,96,384]{2,1,0:T(8,128)(2,1)S(1)}, bf16[2,96,384]{2,1,0:T(8,128)(2,1)S(1)}, u32[]{:S(2)}, u32[]{:S(2)}) collective-permute-start(bf16[2,96,384]{2,1,0:T(8,128)(2,1)S(1)} %get-tuple-element.92), channel_id=1, source_target_pairs={{0,1},{1,0},{2,3},{3,2},{4,5},{5,4},{6,7},{7,6},{8,9},{9,8},{10,11... | collective-permute-start | bytes 442376 | tf_op jit(solution)/shard_map/ppermute | solution.py:299
  17.6 1.3 %collective-permute-start.1 = (bf16[384,128]{1,0:T(8,128)(2,1)S(1)}, bf16[384,128]{1,0:T(8,128)(2,1)S(1)}, u32[]{:S(2)}, u32[]{:S(2)}) collective-permute-start(bf16[384,128]{1,0:T(8,128)(2,1)S(1)} %copy-done.5), channel_id=1, source_target_pairs={{0,1},{1,0},{2,3},{3,2},{4,5},{5,4},{6,7},{7,6},{8,9},{9,8},{10,11... | collective-permute-start | bytes 294920 | tf_op jit(solution)/shard_map/ppermute | solution.py:299
  17.9 1.4 %collective-permute-start.2 = (bf16[384,128]{1,0:T(8,128)(2,1)S(1)}, bf16[384,128]{1,0:T(8,128)(2,1)S(1)}, u32[]{:S(2)}, u32[]{:S(2)}) collective-permute-start(bf16[384,128]{1,0:T(8,128)(2,1)S(1)} %get-tuple-element.103), channel_id=1, source_target_pairs={{0,1},{1,0},{2,3},{3,2},{4,5},{5,4},{6,7},{7,6},{8,9},{9,8},{10,11... | collective-permute-start | bytes 294920 | tf_op jit(solution)/shard_map/ppermute | solution.py:299
  27.2 4.6 %collective-permute-start.13 = (bf16[384,128]{1,0:T(8,128)(2,1)S(1)}, bf16[384,128]{1,0:T(8,128)(2,1)S(1)}, u32[]{:S(2)}, u32[]{:S(2)}) collective-permute-start(bf16[384,128]{1,0:T(8,128)(2,1)S(1)} %get-tuple-element.101), channel_id=1, source_target_pairs={{0,1},{1,0},{2,3},{3,2},{4,5},{5,4},{6,7},{7,6},{8,9},{9,8},{10,11... | collective-permute-start | bytes 294920 | tf_op jit(solution)/shard_map/ppermute | solution.py:299
  27.3 1.7 %collective-permute-start.9 = (bf16[4,96,384]{2,1,0:T(8,128)(2,1)S(1)}, bf16[4,96,384]{2,1,0:T(8,128)(2,1)S(1)}, u32[]{:S(2)}, u32[]{:S(2)}) collective-permute-start(bf16[4,96,384]{2,1,0:T(8,128)(2,1)S(1)} %collective-permute-done.6.refs_4_), channel_id=1, source_target_pairs={{0,1},{1,0},{2,3},{3,2},{4,5},{5,4},{6,7},{7,6},{8,9},{9,8},{10,11... | collective-permute-start | bytes 884744 | tf_op jit(solution)/shard_map/ppermute | solution.py:299
  27.8 4.0 %collective-permute-start.14 = (bf16[384,128]{1,0:T(8,128)(2,1)S(1)}, bf16[384,128]{1,0:T(8,128)(2,1)S(1)}, u32[]{:S(2)}, u32[]{:S(2)}) collective-permute-start(bf16[384,128]{1,0:T(8,128)(2,1)S(1)} %get-tuple-element.99), channel_id=1, source_target_pairs={{0,1},{1,0},{2,3},{3,2},{4,5},{5,4},{6,7},{7,6},{8,9},{9,8},{10,11... | collective-permute-start | bytes 294920 | tf_op jit(solution)/shard_map/ppermute | solution.py:299
  34.6 1.7 %collective-permute-start.15 = (bf16[4,96,384]{2,1,0:T(8,128)(2,1)S(1)}, bf16[4,96,384]{2,1,0:T(8,128)(2,1)S(1)}, u32[]{:S(2)}, u32[]{:S(2)}) collective-permute-start(bf16[4,96,384]{2,1,0:T(8,128)(2,1)S(1)} %get-tuple-element.68), channel_id=1, source_target_pairs={{0,1},{1,0},{2,3},{3,2},{4,5},{5,4},{6,7},{7,6},{8,9},{9,8},{10,11... | collective-permute-start | bytes 884744 | tf_op jit(solution)/shard_map/ppermute | solution.py:299
  36.4 16.7 %collective-permute-start.18 = (bf16[4,96,384]{2,1,0:T(8,128)(2,1)S(1)}, bf16[4,96,384]{2,1,0:T(8,128)(2,1)S(1)}, u32[]{:S(2)}, u32[]{:S(2)}) collective-permute-start(bf16[4,96,384]{2,1,0:T(8,128)(2,1)S(1)} %add_convert_fusion.1), channel_id=1, source_target_pairs={{0,8},{8,0},{1,9},{9,1},{2,10},{10,2},{3,11},{11,3},{4,12},{12,4},... | collective-permute-start | bytes 884744 | tf_op jit(solution)/shard_map/ppermute | solution.py:299
  42.0 11.1 %collective-permute-start.19 = (bf16[4,96,384]{2,1,0:T(8,128)(2,1)S(1)}, bf16[4,96,384]{2,1,0:T(8,128)(2,1)S(1)}, u32[]{:S(2)}, u32[]{:S(2)}) collective-permute-start(bf16[4,96,384]{2,1,0:T(8,128)(2,1)S(1)} %get-tuple-element.78), channel_id=1, source_target_pairs={{0,1},{1,0},{2,3},{3,2},{4,5},{5,4},{6,7},{7,6},{8,9},{9,8},{10,11... | collective-permute-start | bytes 884744 | tf_op jit(solution)/shard_map/ppermute | solution.py:299
  42.1 14.3 %collective-permute-start.10 = (bf16[2,384,128]{2,1,0:T(8,128)(2,1)S(1)}, bf16[2,384,128]{2,1,0:T(8,128)(2,1)S(1)}, u32[]{:S(2)}, u32[]{:S(2)}) collective-permute-start(bf16[2,384,128]{2,1,0:T(8,128)(2,1)S(1)} %get-tuple-element.61), channel_id=1, source_target_pairs={{0,2},{2,0},{4,6},{6,4},{1,3},{3,1},{5,7},{7,5},{8,10},{10,8},{12,... | collective-permute-start | bytes 589832 | tf_op jit(solution)/shard_map/ppermute | solution.py:299
  42.7 14.1 %collective-permute-start.16 = (bf16[2,384,128]{2,1,0:T(8,128)(2,1)S(1)}, bf16[2,384,128]{2,1,0:T(8,128)(2,1)S(1)}, u32[]{:S(2)}, u32[]{:S(2)}) collective-permute-start(bf16[2,384,128]{2,1,0:T(8,128)(2,1)S(1)} %get-tuple-element.74), channel_id=1, source_target_pairs={{0,4},{2,6},{4,0},{6,2},{1,5},{3,7},{5,1},{7,3},{8,12},{10,14},{12... | collective-permute-start | bytes 589832 | tf_op jit(solution)/shard_map/ppermute | solution.py:299
  45.5 15.5 %collective-permute-start.17 = (bf16[2,384,128]{2,1,0:T(8,128)(2,1)S(1)}, bf16[2,384,128]{2,1,0:T(8,128)(2,1)S(1)}, u32[]{:S(2)}, u32[]{:S(2)}) collective-permute-start(bf16[2,384,128]{2,1,0:T(8,128)(2,1)S(1)} %get-tuple-element.75), channel_id=1, source_target_pairs={{0,6},{2,4},{4,2},{6,0},{1,7},{3,5},{5,3},{7,1},{8,14},{10,12},{12... | collective-permute-start | bytes 589832 | tf_op jit(solution)/shard_map/ppermute | solution.py:299
  53.2 9.4 %collective-permute-start.22 = (bf16[96,384]{1,0:T(8,128)(2,1)S(1)}, bf16[96,384]{1,0:T(8,128)(2,1)S(1)}, u32[]{:S(2)}, u32[]{:S(2)}) collective-permute-start(bf16[96,384]{1,0:T(8,128)(2,1)S(1)} %get-tuple-element.87), channel_id=1, source_target_pairs={{0,6},{2,4},{4,2},{6,0},{1,7},{3,5},{5,3},{7,1},{8,14},{10,12},{12... | collective-permute-start | bytes 221192 | tf_op jit(solution)/shard_map/ppermute | solution.py:299
  53.6 9.1 %collective-permute-start.21 = (bf16[96,384]{1,0:T(8,128)(2,1)S(1)}, bf16[96,384]{1,0:T(8,128)(2,1)S(1)}, u32[]{:S(2)}, u32[]{:S(2)}) collective-permute-start(bf16[96,384]{1,0:T(8,128)(2,1)S(1)} %get-tuple-element.88), channel_id=1, source_target_pairs={{0,4},{2,6},{4,0},{6,2},{1,5},{3,7},{5,1},{7,3},{8,12},{10,14},{12... | collective-permute-start | bytes 221192 | tf_op jit(solution)/shard_map/ppermute | solution.py:299
  56.4 7.1 %collective-permute-start.20 = (bf16[96,384]{1,0:T(8,128)(2,1)S(1)}, bf16[96,384]{1,0:T(8,128)(2,1)S(1)}, u32[]{:S(2)}, u32[]{:S(2)}) collective-permute-start(bf16[96,384]{1,0:T(8,128)(2,1)S(1)} %get-tuple-element.89), channel_id=1, source_target_pairs={{0,2},{2,0},{4,6},{6,4},{1,3},{3,1},{5,7},{7,5},{8,10},{10,8},{12,... | collective-permute-start | bytes 221192 | tf_op jit(solution)/shard_map/ppermute | solution.py:299
  63.6 1.9 %copy-start = (bf16[2,384,128]{2,1,0:T(8,128)(2,1)S(1)}, bf16[2,384,128]{2,1,0:T(8,128)(2,1)}, u32[]{:S(2)}) copy-start(bf16[2,384,128]{2,1,0:T(8,128)(2,1)} %gate.1) | copy-start | bytes 589828
  63.6 1.9 %copy-start.1 = (bf16[2,384,128]{2,1,0:T(8,128)(2,1)S(1)}, bf16[2,384,128]{2,1,0:T(8,128)(2,1)}, u32[]{:S(2)}) copy-start(bf16[2,384,128]{2,1,0:T(8,128)(2,1)} %cot.1) | copy-start | bytes 589828
  63.6 1.8 %collective-permute-start.23 = (bf16[4,384,128]{2,1,0:T(8,128)(2,1)S(1)}, bf16[4,384,128]{2,1,0:T(8,128)(2,1)S(1)}, u32[]{:S(2)}, u32[]{:S(2)}) collective-permute-start(bf16[4,384,128]{2,1,0:T(8,128)(2,1)S(1)} %pad_maximum_fusion.1), channel_id=1, source_target_pairs={{0,1},{1,0},{2,3},{3,2},{4,5},{5,4},{6,7},{7,6},{8,9},{9,8},{10,11... | collective-permute-start | bytes 1179656 | tf_op jit(solution)/shard_map/ppermute | solution.py:299
where the time goes:
time: 67.1 us; the launch traced here: 66.9 us
  waiting for transfers between devices  24.7 us (37%)
  starting transfers between devices  23.2 us (35%)
  Pallas kernels  16.6 us (25%)
  local copies, waits for them, and re-layouts  1.17 us (2%)
  between operations  0.9 us (1%)
    ppermute x24, waiting for transfers between devices, swap(): lax.ppermute(value, axes, [(i, i ^ s) for i in range(count)])  24.7 us
    ppermute x24, starting transfers between devices, swap(): lax.ppermute(value, axes, [(i, i ^ s) for i in range(count)])  23.2 us
    pallas_call x4, Pallas kernels, main(): pl.pallas_call(functools.partial(main_kernel, scaling, size, start, relat...  11.4 us
    pallas_call x1, Pallas kernels, make_packs(): pl.pallas_call(pack_kernel, in_specs=[pl.BlockSpec(memory_space=pl.ANY)]...  2.87 us
    pallas_call x1, Pallas kernels, post(): pl.pallas_call(post_kernel, out_shape=[jax.ShapeDtypeStruct(gate.shape, j...  1.45 us
  transfers between devices with their start and end apart: 24, of which 14 were waited for; matrix products, arithmetic and copies ran while one was open for 1% of the time, Pallas kernels for 18%

commit v1 on v0

--- a/solution.py
+++ b/solution.py
@@ -320,49 +320,44 @@
     if not relative:
         starts, groups = [0], [jnp.concatenate(groups)[chip ^ jnp.arange(chips)].reshape(8, -1, half)]
     others = [jnp.concatenate([other_core(part) for part in jnp.split(groups[0], NEAR_PARTS)])] + [None] * (len(starts) - 1)
-    orders = [list(range(len(starts))), list(range(len(starts)))[::-1]]
-    before, sums, returned = [[]] * len(starts), [None] * len(starts), []
-    for a, order in enumerate(orders):
-        ours = [packs[0]] if a == 0 else packs[1:]
-        if a:
-            ours = list(lax.optimization_barrier((*ours, before[0][0]))[:2])
-        swapped = [other_core(pack[1]) for pack in ours]
-        ours = [pack[0] for pack in ours]
-        if a == 0:
-            spare = lax.optimization_barrier((spare, ours[0]))[0]
-            ours, swapped = [kept] + ours, [other_core(spare)] + swapped
-        earlier = []
-        for g in order:
-            if others[g] is None:
-                groups[g] = lax.optimization_barrier((groups[g], before[0][0]))[0]
+    sets = [None, None]
+    before, sums, returned, state = [[]] * len(starts), [None] * len(starts), [], [[], []]
+    for g, start in enumerate(starts):
+        ended = g == len(starts) - 1
+        for a in range(2):
+            if g == 0:
+                ours = [packs[0]] if a == 0 else packs[1:]
+                if a:
+                    ours = list(lax.optimization_barrier((*ours, before[0][0]))[:2])
+                swapped = [other_core(pack[1]) for pack in ours]
+                ours = [pack[0] for pack in ours]
+                if a == 0:
+                    spare = lax.optimization_barrier((spare, ours[0]))[0]
+                    ours, swapped = [kept] + ours, [other_core(spare)] + swapped
+                sets[a] = ours, swapped
+            elif a == 0:
+                groups[g] = lax.optimization_barrier((groups[g], d_mine))[0]
                 others[g] = other_core(groups[g])
-            mine, closed, ended = groups[g], a == len(orders) - 1, g == order[-1]
-            if closed and g != order[0]:
-                mine, last = lax.optimization_barrier((mine, sums[order[order.index(g) - 1]]))
-                sums[order[order.index(g) - 1]] = last
             out = main(
-                ours, swapped, mine, others[g], earlier, before[g], scaling, size, starts[g], relative, ended, closed, 1 - a
+                *sets[a], groups[g], others[g], state[a], before[g], scaling, size, start, relative, ended, bool(a), 1 - a
             )
-            if not closed:
-                before[g], earlier = out[:1], out[1:]
-                continue
-            d_mine, d_other, *earlier = out
-            d_mine = wide(d_mine)
-            if ended and relative:
-                for f in range(1, far):
-                    d_mine = d_mine + wide(far_swap(sums[f], f))
-                d_mine = lax.optimization_barrier(d_mine)
-            sums[g] = (d_mine + wide(other_core(d_other))).astype(jnp.bfloat16)
-        if a == 0:
-            stay, pass_on, *earlier = earlier
-        returned += [near_swap(value, len(returned) + i + 1) for i, value in enumerate(earlier)]
-    d_sum = sums[0]
-    if not relative:
-        d_sum = d_sum.reshape(chips, own, half)[chip ^ jnp.arange(chips)]
+            if a == 0:
+                before[g], state[a] = out[:1], out[1:]
+            else:
+                d_mine, d_other, *state[a] = out
+                sums[g] = (wide(d_mine) + wide(other_core(d_other))).astype(jnp.bfloat16)
+    stay, pass_on, *state[0] = state[0]
+    returned = [near_swap(value, i + 1) for i, value in enumerate([*state[0], *state[1]])]
+    if relative:
+        total = wide(sums[0])
+        for f in range(1, far):
+            total = total + wide(far_swap(sums[f], f))
+    else:
+        d_sum = sums[0].reshape(chips, own, half)[chip ^ jnp.arange(chips)]
         total = wide(d_sum[:4])
         for f in range(1, far):
             total = total + wide(far_swap(d_sum[4 * f : 4 * f + 4], f))
-        d_sum = total.astype(jnp.bfloat16)
+    d_sum = total.astype(jnp.bfloat16)
     pieces = [near_swap(d_sum[s], s) for s in range(4)]
     returned = lax.optimization_barrier((*returned, *pieces))[:3]
     swapped = other_core(jnp.stack([pass_on] + [pack[1] for pack in returned]))

time: 67.1 us -> 68.8 us (1.025)
  waiting for transfers between devices: 24.7 us -> 26.7 us
    ppermute x24, waiting for transfers between devices: 24.7 us -> 26.7 us  [swap(): lax.ppermute(value, axes, [(i, i ^ s) for i in range(count)])]
  transfers between devices with their start and end apart: 24 -> 24, of which waited for: 14 -> 15; matrix products, arithmetic and copies ran while one was open for 1% -> 1% of each run, Pallas kernels for 18% -> 13%
where the time goes in v1:
time: 68.8 us; the launch traced here: 68.6 us
  waiting for transfers between devices  26.7 us (39%)
  starting transfers between devices  22.9 us (33%)
  Pallas kernels  16.6 us (24%)
  local copies, waits for them, and re-layouts  1.17 us (2%)
  between operations  0.88 us (1%)
    ppermute x24, waiting for transfers between devices, swap(): lax.ppermute(value, axes, [(i, i ^ s) for i in range(count)])  26.7 us
    ppermute x24, starting transfers between devices, swap(): lax.ppermute(value, axes, [(i, i ^ s) for i in range(count)])  22.9 us
    pallas_call x4, Pallas kernels, main(): pl.pallas_call(functools.partial(main_kernel, scaling, size, start, relat...  11.4 us
    pallas_call x1, Pallas kernels, make_packs(): pl.pallas_call(pack_kernel, in_specs=[pl.BlockSpec(memory_space=pl.ANY)]...  2.87 us
    pallas_call x1, Pallas kernels, post(): pl.pallas_call(post_kernel, out_shape=[jax.ShapeDtypeStruct(gate.shape, j...  1.45 us
  transfers between devices with their start and end apart: 24, of which 15 were waited for; matrix products, arithmetic and copies ran while one was open for 1% of the time, Pallas kernels for 13%

profile of v1, /device:TPU:0, one launch (start us, length us, event | category | flops | bytes accessed | tf_op | source)
XLA Modules:
  0.0 68.6 jit_solution(1192819457100899863)
XLA Ops:
  0.6 1.0 %copy-done.3 = bf16[4,96,384]{2,1,0:T(8,128)(2,1)S(1)} copy-done((bf16[4,96,384]{2,1,0:T(8,128)(2,1)S(1)}, bf16[4,96,384]{2,1,0:T(8,128)(2,1)}, u32[]{:S(2)}) %copy-start.3) | copy-done | bytes 294936
  1.6 3.0 %collective-permute-start.3 = (bf16[96,384]{1,0:T(8,128)(2,1)S(1)}, bf16[96,384]{1,0:T(8,128)(2,1)S(1)}, u32[]{:S(2)}, u32[]{:S(2)}) collective-permute-start(bf16[96,384]{1,0:T(8,128)(2,1)S(1)} %get-tuple-element.49), channel_id=1, source_target_pairs={{0,2},{2,0},{4,6},{6,4},{1,3},{3,1},{5,7},{7,5},{8,10},{10,8},{12,... | collective-permute-start | bytes 221192 | tf_op jit(solution)/shard_map/ppermute | solution.py:299
  4.6 1.6 %collective-permute-start.4 = (bf16[96,384]{1,0:T(8,128)(2,1)S(1)}, bf16[96,384]{1,0:T(8,128)(2,1)S(1)}, u32[]{:S(2)}, u32[]{:S(2)}) collective-permute-start(bf16[96,384]{1,0:T(8,128)(2,1)S(1)} %get-tuple-element.50), channel_id=1, source_target_pairs={{0,4},{2,6},{4,0},{6,2},{1,5},{3,7},{5,1},{7,3},{8,12},{10,14},{12... | collective-permute-start | bytes 221192 | tf_op jit(solution)/shard_map/ppermute | solution.py:299
  6.2 2.9 %pack.1 = (bf16[2,384,128]{2,1,0:T(8,128)(2,1)}, bf16[2,384,128]{2,1,0:T(8,128)(2,1)}, bf16[2,384,128]{2,1,0:T(8,128)(2,1)}, bf16[384,128]{1,0:T(8,128)(2,1)}, bf16[384,128]{1,0:T(8,128)(2,1)}) custom-call(bf16[2,384,128]{2,1,0:T(8,128)(2,1)} %refs_0_.1, bf16[2,384,128]{2,1,0:T(8,128)(2,1)} %refs_1_.1, bf16[2,384,128]{2,1,0:T(8,128)(2,1)} %refs_2_.1, ...), custom_call_target="tpu_custom_call" | custom-call | tf_op jit(solution)/shard_map/pack/pallas_call | solution.py:67
  9.1 2.0 %collective-permute-start = (bf16[2,384,128]{2,1,0:T(8,128)(2,1)}, bf16[2,384,128]{2,1,0:T(8,128)(2,1)S(1)}, u32[]{:S(2)}, u32[]{:S(2)}) collective-permute-start(bf16[2,384,128]{2,1,0:T(8,128)(2,1)} %get-tuple-element.45), channel_id=1, source_target_pairs={{0,2},{2,0},{4,6},{6,4},{1,3},{3,1},{5,7},{7,5},{8,10},{10,8},{12,... | collective-permute-start | bytes 589832 | tf_op jit(solution)/shard_map/ppermute | solution.py:299
  11.1 1.6 %collective-permute-start.7 = (bf16[2,384,128]{2,1,0:T(8,128)(2,1)}, bf16[2,384,128]{2,1,0:T(8,128)(2,1)S(1)}, u32[]{:S(2)}, u32[]{:S(2)}) collective-permute-start(bf16[2,384,128]{2,1,0:T(8,128)(2,1)} %get-tuple-element.52), channel_id=1, source_target_pairs={{0,4},{2,6},{4,0},{6,2},{1,5},{3,7},{5,1},{7,3},{8,12},{10,14},{12... | collective-permute-start | bytes 589832 | tf_op jit(solution)/shard_map/ppermute | solution.py:299
  12.9 3.0 %collective-permute-start.6 = (bf16[4,96,384]{2,1,0:T(8,128)(2,1)S(1)}, bf16[4,96,384]{2,1,0:T(8,128)(2,1)S(1)}, u32[]{:S(2)}, u32[]{:S(2)}) collective-permute-start(bf16[4,96,384]{2,1,0:T(8,128)(2,1)S(1)} %maximum_select_fusion.refs_4_), channel_id=1, source_target_pairs={{0,8},{8,0},{1,9},{9,1},{2,10},{10,2},{3,11},{11,3},{4,12},{12,4},... | collective-permute-start | bytes 884744 | tf_op jit(solution)/shard_map/ppermute | solution.py:299
  16.5 1.1 %collective-permute-done.9 = bf16[2,96,384]{2,1,0:T(8,128)(2,1)S(1)} collective-permute-done((bf16[2,96,384]{2,1,0:T(8,128)(2,1)S(1)}, bf16[2,96,384]{2,1,0:T(8,128)(2,1)S(1)}, u32[]{:S(2)}, u32[]{:S(2)}) %collective-permute-start.9) | collective-permute-done | bytes 147488 | tf_op jit(solution)/shard_map/ppermute | solution.py:299
  18.2 0.7 collective-permute-done.1.refs_2_
  18.9 0.4 collective-permute-done.2.refs_3_
  19.3 2.7 %attention.4 = (f32[384,768]{1,0:T(8,128)S(1)}, bf16[768,64]{1,0:T(8,128)(2,1)S(1)}, bf16[768,64]{1,0:T(8,128)(2,1)S(1)}, f32[64,768]{1,0:T(8,128)S(1)}, f32[64,768]{1,0:T(8,128)S(1)}) custom-call(bf16[384,128]{1,0:T(8,128)(2,1)S(1)} %copy-done.2, bf16[384,128]{1,0:T(8,128)(2,1)S(1)} %get-tuple-element.100.refs_1_, ...), custom_call_target="tpu_custom_call" | custom-call | flops 1 | bytes 1 | tf_op jit(solution)/shard_map/attention/pallas_call | solution.py:213
  22.0 3.2 %collective-permute-done.7 = bf16[2,384,128]{2,1,0:T(8,128)(2,1)S(1)} collective-permute-done((bf16[2,384,128]{2,1,0:T(8,128)(2,1)}, bf16[2,384,128]{2,1,0:T(8,128)(2,1)S(1)}, u32[]{:S(2)}, u32[]{:S(2)}) %collective-permute-start.7) | collective-permute-done | bytes 196640 | tf_op jit(solution)/shard_map/ppermute | solution.py:299
  25.2 1.9 %collective-permute-done.8 = bf16[2,384,128]{2,1,0:T(8,128)(2,1)S(1)} collective-permute-done((bf16[2,384,128]{2,1,0:T(8,128)(2,1)}, bf16[2,384,128]{2,1,0:T(8,128)(2,1)S(1)}, u32[]{:S(2)}, u32[]{:S(2)}) %collective-permute-start.8) | collective-permute-done | bytes 196640 | tf_op jit(solution)/shard_map/ppermute | solution.py:299
  27.3 0.6 collective-permute-start.12
  27.9 0.7 %collective-permute-done.11.refs_2_ = bf16[384,128]{1,0:T(8,128)(2,1)S(1)} collective-permute-done((bf16[384,128]{1,0:T(8,128)(2,1)S(1)}, bf16[384,128]{1,0:T(8,128)(2,1)S(1)}, u32[]{:S(2)}, u32[]{:S(2)}) %collective-permute-start.11) | collective-permute-done | bytes 98336 | tf_op jit(solution)/shard_map/ppermute | solution.py:299
  28.8 2.8 %attention.5 = (bf16[4,96,384]{2,1,0:T(8,128)(2,1)S(1)}, bf16[4,96,384]{2,1,0:T(8,128)(2,1)S(1)}, bf16[768,64]{1,0:T(8,128)(2,1)S(1)}, bf16[768,64]{1,0:T(8,128)...) custom-call(bf16[384,128]{1,0:T(8,128)(2,1)S(1)} %get-tuple-element.98.refs_0_, ...), custom_call_target="tpu_custom_call" | custom-call | flops 1 | bytes 1 | tf_op jit(solution)/shard_map/attention/pallas_call | solution.py:213
  31.6 0.4 collective-permute-start.13
  32.0 1.2 %collective-permute-done.13.refs_5_ = bf16[4,96,384]{2,1,0:T(8,128)(2,1)S(1)} collective-permute-done((bf16[4,96,384]{2,1,0:T(8,128)(2,1)S(1)}, bf16[4,96,384]{2,1,0:T(8,128)(2,1)S(1)}, u32[]{:S(2)}, u32[]{:S(2)}) %collective-permute-start.13) | collective-permute-done | bytes 294944 | tf_op jit(solution)/shard_map/ppermute | solution.py:299
  33.2 2.8 %attention.6 = (f32[384,768]{1,0:T(8,128)S(1)}, bf16[384,128]{1,0:T(8,128)(2,1)S(1)}, bf16[384,128]{1,0:T(8,128)(2,1)S(1)}, bf16[2,384,128]{2,1,0:T(8,128)(2,1)S(1)}) custom-call(bf16[384,128]{1,0:T(8,128)(2,1)S(1)} %copy-done.2, bf16[384,128]{1,0:T(8,128)(2,1)S(1)} %get-tuple-element.100.refs_1_, bf16[384,128]{1,0:T(8,128)(2,1)S(1)} %collective-permute-done.1.refs_2_, ...), custom_call_target="tpu_custom_call" | custom-call | flops 1 | bytes 1 | tf_op jit(solution)/shard_map/attention/pallas_call | solution.py:213
  36.1 3.1 %attention.7 = (bf16[4,96,384]{2,1,0:T(8,128)(2,1)S(1)}, bf16[4,96,384]{2,1,0:T(8,128)(2,1)S(1)}, bf16[2,384,128]{2,1,0:T(8,128)(2,1)S(1)}, bf16[2,384,128]{2,1,0:T(8,128)(2,1)S(1)}) custom-call(bf16[384,128]{1,0:T(8,128)(2,1)S(1)} %get-tuple-element.98.refs_0_, bf16[384,128]{1,0:T(8,128)(2,1)S(1)} %get-tuple-element.96.refs_1_, ...), custom_call_target="tpu_custom_call" | custom-call | flops 1 | bytes 1 | tf_op jit(solution)/shard_map/attention/pallas_call | solution.py:213
  39.2 0.4 collective-permute-start.18
  39.8 1.1 %collective-permute-done.18 = bf16[4,96,384]{2,1,0:T(8,128)(2,1)S(1)} collective-permute-done((bf16[4,96,384]{2,1,0:T(8,128)(2,1)S(1)}, bf16[4,96,384]{2,1,0:T(8,128)(2,1)S(1)}, u32[]{:S(2)}, u32[]{:S(2)}) %collective-permute-start.18) | collective-permute-done | bytes 294944 | tf_op jit(solution)/shard_map/ppermute | solution.py:299
  40.9 1.6 %collective-permute-start.19 = (bf16[4,96,384]{2,1,0:T(8,128)(2,1)S(1)}, bf16[4,96,384]{2,1,0:T(8,128)(2,1)S(1)}, u32[]{:S(2)}, u32[]{:S(2)}) collective-permute-start(bf16[4,96,384]{2,1,0:T(8,128)(2,1)S(1)} %add_convert_fusion.1), channel_id=1, source_target_pairs={{0,8},{8,0},{1,9},{9,1},{2,10},{10,2},{3,11},{11,3},{4,12},{12,4},... | collective-permute-start | bytes 884744 | tf_op jit(solution)/shard_map/ppermute | solution.py:299
  42.7 3.7 %collective-permute-start.15 = (bf16[2,384,128]{2,1,0:T(8,128)(2,1)S(1)}, bf16[2,384,128]{2,1,0:T(8,128)(2,1)S(1)}, u32[]{:S(2)}, u32[]{:S(2)}) collective-permute-start(bf16[2,384,128]{2,1,0:T(8,128)(2,1)S(1)} %get-tuple-element.70), channel_id=1, source_target_pairs={{0,4},{2,6},{4,0},{6,2},{1,5},{3,7},{5,1},{7,3},{8,12},{10,14},{12... | collective-permute-start | bytes 589832 | tf_op jit(solution)/shard_map/ppermute | solution.py:299
  46.4 10.9 %collective-permute-done.19 = bf16[4,96,384]{2,1,0:T(8,128)(2,1)S(1)} collective-permute-done((bf16[4,96,384]{2,1,0:T(8,128)(2,1)S(1)}, bf16[4,96,384]{2,1,0:T(8,128)(2,1)S(1)}, u32[]{:S(2)}, u32[]{:S(2)}) %collective-permute-start.19) | collective-permute-done | bytes 294944 | tf_op jit(solution)/shard_map/ppermute | solution.py:299
  57.5 3.3 %collective-permute-start.21 = (bf16[96,384]{1,0:T(8,128)(2,1)S(1)}, bf16[96,384]{1,0:T(8,128)(2,1)S(1)}, u32[]{:S(2)}, u32[]{:S(2)}) collective-permute-start(bf16[96,384]{1,0:T(8,128)(2,1)S(1)} %get-tuple-element.84), channel_id=1, source_target_pairs={{0,4},{2,6},{4,0},{6,2},{1,5},{3,7},{5,1},{7,3},{8,12},{10,14},{12... | collective-permute-start | bytes 221192 | tf_op jit(solution)/shard_map/ppermute | solution.py:299
  61.0 2.5 %collective-permute-done.22.refs_3_ = bf16[96,384]{1,0:T(8,128)(2,1)S(1)} collective-permute-done((bf16[96,384]{1,0:T(8,128)(2,1)S(1)}, bf16[96,384]{1,0:T(8,128)(2,1)S(1)}, u32[]{:S(2)}, u32[]{:S(2)}) %collective-permute-start.22) | collective-permute-done | bytes 73760 | tf_op jit(solution)/shard_map/ppermute | solution.py:299
  63.5 1.3 %collective-permute-done.21.refs_2_ = bf16[96,384]{1,0:T(8,128)(2,1)S(1)} collective-permute-done((bf16[96,384]{1,0:T(8,128)(2,1)S(1)}, bf16[96,384]{1,0:T(8,128)(2,1)S(1)}, u32[]{:S(2)}, u32[]{:S(2)}) %collective-permute-start.21) | collective-permute-done | bytes 73760 | tf_op jit(solution)/shard_map/ppermute | solution.py:299
  64.8 0.4 collective-permute-done.20.refs_1_
  65.5 0.9 %bias_grad.1 = f32[4,96,384]{2,1,0:T(8,128)} custom-call(bf16[96,384]{1,0:T(8,128)(2,1)S(1)} %get-tuple-element.86.refs_0_, bf16[96,384]{1,0:T(8,128)(2,1)S(1)} %collective-permute-done.20.refs_1_, bf16[96,384]{1,0:T(8,128)(2,1)S(1)} %collective-permute-done.21.refs_2_, bf16[96,384]{1,0:T(8,128)(2,1)S(1)} %collective-permute-done.22.refs_3_), custom_call_target="tpu_custom_call" | custom-call | tf_op jit(solution)/shard_map/bias_grad/pallas_call | solution.py:279
  66.4 0.8 %collective-permute-done.23.swapped = bf16[4,384,128]{2,1,0:T(8,128)(2,1)S(1)} collective-permute-done((bf16[4,384,128]{2,1,0:T(8,128)(2,1)S(1)}, bf16[4,384,128]{2,1,0:T(8,128)(2,1)S(1)}, u32[]{:S(2)}, u32[]{:S(2)}) %collective-permute-start.23) | collective-permute-done | bytes 393248 | tf_op jit(solution)/shard_map/ppermute | solution.py:299
  67.2 1.5 %unpack.1 = (bf16[2,384,128]{2,1,0:T(8,128)(2,1)}, bf16[2,384,128]{2,1,0:T(8,128)(2,1)}, bf16[2,384,128]{2,1,0:T(8,128)(2,1)}, bf16[2,384,128]{2,1,0:T(8,128)(2,1)}) custom-call(bf16[2,384,128]{2,1,0:T(8,128)(2,1)S(1)} %copy-done, bf16[2,384,128]{2,1,0:T(8,128)(2,1)S(1)} %copy-done.1, bf16[4,384,128]{2,1,0:T(8,128)(2,1)S(1)} %pad_maximum_fusion.packs, ...), custom_call_target="tpu_custom_call" | custom-call | tf_op jit(solution)/shard_map/unpack/pallas_call | solution.py:263
  (51 shorter events, 2.7 us)
Async XLA Ops:
  0.6 1.0 %copy-start.3 = (bf16[4,96,384]{2,1,0:T(8,128)(2,1)S(1)}, bf16[4,96,384]{2,1,0:T(8,128)(2,1)}, u32[]{:S(2)}) copy-start(bf16[4,96,384]{2,1,0:T(8,128)(2,1)} %bias.1) | copy-start | bytes 884740
  1.6 11.1 %copy-start.4 = (s32[384]{0:T(512)S(1)}, s32[384]{0:T(512)}, u32[]{:S(2)}) copy-start(s32[384]{0:T(512)} %param.12) | copy-start | bytes 4612
  1.6 11.1 %collective-permute-start.3 = (bf16[96,384]{1,0:T(8,128)(2,1)S(1)}, bf16[96,384]{1,0:T(8,128)(2,1)S(1)}, u32[]{:S(2)}, u32[]{:S(2)}) collective-permute-start(bf16[96,384]{1,0:T(8,128)(2,1)S(1)} %get-tuple-element.49), channel_id=1, source_target_pairs={{0,2},{2,0},{4,6},{6,4},{1,3},{3,1},{5,7},{7,5},{8,10},{10,8},{12,... | collective-permute-start | bytes 221192 | tf_op jit(solution)/shard_map/ppermute | solution.py:299
  4.6 8.1 %collective-permute-start.4 = (bf16[96,384]{1,0:T(8,128)(2,1)S(1)}, bf16[96,384]{1,0:T(8,128)(2,1)S(1)}, u32[]{:S(2)}, u32[]{:S(2)}) collective-permute-start(bf16[96,384]{1,0:T(8,128)(2,1)S(1)} %get-tuple-element.50), channel_id=1, source_target_pairs={{0,4},{2,6},{4,0},{6,2},{1,5},{3,7},{5,1},{7,3},{8,12},{10,14},{12... | collective-permute-start | bytes 221192 | tf_op jit(solution)/shard_map/ppermute | solution.py:299
  6.2 6.6 %collective-permute-start.5 = (bf16[96,384]{1,0:T(8,128)(2,1)S(1)}, bf16[96,384]{1,0:T(8,128)(2,1)S(1)}, u32[]{:S(2)}, u32[]{:S(2)}) collective-permute-start(bf16[96,384]{1,0:T(8,128)(2,1)S(1)} %get-tuple-element.51), channel_id=1, source_target_pairs={{0,6},{2,4},{4,2},{6,0},{1,7},{3,5},{5,3},{7,1},{8,14},{10,12},{12... | collective-permute-start | bytes 221192 | tf_op jit(solution)/shard_map/ppermute | solution.py:299
  9.1 8.5 %copy-start.5 = (bf16[384,128]{1,0:T(8,128)(2,1)S(1)}, bf16[384,128]{1,0:T(8,128)(2,1)}, u32[]{:S(2)}) copy-start(bf16[384,128]{1,0:T(8,128)(2,1)} %get-tuple-element.47) | copy-start | bytes 294916
  9.1 10.2 %copy-start.2 = (bf16[384,128]{1,0:T(8,128)(2,1)S(1)}, bf16[384,128]{1,0:T(8,128)(2,1)}, u32[]{:S(2)}) copy-start(bf16[384,128]{1,0:T(8,128)(2,1)} %get-tuple-element.44.refs_0_) | copy-start | bytes 294916
  9.1 7.1 %collective-permute-start = (bf16[2,384,128]{2,1,0:T(8,128)(2,1)}, bf16[2,384,128]{2,1,0:T(8,128)(2,1)S(1)}, u32[]{:S(2)}, u32[]{:S(2)}) collective-permute-start(bf16[2,384,128]{2,1,0:T(8,128)(2,1)} %get-tuple-element.45), channel_id=1, source_target_pairs={{0,2},{2,0},{4,6},{6,4},{1,3},{3,1},{5,7},{7,5},{8,10},{10,8},{12,... | collective-permute-start | bytes 589832 | tf_op jit(solution)/shard_map/ppermute | solution.py:299
  11.1 14.2 %collective-permute-start.7 = (bf16[2,384,128]{2,1,0:T(8,128)(2,1)}, bf16[2,384,128]{2,1,0:T(8,128)(2,1)S(1)}, u32[]{:S(2)}, u32[]{:S(2)}) collective-permute-start(bf16[2,384,128]{2,1,0:T(8,128)(2,1)} %get-tuple-element.52), channel_id=1, source_target_pairs={{0,4},{2,6},{4,0},{6,2},{1,5},{3,7},{5,1},{7,3},{8,12},{10,14},{12... | collective-permute-start | bytes 589832 | tf_op jit(solution)/shard_map/ppermute | solution.py:299
  12.7 14.5 %collective-permute-start.8 = (bf16[2,384,128]{2,1,0:T(8,128)(2,1)}, bf16[2,384,128]{2,1,0:T(8,128)(2,1)S(1)}, u32[]{:S(2)}, u32[]{:S(2)}) collective-permute-start(bf16[2,384,128]{2,1,0:T(8,128)(2,1)} %get-tuple-element.53), channel_id=1, source_target_pairs={{0,6},{2,4},{4,2},{6,0},{1,7},{3,5},{5,3},{7,1},{8,14},{10,12},{12... | collective-permute-start | bytes 589832 | tf_op jit(solution)/shard_map/ppermute | solution.py:299
  12.9 18.7 %collective-permute-start.6 = (bf16[4,96,384]{2,1,0:T(8,128)(2,1)S(1)}, bf16[4,96,384]{2,1,0:T(8,128)(2,1)S(1)}, u32[]{:S(2)}, u32[]{:S(2)}) collective-permute-start(bf16[4,96,384]{2,1,0:T(8,128)(2,1)S(1)} %maximum_select_fusion.refs_4_), channel_id=1, source_target_pairs={{0,8},{8,0},{1,9},{9,1},{2,10},{10,2},{3,11},{11,3},{4,12},{12,4},... | collective-permute-start | bytes 884744 | tf_op jit(solution)/shard_map/ppermute | solution.py:299
  15.9 2.0 %collective-permute-start.10 = (bf16[2,96,384]{2,1,0:T(8,128)(2,1)S(1)}, bf16[2,96,384]{2,1,0:T(8,128)(2,1)S(1)}, u32[]{:S(2)}, u32[]{:S(2)}) collective-permute-start(bf16[2,96,384]{2,1,0:T(8,128)(2,1)S(1)} %get-tuple-element.87), channel_id=1, source_target_pairs={{0,1},{1,0},{2,3},{3,2},{4,5},{5,4},{6,7},{7,6},{8,9},{9,8},{10,11... | collective-permute-start | bytes 442376 | tf_op jit(solution)/shard_map/ppermute | solution.py:299
  16.2 1.4 %collective-permute-start.9 = (bf16[2,96,384]{2,1,0:T(8,128)(2,1)S(1)}, bf16[2,96,384]{2,1,0:T(8,128)(2,1)S(1)}, u32[]{:S(2)}, u32[]{:S(2)}) collective-permute-start(bf16[2,96,384]{2,1,0:T(8,128)(2,1)S(1)} %get-tuple-element.88), channel_id=1, source_target_pairs={{0,1},{1,0},{2,3},{3,2},{4,5},{5,4},{6,7},{7,6},{8,9},{9,8},{10,11... | collective-permute-start | bytes 442376 | tf_op jit(solution)/shard_map/ppermute | solution.py:299
  17.6 1.3 %collective-permute-start.1 = (bf16[384,128]{1,0:T(8,128)(2,1)S(1)}, bf16[384,128]{1,0:T(8,128)(2,1)S(1)}, u32[]{:S(2)}, u32[]{:S(2)}) collective-permute-start(bf16[384,128]{1,0:T(8,128)(2,1)S(1)} %copy-done.5), channel_id=1, source_target_pairs={{0,1},{1,0},{2,3},{3,2},{4,5},{5,4},{6,7},{7,6},{8,9},{9,8},{10,11... | collective-permute-start | bytes 294920 | tf_op jit(solution)/shard_map/ppermute | solution.py:299
  17.9 1.4 %collective-permute-start.2 = (bf16[384,128]{1,0:T(8,128)(2,1)S(1)}, bf16[384,128]{1,0:T(8,128)(2,1)S(1)}, u32[]{:S(2)}, u32[]{:S(2)}) collective-permute-start(bf16[384,128]{1,0:T(8,128)(2,1)S(1)} %get-tuple-element.99), channel_id=1, source_target_pairs={{0,1},{1,0},{2,3},{3,2},{4,5},{5,4},{6,7},{7,6},{8,9},{9,8},{10,11... | collective-permute-start | bytes 294920 | tf_op jit(solution)/shard_map/ppermute | solution.py:299
  27.2 1.4 %collective-permute-start.11 = (bf16[384,128]{1,0:T(8,128)(2,1)S(1)}, bf16[384,128]{1,0:T(8,128)(2,1)S(1)}, u32[]{:S(2)}, u32[]{:S(2)}) collective-permute-start(bf16[384,128]{1,0:T(8,128)(2,1)S(1)} %get-tuple-element.97), channel_id=1, source_target_pairs={{0,1},{1,0},{2,3},{3,2},{4,5},{5,4},{6,7},{7,6},{8,9},{9,8},{10,11... | collective-permute-start | bytes 294920 | tf_op jit(solution)/shard_map/ppermute | solution.py:299
  27.3 1.5 %collective-permute-start.12 = (bf16[384,128]{1,0:T(8,128)(2,1)S(1)}, bf16[384,128]{1,0:T(8,128)(2,1)S(1)}, u32[]{:S(2)}, u32[]{:S(2)}) collective-permute-start(bf16[384,128]{1,0:T(8,128)(2,1)S(1)} %get-tuple-element.95), channel_id=1, source_target_pairs={{0,1},{1,0},{2,3},{3,2},{4,5},{5,4},{6,7},{7,6},{8,9},{9,8},{10,11... | collective-permute-start | bytes 294920 | tf_op jit(solution)/shard_map/ppermute | solution.py:299
  31.6 1.6 %collective-permute-start.13 = (bf16[4,96,384]{2,1,0:T(8,128)(2,1)S(1)}, bf16[4,96,384]{2,1,0:T(8,128)(2,1)S(1)}, u32[]{:S(2)}, u32[]{:S(2)}) collective-permute-start(bf16[4,96,384]{2,1,0:T(8,128)(2,1)S(1)} %collective-permute-done.6.refs_4_), channel_id=1, source_target_pairs={{0,1},{1,0},{2,3},{3,2},{4,5},{5,4},{6,7},{7,6},{8,9},{9,8},{10,11... | collective-permute-start | bytes 884744 | tf_op jit(solution)/shard_map/ppermute | solution.py:299
  39.2 1.6 %collective-permute-start.18 = (bf16[4,96,384]{2,1,0:T(8,128)(2,1)S(1)}, bf16[4,96,384]{2,1,0:T(8,128)(2,1)S(1)}, u32[]{:S(2)}, u32[]{:S(2)}) collective-permute-start(bf16[4,96,384]{2,1,0:T(8,128)(2,1)S(1)} %get-tuple-element.74), channel_id=1, source_target_pairs={{0,1},{1,0},{2,3},{3,2},{4,5},{5,4},{6,7},{7,6},{8,9},{9,8},{10,11... | collective-permute-start | bytes 884744 | tf_op jit(solution)/shard_map/ppermute | solution.py:299
  39.6 6.8 %collective-permute-start.17 = (bf16[4,96,384]{2,1,0:T(8,128)(2,1)S(1)}, bf16[4,96,384]{2,1,0:T(8,128)(2,1)S(1)}, u32[]{:S(2)}, u32[]{:S(2)}) collective-permute-start(bf16[4,96,384]{2,1,0:T(8,128)(2,1)S(1)} %get-tuple-element.72), channel_id=1, source_target_pairs={{0,1},{1,0},{2,3},{3,2},{4,5},{5,4},{6,7},{7,6},{8,9},{9,8},{10,11... | collective-permute-start | bytes 884744 | tf_op jit(solution)/shard_map/ppermute | solution.py:299
  40.9 16.4 %collective-permute-start.19 = (bf16[4,96,384]{2,1,0:T(8,128)(2,1)S(1)}, bf16[4,96,384]{2,1,0:T(8,128)(2,1)S(1)}, u32[]{:S(2)}, u32[]{:S(2)}) collective-permute-start(bf16[4,96,384]{2,1,0:T(8,128)(2,1)S(1)} %add_convert_fusion.1), channel_id=1, source_target_pairs={{0,8},{8,0},{1,9},{9,1},{2,10},{10,2},{3,11},{11,3},{4,12},{12,4},... | collective-permute-start | bytes 884744 | tf_op jit(solution)/shard_map/ppermute | solution.py:299
  42.5 18.3 %collective-permute-start.14 = (bf16[2,384,128]{2,1,0:T(8,128)(2,1)S(1)}, bf16[2,384,128]{2,1,0:T(8,128)(2,1)S(1)}, u32[]{:S(2)}, u32[]{:S(2)}) collective-permute-start(bf16[2,384,128]{2,1,0:T(8,128)(2,1)S(1)} %get-tuple-element.64), channel_id=1, source_target_pairs={{0,2},{2,0},{4,6},{6,4},{1,3},{3,1},{5,7},{7,5},{8,10},{10,8},{12,... | collective-permute-start | bytes 589832 | tf_op jit(solution)/shard_map/ppermute | solution.py:299
  42.7 18.3 %collective-permute-start.15 = (bf16[2,384,128]{2,1,0:T(8,128)(2,1)S(1)}, bf16[2,384,128]{2,1,0:T(8,128)(2,1)S(1)}, u32[]{:S(2)}, u32[]{:S(2)}) collective-permute-start(bf16[2,384,128]{2,1,0:T(8,128)(2,1)S(1)} %get-tuple-element.70), channel_id=1, source_target_pairs={{0,4},{2,6},{4,0},{6,2},{1,5},{3,7},{5,1},{7,3},{8,12},{10,14},{12... | collective-permute-start | bytes 589832 | tf_op jit(solution)/shard_map/ppermute | solution.py:299
  46.4 14.7 %collective-permute-start.16 = (bf16[2,384,128]{2,1,0:T(8,128)(2,1)S(1)}, bf16[2,384,128]{2,1,0:T(8,128)(2,1)S(1)}, u32[]{:S(2)}, u32[]{:S(2)}) collective-permute-start(bf16[2,384,128]{2,1,0:T(8,128)(2,1)S(1)} %get-tuple-element.71), channel_id=1, source_target_pairs={{0,6},{2,4},{4,2},{6,0},{1,7},{3,5},{5,3},{7,1},{8,14},{10,12},{12... | collective-permute-start | bytes 589832 | tf_op jit(solution)/shard_map/ppermute | solution.py:299
  57.5 6.0 %collective-permute-start.22 = (bf16[96,384]{1,0:T(8,128)(2,1)S(1)}, bf16[96,384]{1,0:T(8,128)(2,1)S(1)}, u32[]{:S(2)}, u32[]{:S(2)}) collective-permute-start(bf16[96,384]{1,0:T(8,128)(2,1)S(1)} %get-tuple-element.83), channel_id=1, source_target_pairs={{0,6},{2,4},{4,2},{6,0},{1,7},{3,5},{5,3},{7,1},{8,14},{10,12},{12... | collective-permute-start | bytes 221192 | tf_op jit(solution)/shard_map/ppermute | solution.py:299
  57.5 7.3 %collective-permute-start.21 = (bf16[96,384]{1,0:T(8,128)(2,1)S(1)}, bf16[96,384]{1,0:T(8,128)(2,1)S(1)}, u32[]{:S(2)}, u32[]{:S(2)}) collective-permute-start(bf16[96,384]{1,0:T(8,128)(2,1)S(1)} %get-tuple-element.84), channel_id=1, source_target_pairs={{0,4},{2,6},{4,0},{6,2},{1,5},{3,7},{5,1},{7,3},{8,12},{10,14},{12... | collective-permute-start | bytes 221192 | tf_op jit(solution)/shard_map/ppermute | solution.py:299
  60.9 4.4 %collective-permute-start.20 = (bf16[96,384]{1,0:T(8,128)(2,1)S(1)}, bf16[96,384]{1,0:T(8,128)(2,1)S(1)}, u32[]{:S(2)}, u32[]{:S(2)}) collective-permute-start(bf16[96,384]{1,0:T(8,128)(2,1)S(1)} %get-tuple-element.85), channel_id=1, source_target_pairs={{0,2},{2,0},{4,6},{6,4},{1,3},{3,1},{5,7},{7,5},{8,10},{10,8},{12,... | collective-permute-start | bytes 221192 | tf_op jit(solution)/shard_map/ppermute | solution.py:299
  65.3 1.9 %copy-start = (bf16[2,384,128]{2,1,0:T(8,128)(2,1)S(1)}, bf16[2,384,128]{2,1,0:T(8,128)(2,1)}, u32[]{:S(2)}) copy-start(bf16[2,384,128]{2,1,0:T(8,128)(2,1)} %gate.1) | copy-start | bytes 589828
  65.3 1.9 %copy-start.1 = (bf16[2,384,128]{2,1,0:T(8,128)(2,1)S(1)}, bf16[2,384,128]{2,1,0:T(8,128)(2,1)}, u32[]{:S(2)}) copy-start(bf16[2,384,128]{2,1,0:T(8,128)(2,1)} %cot.1) | copy-start | bytes 589828
  65.4 1.8 %collective-permute-start.23 = (bf16[4,384,128]{2,1,0:T(8,128)(2,1)S(1)}, bf16[4,384,128]{2,1,0:T(8,128)(2,1)S(1)}, u32[]{:S(2)}, u32[]{:S(2)}) collective-permute-start(bf16[4,384,128]{2,1,0:T(8,128)(2,1)S(1)} %pad_maximum_fusion.1), channel_id=1, source_target_pairs={{0,1},{1,0},{2,3},{3,2},{4,5},{5,4},{6,7},{7,6},{8,9},{9,8},{10,11... | collective-permute-start | bytes 1179656 | tf_op jit(solution)/shard_map/ppermute | solution.py:299

commit v2 on v0

--- a/solution.py
+++ b/solution.py
@@ -83,24 +83,24 @@
     return lax.dot_general(a, b, dims, preferred_element_type=jnp.float32)
 
 
-def main_kernel(scaling, size, start, relative, begun, ended, opened, closed, split, *refs):
+def main_kernel(scaling, size, blocks, start, relative, begun, ended, opened, closed, split, *refs):
     packs, swapped, (mine, other), refs = refs[:2], refs[2:4], refs[4:6], refs[6:]
     earlier, refs = refs[: 4 if begun else 0], refs[4 if begun else 0 :]
     before, refs = refs[: 1 if opened else 0], refs[1 if opened else 0 :]
     d_bias, refs = refs[: 2 if closed else 1], refs[2 if closed else 1 :]
     results, refs = refs[: 2 + split if ended else 4], refs[2 + split if ended else 4 :]
     q_all, d_all, k_of, v_of, dk_t, dv_t, att_all, dq_all, bias_wide, q_now, d_now, s_now, p_now, low_now, d_low_now, bias_sum = refs
-    step = pl.program_id(0)
+    steps = q_all.shape[0] // (blocks * mine.shape[1]) if not relative else 1
+    step = pl.program_id(0) if steps > 1 else 0
     chip, _, core = places()
     parts, (half, _) = len(packs), packs[0].shape
-    blocks, own, _ = mine.shape
+    own = mine.shape[1]
     lanes = parts * size
 
     def side(i):
         return pl.ds(pl.multiple_of((core ^ i) * half, half), half)
 
-    @pl.when(step == 0)
-    def _():
+    def first():
         lane = lax.broadcasted_iota(jnp.int32, (half, lanes), 1) // size
         for i in range(2):
             here = [(swapped if i else packs)[p][...] for p in range(parts)]
@@ -114,6 +114,8 @@
                 v_of[r, rows] = jnp.where(lane == r, v, 0)
         for i, ref in enumerate((att_all, dq_all, dk_t, dv_t)):
             ref[...] = earlier[i][...] if begun else jnp.zeros_like(ref)
+
+    first() if steps == 1 else pl.when(step == 0)(first)
 
     def strip(i):
         at = start + step * blocks + i
@@ -170,8 +172,7 @@
     if not closed:
         d_bias[0][...] = bias_sum[...]
 
-    @pl.when(step == pl.num_programs(0) - 1)
-    def _():
+    def last():
         if not ended:
             for ref, value in zip(results, (att_all, dq_all, dk_t, dv_t)):
                 ref[...] = value[...]
@@ -187,6 +188,8 @@
                     results[i][...] = pack
                 else:
                     results[p + split][i] = pack
+
+    last() if steps == 1 else pl.when(step == steps - 1)(last)
 
 
 def fixed(value):
@@ -210,14 +213,21 @@
         results = [jax.ShapeDtypeStruct((2, half, width), jnp.bfloat16)] * (parts - split)
         results = ours * split + results
     d_bias = [mine, other] if closed else [wide]
-    return pl.pallas_call(
-        functools.partial(main_kernel, scaling, size, start, relative, bool(earlier), ended, bool(before), closed, split),
-        grid=(strips // blocks,),
-        in_specs=[fixed(one) for one in [*packs, *swapped]]
-        + [strip, strip]
-        + [fixed(one) for one in earlier]
-        + [wide_strip] * len(before),
-        out_specs=([strip] * 2 if closed else [wide_strip]) + [fixed(one) for one in results],
+    grid = {}
+    if not relative:
+        grid = dict(
+            grid=(strips // blocks,),
+            in_specs=[fixed(one) for one in [*packs, *swapped]]
+            + [strip, strip]
+            + [fixed(one) for one in earlier]
+            + [wide_strip] * len(before),
+            out_specs=([strip] * 2 if closed else [wide_strip]) + [fixed(one) for one in results],
+        )
+    return pl.pallas_call(
+        functools.partial(
+            main_kernel, scaling, size, blocks, start, relative, bool(earlier), ended, bool(before), closed, split
+        ),
+        **grid,
         out_shape=[jax.ShapeDtypeStruct(one.shape, one.dtype) for one in d_bias + results],
         scratch_shapes=[
             VMEM(rows.shape, jnp.bfloat16),

time: 67.1 us -> 67.1 us (level)
  no operation moved by 1% of the time
where the time goes in v2:
time: 67.1 us; the launch traced here: 66.9 us
  waiting for transfers between devices  24.7 us (37%)
  starting transfers between devices  23.2 us (35%)
  Pallas kernels  16.6 us (25%)
  local copies, waits for them, and re-layouts  1.17 us (2%)
  between operations  0.9 us (1%)
    ppermute x24, waiting for transfers between devices, swap(): lax.ppermute(value, axes, [(i, i ^ s) for i in range(count)])  24.7 us
    ppermute x24, starting transfers between devices, swap(): lax.ppermute(value, axes, [(i, i ^ s) for i in range(count)])  23.2 us
    pallas_call x4, Pallas kernels, main(): pl.pallas_call(functools.partial(main_kernel, scaling, size, blocks, star...  11.4 us
    pallas_call x1, Pallas kernels, make_packs(): pl.pallas_call(pack_kernel, in_specs=[pl.BlockSpec(memory_space=pl.ANY)]...  2.87 us
    pallas_call x1, Pallas kernels, post(): pl.pallas_call(post_kernel, out_shape=[jax.ShapeDtypeStruct(gate.shape, j...  1.45 us
  transfers between devices with their start and end apart: 24, of which 14 were waited for; matrix products, arithmetic and copies ran while one was open for 1% of the time, Pallas kernels for 18%

profile of v2, /device:TPU:0, one launch (start us, length us, event | category | flops | bytes accessed | tf_op | source)
XLA Modules:
  0.0 66.9 jit_solution(16900973083571129550)
XLA Ops:
  0.6 1.0 %copy-done.3 = bf16[4,96,384]{2,1,0:T(8,128)(2,1)S(1)} copy-done((bf16[4,96,384]{2,1,0:T(8,128)(2,1)S(1)}, bf16[4,96,384]{2,1,0:T(8,128)(2,1)}, u32[]{:S(2)}) %copy-start.3) | copy-done | bytes 294936
  1.6 3.0 %collective-permute-start.3 = (bf16[96,384]{1,0:T(8,128)(2,1)S(1)}, bf16[96,384]{1,0:T(8,128)(2,1)S(1)}, u32[]{:S(2)}, u32[]{:S(2)}) collective-permute-start(bf16[96,384]{1,0:T(8,128)(2,1)S(1)} %get-tuple-element.51), channel_id=1, source_target_pairs={{0,2},{2,0},{4,6},{6,4},{1,3},{3,1},{5,7},{7,5},{8,10},{10,8},{12,... | collective-permute-start | bytes 221192 | tf_op jit(solution)/shard_map/ppermute | solution.py:309
  4.6 1.6 %collective-permute-start.4 = (bf16[96,384]{1,0:T(8,128)(2,1)S(1)}, bf16[96,384]{1,0:T(8,128)(2,1)S(1)}, u32[]{:S(2)}, u32[]{:S(2)}) collective-permute-start(bf16[96,384]{1,0:T(8,128)(2,1)S(1)} %get-tuple-element.52), channel_id=1, source_target_pairs={{0,4},{2,6},{4,0},{6,2},{1,5},{3,7},{5,1},{7,3},{8,12},{10,14},{12... | collective-permute-start | bytes 221192 | tf_op jit(solution)/shard_map/ppermute | solution.py:309
  6.2 2.9 %pack.1 = (bf16[2,384,128]{2,1,0:T(8,128)(2,1)}, bf16[2,384,128]{2,1,0:T(8,128)(2,1)}, bf16[2,384,128]{2,1,0:T(8,128)(2,1)}, bf16[384,128]{1,0:T(8,128)(2,1)}, bf16[384,128]{1,0:T(8,128)(2,1)}) custom-call(bf16[2,384,128]{2,1,0:T(8,128)(2,1)} %refs_0_.1, bf16[2,384,128]{2,1,0:T(8,128)(2,1)} %refs_1_.1, bf16[2,384,128]{2,1,0:T(8,128)(2,1)} %refs_2_.1, ...), custom_call_target="tpu_custom_call" | custom-call | tf_op jit(solution)/shard_map/pack/pallas_call | solution.py:67
  9.1 2.0 %collective-permute-start = (bf16[2,384,128]{2,1,0:T(8,128)(2,1)}, bf16[2,384,128]{2,1,0:T(8,128)(2,1)S(1)}, u32[]{:S(2)}, u32[]{:S(2)}) collective-permute-start(bf16[2,384,128]{2,1,0:T(8,128)(2,1)} %get-tuple-element.47), channel_id=1, source_target_pairs={{0,2},{2,0},{4,6},{6,4},{1,3},{3,1},{5,7},{7,5},{8,10},{10,8},{12,... | collective-permute-start | bytes 589832 | tf_op jit(solution)/shard_map/ppermute | solution.py:309
  11.1 1.6 %collective-permute-start.11 = (bf16[2,384,128]{2,1,0:T(8,128)(2,1)}, bf16[2,384,128]{2,1,0:T(8,128)(2,1)S(1)}, u32[]{:S(2)}, u32[]{:S(2)}) collective-permute-start(bf16[2,384,128]{2,1,0:T(8,128)(2,1)} %get-tuple-element.62), channel_id=1, source_target_pairs={{0,4},{2,6},{4,0},{6,2},{1,5},{3,7},{5,1},{7,3},{8,12},{10,14},{12... | collective-permute-start | bytes 589832 | tf_op jit(solution)/shard_map/ppermute | solution.py:309
  12.9 3.0 %collective-permute-start.6 = (bf16[4,96,384]{2,1,0:T(8,128)(2,1)S(1)}, bf16[4,96,384]{2,1,0:T(8,128)(2,1)S(1)}, u32[]{:S(2)}, u32[]{:S(2)}) collective-permute-start(bf16[4,96,384]{2,1,0:T(8,128)(2,1)S(1)} %maximum_select_fusion.refs_4_), channel_id=1, source_target_pairs={{0,8},{8,0},{1,9},{9,1},{2,10},{10,2},{3,11},{11,3},{4,12},{12,4},... | collective-permute-start | bytes 884744 | tf_op jit(solution)/shard_map/ppermute | solution.py:309
  16.5 1.1 %collective-permute-done.7 = bf16[2,96,384]{2,1,0:T(8,128)(2,1)S(1)} collective-permute-done((bf16[2,96,384]{2,1,0:T(8,128)(2,1)S(1)}, bf16[2,96,384]{2,1,0:T(8,128)(2,1)S(1)}, u32[]{:S(2)}, u32[]{:S(2)}) %collective-permute-start.7) | collective-permute-done | bytes 147488 | tf_op jit(solution)/shard_map/ppermute | solution.py:309
  18.2 0.7 collective-permute-done.1.refs_2_
  18.9 0.4 collective-permute-done.2.refs_3_
  19.3 2.7 %attention.4 = (f32[384,768]{1,0:T(8,128)S(1)}, bf16[768,64]{1,0:T(8,128)(2,1)S(1)}, bf16[768,64]{1,0:T(8,128)(2,1)S(1)}, f32[64,768]{1,0:T(8,128)S(1)}, f32[64,768]{1,0:T(8,128)S(1)}) custom-call(bf16[384,128]{1,0:T(8,128)(2,1)S(1)} %copy-done.2, bf16[384,128]{1,0:T(8,128)(2,1)S(1)} %get-tuple-element.104.refs_1_, ...), custom_call_target="tpu_custom_call" | custom-call | flops 1 | bytes 1 | tf_op jit(solution)/shard_map/attention/pallas_call | solution.py:226
  22.0 3.2 %collective-permute-done.11 = bf16[2,384,128]{2,1,0:T(8,128)(2,1)S(1)} collective-permute-done((bf16[2,384,128]{2,1,0:T(8,128)(2,1)}, bf16[2,384,128]{2,1,0:T(8,128)(2,1)S(1)}, u32[]{:S(2)}, u32[]{:S(2)}) %collective-permute-start.11) | collective-permute-done | bytes 196640 | tf_op jit(solution)/shard_map/ppermute | solution.py:309
  25.2 1.9 %collective-permute-done.12 = bf16[2,384,128]{2,1,0:T(8,128)(2,1)S(1)} collective-permute-done((bf16[2,384,128]{2,1,0:T(8,128)(2,1)}, bf16[2,384,128]{2,1,0:T(8,128)(2,1)S(1)}, u32[]{:S(2)}, u32[]{:S(2)}) %collective-permute-start.12) | collective-permute-done | bytes 196640 | tf_op jit(solution)/shard_map/ppermute | solution.py:309
  27.3 0.5 collective-permute-start.9
  28.0 1.0 %collective-permute-done.9.refs_5_ = bf16[4,96,384]{2,1,0:T(8,128)(2,1)S(1)} collective-permute-done((bf16[4,96,384]{2,1,0:T(8,128)(2,1)S(1)}, bf16[4,96,384]{2,1,0:T(8,128)(2,1)S(1)}, u32[]{:S(2)}, u32[]{:S(2)}) %collective-permute-start.9) | collective-permute-done | bytes 294944 | tf_op jit(solution)/shard_map/ppermute | solution.py:309
  29.0 2.8 %attention.5 = (f32[384,768]{1,0:T(8,128)S(1)}, bf16[384,128]{1,0:T(8,128)(2,1)S(1)}, bf16[384,128]{1,0:T(8,128)(2,1)S(1)}, bf16[2,384,128]{2,1,0:T(8,128)(2,1)S(1)}) custom-call(bf16[384,128]{1,0:T(8,128)(2,1)S(1)} %copy-done.2, bf16[384,128]{1,0:T(8,128)(2,1)S(1)} %get-tuple-element.104.refs_1_, bf16[384,128]{1,0:T(8,128)(2,1)S(1)} %collective-permute-done.1.refs_2_, ...), custom_call_target="tpu_custom_call" | custom-call | flops 1 | bytes 1 | tf_op jit(solution)/shard_map/attention/pallas_call | solution.py:226
  31.9 2.8 %attention.6 = (bf16[4,96,384]{2,1,0:T(8,128)(2,1)S(1)}, bf16[4,96,384]{2,1,0:T(8,128)(2,1)S(1)}, bf16[768,64]{1,0:T(8,128)(2,1)S(1)}, bf16[768,64]{1,0:T(8,128)...) custom-call(bf16[384,128]{1,0:T(8,128)(2,1)S(1)} %get-tuple-element.102.refs_0_, ...), custom_call_target="tpu_custom_call" | custom-call | flops 1 | bytes 1 | tf_op jit(solution)/shard_map/attention/pallas_call | solution.py:226
  34.6 0.4 collective-permute-start.15
  35.1 1.2 %collective-permute-done.15 = bf16[4,96,384]{2,1,0:T(8,128)(2,1)S(1)} collective-permute-done((bf16[4,96,384]{2,1,0:T(8,128)(2,1)S(1)}, bf16[4,96,384]{2,1,0:T(8,128)(2,1)S(1)}, u32[]{:S(2)}, u32[]{:S(2)}) %collective-permute-start.15) | collective-permute-done | bytes 294944 | tf_op jit(solution)/shard_map/ppermute | solution.py:309
  36.4 2.6 %collective-permute-start.18 = (bf16[4,96,384]{2,1,0:T(8,128)(2,1)S(1)}, bf16[4,96,384]{2,1,0:T(8,128)(2,1)S(1)}, u32[]{:S(2)}, u32[]{:S(2)}) collective-permute-start(bf16[4,96,384]{2,1,0:T(8,128)(2,1)S(1)} %add_convert_fusion.1), channel_id=1, source_target_pairs={{0,8},{8,0},{1,9},{9,1},{2,10},{10,2},{3,11},{11,3},{4,12},{12,4},... | collective-permute-start | bytes 884744 | tf_op jit(solution)/shard_map/ppermute | solution.py:309
  38.9 3.1 %attention.7 = (bf16[4,96,384]{2,1,0:T(8,128)(2,1)S(1)}, bf16[4,96,384]{2,1,0:T(8,128)(2,1)S(1)}, bf16[2,384,128]{2,1,0:T(8,128)(2,1)S(1)}, bf16[2,384,128]{2,1,0:T(8,128)(2,1)S(1)}) custom-call(bf16[384,128]{1,0:T(8,128)(2,1)S(1)} %get-tuple-element.102.refs_0_, bf16[384,128]{1,0:T(8,128)(2,1)S(1)} %get-tuple-element.100.refs_1_, ...), custom_call_target="tpu_custom_call" | custom-call | flops 1 | bytes 1 | tf_op jit(solution)/shard_map/attention/pallas_call | solution.py:226
  42.1 0.6 collective-permute-start.10
  42.7 2.8 %collective-permute-start.16 = (bf16[2,384,128]{2,1,0:T(8,128)(2,1)S(1)}, bf16[2,384,128]{2,1,0:T(8,128)(2,1)S(1)}, u32[]{:S(2)}, u32[]{:S(2)}) collective-permute-start(bf16[2,384,128]{2,1,0:T(8,128)(2,1)S(1)} %get-tuple-element.74), channel_id=1, source_target_pairs={{0,4},{2,6},{4,0},{6,2},{1,5},{3,7},{5,1},{7,3},{8,12},{10,14},{12... | collective-permute-start | bytes 589832 | tf_op jit(solution)/shard_map/ppermute | solution.py:309
  45.7 7.4 %collective-permute-done.18 = bf16[4,96,384]{2,1,0:T(8,128)(2,1)S(1)} collective-permute-done((bf16[4,96,384]{2,1,0:T(8,128)(2,1)S(1)}, bf16[4,96,384]{2,1,0:T(8,128)(2,1)S(1)}, u32[]{:S(2)}, u32[]{:S(2)}) %collective-permute-start.18) | collective-permute-done | bytes 294944 | tf_op jit(solution)/shard_map/ppermute | solution.py:309
  53.6 2.8 %collective-permute-start.21 = (bf16[96,384]{1,0:T(8,128)(2,1)S(1)}, bf16[96,384]{1,0:T(8,128)(2,1)S(1)}, u32[]{:S(2)}, u32[]{:S(2)}) collective-permute-start(bf16[96,384]{1,0:T(8,128)(2,1)S(1)} %get-tuple-element.88), channel_id=1, source_target_pairs={{0,4},{2,6},{4,0},{6,2},{1,5},{3,7},{5,1},{7,3},{8,12},{10,14},{12... | collective-permute-start | bytes 221192 | tf_op jit(solution)/shard_map/ppermute | solution.py:309
  56.4 0.4 collective-permute-start.20
  56.8 4.3 %collective-permute-done.17 = bf16[2,384,128]{2,1,0:T(8,128)(2,1)S(1)} collective-permute-done((bf16[2,384,128]{2,1,0:T(8,128)(2,1)S(1)}, bf16[2,384,128]{2,1,0:T(8,128)(2,1)S(1)}, u32[]{:S(2)}, u32[]{:S(2)}) %collective-permute-start.17) | collective-permute-done | bytes 196640 | tf_op jit(solution)/shard_map/ppermute | solution.py:309
  61.1 1.5 %collective-permute-done.22.refs_3_ = bf16[96,384]{1,0:T(8,128)(2,1)S(1)} collective-permute-done((bf16[96,384]{1,0:T(8,128)(2,1)S(1)}, bf16[96,384]{1,0:T(8,128)(2,1)S(1)}, u32[]{:S(2)}, u32[]{:S(2)}) %collective-permute-start.22) | collective-permute-done | bytes 73760 | tf_op jit(solution)/shard_map/ppermute | solution.py:309
  62.7 0.8 %collective-permute-done.20.refs_1_ = bf16[96,384]{1,0:T(8,128)(2,1)S(1)} collective-permute-done((bf16[96,384]{1,0:T(8,128)(2,1)S(1)}, bf16[96,384]{1,0:T(8,128)(2,1)S(1)}, u32[]{:S(2)}, u32[]{:S(2)}) %collective-permute-start.20) | collective-permute-done | bytes 73760 | tf_op jit(solution)/shard_map/ppermute | solution.py:309
  63.7 0.9 %bias_grad.1 = f32[4,96,384]{2,1,0:T(8,128)} custom-call(bf16[96,384]{1,0:T(8,128)(2,1)S(1)} %get-tuple-element.90.refs_0_, bf16[96,384]{1,0:T(8,128)(2,1)S(1)} %collective-permute-done.20.refs_1_, bf16[96,384]{1,0:T(8,128)(2,1)S(1)} %collective-permute-done.21.refs_2_, bf16[96,384]{1,0:T(8,128)(2,1)S(1)} %collective-permute-done.22.refs_3_), custom_call_target="tpu_custom_call" | custom-call | tf_op jit(solution)/shard_map/bias_grad/pallas_call | solution.py:289
  64.6 0.8 %collective-permute-done.23.swapped = bf16[4,384,128]{2,1,0:T(8,128)(2,1)S(1)} collective-permute-done((bf16[4,384,128]{2,1,0:T(8,128)(2,1)S(1)}, bf16[4,384,128]{2,1,0:T(8,128)(2,1)S(1)}, u32[]{:S(2)}, u32[]{:S(2)}) %collective-permute-start.23) | collective-permute-done | bytes 393248 | tf_op jit(solution)/shard_map/ppermute | solution.py:309
  65.4 1.5 %unpack.1 = (bf16[2,384,128]{2,1,0:T(8,128)(2,1)}, bf16[2,384,128]{2,1,0:T(8,128)(2,1)}, bf16[2,384,128]{2,1,0:T(8,128)(2,1)}, bf16[2,384,128]{2,1,0:T(8,128)(2,1)}) custom-call(bf16[2,384,128]{2,1,0:T(8,128)(2,1)S(1)} %copy-done, bf16[2,384,128]{2,1,0:T(8,128)(2,1)S(1)} %copy-done.1, bf16[4,384,128]{2,1,0:T(8,128)(2,1)S(1)} %pad_maximum_fusion.packs, ...), custom_call_target="tpu_custom_call" | custom-call | tf_op jit(solution)/shard_map/unpack/pallas_call | solution.py:273
  (52 shorter events, 2.8 us)
Async XLA Ops:
  0.6 1.0 %copy-start.3 = (bf16[4,96,384]{2,1,0:T(8,128)(2,1)S(1)}, bf16[4,96,384]{2,1,0:T(8,128)(2,1)}, u32[]{:S(2)}) copy-start(bf16[4,96,384]{2,1,0:T(8,128)(2,1)} %bias.1) | copy-start | bytes 884740
  1.6 11.1 %copy-start.4 = (s32[384]{0:T(512)S(1)}, s32[384]{0:T(512)}, u32[]{:S(2)}) copy-start(s32[384]{0:T(512)} %param.12) | copy-start | bytes 4612
  1.6 11.1 %collective-permute-start.3 = (bf16[96,384]{1,0:T(8,128)(2,1)S(1)}, bf16[96,384]{1,0:T(8,128)(2,1)S(1)}, u32[]{:S(2)}, u32[]{:S(2)}) collective-permute-start(bf16[96,384]{1,0:T(8,128)(2,1)S(1)} %get-tuple-element.51), channel_id=1, source_target_pairs={{0,2},{2,0},{4,6},{6,4},{1,3},{3,1},{5,7},{7,5},{8,10},{10,8},{12,... | collective-permute-start | bytes 221192 | tf_op jit(solution)/shard_map/ppermute | solution.py:309
  4.6 8.1 %collective-permute-start.4 = (bf16[96,384]{1,0:T(8,128)(2,1)S(1)}, bf16[96,384]{1,0:T(8,128)(2,1)S(1)}, u32[]{:S(2)}, u32[]{:S(2)}) collective-permute-start(bf16[96,384]{1,0:T(8,128)(2,1)S(1)} %get-tuple-element.52), channel_id=1, source_target_pairs={{0,4},{2,6},{4,0},{6,2},{1,5},{3,7},{5,1},{7,3},{8,12},{10,14},{12... | collective-permute-start | bytes 221192 | tf_op jit(solution)/shard_map/ppermute | solution.py:309
  6.2 6.6 %collective-permute-start.5 = (bf16[96,384]{1,0:T(8,128)(2,1)S(1)}, bf16[96,384]{1,0:T(8,128)(2,1)S(1)}, u32[]{:S(2)}, u32[]{:S(2)}) collective-permute-start(bf16[96,384]{1,0:T(8,128)(2,1)S(1)} %get-tuple-element.53), channel_id=1, source_target_pairs={{0,6},{2,4},{4,2},{6,0},{1,7},{3,5},{5,3},{7,1},{8,14},{10,12},{12... | collective-permute-start | bytes 221192 | tf_op jit(solution)/shard_map/ppermute | solution.py:309
  9.1 8.5 %copy-start.5 = (bf16[384,128]{1,0:T(8,128)(2,1)S(1)}, bf16[384,128]{1,0:T(8,128)(2,1)}, u32[]{:S(2)}) copy-start(bf16[384,128]{1,0:T(8,128)(2,1)} %get-tuple-element.49) | copy-start | bytes 294916
  9.1 10.2 %copy-start.2 = (bf16[384,128]{1,0:T(8,128)(2,1)S(1)}, bf16[384,128]{1,0:T(8,128)(2,1)}, u32[]{:S(2)}) copy-start(bf16[384,128]{1,0:T(8,128)(2,1)} %get-tuple-element.46.refs_0_) | copy-start | bytes 294916
  9.1 7.1 %collective-permute-start = (bf16[2,384,128]{2,1,0:T(8,128)(2,1)}, bf16[2,384,128]{2,1,0:T(8,128)(2,1)S(1)}, u32[]{:S(2)}, u32[]{:S(2)}) collective-permute-start(bf16[2,384,128]{2,1,0:T(8,128)(2,1)} %get-tuple-element.47), channel_id=1, source_target_pairs={{0,2},{2,0},{4,6},{6,4},{1,3},{3,1},{5,7},{7,5},{8,10},{10,8},{12,... | collective-permute-start | bytes 589832 | tf_op jit(solution)/shard_map/ppermute | solution.py:309
  11.1 14.2 %collective-permute-start.11 = (bf16[2,384,128]{2,1,0:T(8,128)(2,1)}, bf16[2,384,128]{2,1,0:T(8,128)(2,1)S(1)}, u32[]{:S(2)}, u32[]{:S(2)}) collective-permute-start(bf16[2,384,128]{2,1,0:T(8,128)(2,1)} %get-tuple-element.62), channel_id=1, source_target_pairs={{0,4},{2,6},{4,0},{6,2},{1,5},{3,7},{5,1},{7,3},{8,12},{10,14},{12... | collective-permute-start | bytes 589832 | tf_op jit(solution)/shard_map/ppermute | solution.py:309
  12.7 14.5 %collective-permute-start.12 = (bf16[2,384,128]{2,1,0:T(8,128)(2,1)}, bf16[2,384,128]{2,1,0:T(8,128)(2,1)S(1)}, u32[]{:S(2)}, u32[]{:S(2)}) collective-permute-start(bf16[2,384,128]{2,1,0:T(8,128)(2,1)} %get-tuple-element.63), channel_id=1, source_target_pairs={{0,6},{2,4},{4,2},{6,0},{1,7},{3,5},{5,3},{7,1},{8,14},{10,12},{12... | collective-permute-start | bytes 589832 | tf_op jit(solution)/shard_map/ppermute | solution.py:309
  12.9 14.4 %collective-permute-start.6 = (bf16[4,96,384]{2,1,0:T(8,128)(2,1)S(1)}, bf16[4,96,384]{2,1,0:T(8,128)(2,1)S(1)}, u32[]{:S(2)}, u32[]{:S(2)}) collective-permute-start(bf16[4,96,384]{2,1,0:T(8,128)(2,1)S(1)} %maximum_select_fusion.refs_4_), channel_id=1, source_target_pairs={{0,8},{8,0},{1,9},{9,1},{2,10},{10,2},{3,11},{11,3},{4,12},{12,4},... | collective-permute-start | bytes 884744 | tf_op jit(solution)/shard_map/ppermute | solution.py:309
  15.9 2.0 %collective-permute-start.8 = (bf16[2,96,384]{2,1,0:T(8,128)(2,1)S(1)}, bf16[2,96,384]{2,1,0:T(8,128)(2,1)S(1)}, u32[]{:S(2)}, u32[]{:S(2)}) collective-permute-start(bf16[2,96,384]{2,1,0:T(8,128)(2,1)S(1)} %get-tuple-element.91), channel_id=1, source_target_pairs={{0,1},{1,0},{2,3},{3,2},{4,5},{5,4},{6,7},{7,6},{8,9},{9,8},{10,11... | collective-permute-start | bytes 442376 | tf_op jit(solution)/shard_map/ppermute | solution.py:309
  16.2 1.4 %collective-permute-start.7 = (bf16[2,96,384]{2,1,0:T(8,128)(2,1)S(1)}, bf16[2,96,384]{2,1,0:T(8,128)(2,1)S(1)}, u32[]{:S(2)}, u32[]{:S(2)}) collective-permute-start(bf16[2,96,384]{2,1,0:T(8,128)(2,1)S(1)} %get-tuple-element.92), channel_id=1, source_target_pairs={{0,1},{1,0},{2,3},{3,2},{4,5},{5,4},{6,7},{7,6},{8,9},{9,8},{10,11... | collective-permute-start | bytes 442376 | tf_op jit(solution)/shard_map/ppermute | solution.py:309
  17.6 1.3 %collective-permute-start.1 = (bf16[384,128]{1,0:T(8,128)(2,1)S(1)}, bf16[384,128]{1,0:T(8,128)(2,1)S(1)}, u32[]{:S(2)}, u32[]{:S(2)}) collective-permute-start(bf16[384,128]{1,0:T(8,128)(2,1)S(1)} %copy-done.5), channel_id=1, source_target_pairs={{0,1},{1,0},{2,3},{3,2},{4,5},{5,4},{6,7},{7,6},{8,9},{9,8},{10,11... | collective-permute-start | bytes 294920 | tf_op jit(solution)/shard_map/ppermute | solution.py:309
  17.9 1.4 %collective-permute-start.2 = (bf16[384,128]{1,0:T(8,128)(2,1)S(1)}, bf16[384,128]{1,0:T(8,128)(2,1)S(1)}, u32[]{:S(2)}, u32[]{:S(2)}) collective-permute-start(bf16[384,128]{1,0:T(8,128)(2,1)S(1)} %get-tuple-element.103), channel_id=1, source_target_pairs={{0,1},{1,0},{2,3},{3,2},{4,5},{5,4},{6,7},{7,6},{8,9},{9,8},{10,11... | collective-permute-start | bytes 294920 | tf_op jit(solution)/shard_map/ppermute | solution.py:309
  27.2 4.6 %collective-permute-start.13 = (bf16[384,128]{1,0:T(8,128)(2,1)S(1)}, bf16[384,128]{1,0:T(8,128)(2,1)S(1)}, u32[]{:S(2)}, u32[]{:S(2)}) collective-permute-start(bf16[384,128]{1,0:T(8,128)(2,1)S(1)} %get-tuple-element.101), channel_id=1, source_target_pairs={{0,1},{1,0},{2,3},{3,2},{4,5},{5,4},{6,7},{7,6},{8,9},{9,8},{10,11... | collective-permute-start | bytes 294920 | tf_op jit(solution)/shard_map/ppermute | solution.py:309
  27.3 1.7 %collective-permute-start.9 = (bf16[4,96,384]{2,1,0:T(8,128)(2,1)S(1)}, bf16[4,96,384]{2,1,0:T(8,128)(2,1)S(1)}, u32[]{:S(2)}, u32[]{:S(2)}) collective-permute-start(bf16[4,96,384]{2,1,0:T(8,128)(2,1)S(1)} %collective-permute-done.6.refs_4_), channel_id=1, source_target_pairs={{0,1},{1,0},{2,3},{3,2},{4,5},{5,4},{6,7},{7,6},{8,9},{9,8},{10,11... | collective-permute-start | bytes 884744 | tf_op jit(solution)/shard_map/ppermute | solution.py:309
  27.8 4.0 %collective-permute-start.14 = (bf16[384,128]{1,0:T(8,128)(2,1)S(1)}, bf16[384,128]{1,0:T(8,128)(2,1)S(1)}, u32[]{:S(2)}, u32[]{:S(2)}) collective-permute-start(bf16[384,128]{1,0:T(8,128)(2,1)S(1)} %get-tuple-element.99), channel_id=1, source_target_pairs={{0,1},{1,0},{2,3},{3,2},{4,5},{5,4},{6,7},{7,6},{8,9},{9,8},{10,11... | collective-permute-start | bytes 294920 | tf_op jit(solution)/shard_map/ppermute | solution.py:309
  34.6 1.7 %collective-permute-start.15 = (bf16[4,96,384]{2,1,0:T(8,128)(2,1)S(1)}, bf16[4,96,384]{2,1,0:T(8,128)(2,1)S(1)}, u32[]{:S(2)}, u32[]{:S(2)}) collective-permute-start(bf16[4,96,384]{2,1,0:T(8,128)(2,1)S(1)} %get-tuple-element.68), channel_id=1, source_target_pairs={{0,1},{1,0},{2,3},{3,2},{4,5},{5,4},{6,7},{7,6},{8,9},{9,8},{10,11... | collective-permute-start | bytes 884744 | tf_op jit(solution)/shard_map/ppermute | solution.py:309
  36.4 16.7 %collective-permute-start.18 = (bf16[4,96,384]{2,1,0:T(8,128)(2,1)S(1)}, bf16[4,96,384]{2,1,0:T(8,128)(2,1)S(1)}, u32[]{:S(2)}, u32[]{:S(2)}) collective-permute-start(bf16[4,96,384]{2,1,0:T(8,128)(2,1)S(1)} %add_convert_fusion.1), channel_id=1, source_target_pairs={{0,8},{8,0},{1,9},{9,1},{2,10},{10,2},{3,11},{11,3},{4,12},{12,4},... | collective-permute-start | bytes 884744 | tf_op jit(solution)/shard_map/ppermute | solution.py:309
  42.0 11.1 %collective-permute-start.19 = (bf16[4,96,384]{2,1,0:T(8,128)(2,1)S(1)}, bf16[4,96,384]{2,1,0:T(8,128)(2,1)S(1)}, u32[]{:S(2)}, u32[]{:S(2)}) collective-permute-start(bf16[4,96,384]{2,1,0:T(8,128)(2,1)S(1)} %get-tuple-element.78), channel_id=1, source_target_pairs={{0,1},{1,0},{2,3},{3,2},{4,5},{5,4},{6,7},{7,6},{8,9},{9,8},{10,11... | collective-permute-start | bytes 884744 | tf_op jit(solution)/shard_map/ppermute | solution.py:309
  42.1 14.3 %collective-permute-start.10 = (bf16[2,384,128]{2,1,0:T(8,128)(2,1)S(1)}, bf16[2,384,128]{2,1,0:T(8,128)(2,1)S(1)}, u32[]{:S(2)}, u32[]{:S(2)}) collective-permute-start(bf16[2,384,128]{2,1,0:T(8,128)(2,1)S(1)} %get-tuple-element.61), channel_id=1, source_target_pairs={{0,2},{2,0},{4,6},{6,4},{1,3},{3,1},{5,7},{7,5},{8,10},{10,8},{12,... | collective-permute-start | bytes 589832 | tf_op jit(solution)/shard_map/ppermute | solution.py:309
  42.7 14.1 %collective-permute-start.16 = (bf16[2,384,128]{2,1,0:T(8,128)(2,1)S(1)}, bf16[2,384,128]{2,1,0:T(8,128)(2,1)S(1)}, u32[]{:S(2)}, u32[]{:S(2)}) collective-permute-start(bf16[2,384,128]{2,1,0:T(8,128)(2,1)S(1)} %get-tuple-element.74), channel_id=1, source_target_pairs={{0,4},{2,6},{4,0},{6,2},{1,5},{3,7},{5,1},{7,3},{8,12},{10,14},{12... | collective-permute-start | bytes 589832 | tf_op jit(solution)/shard_map/ppermute | solution.py:309
  45.5 15.5 %collective-permute-start.17 = (bf16[2,384,128]{2,1,0:T(8,128)(2,1)S(1)}, bf16[2,384,128]{2,1,0:T(8,128)(2,1)S(1)}, u32[]{:S(2)}, u32[]{:S(2)}) collective-permute-start(bf16[2,384,128]{2,1,0:T(8,128)(2,1)S(1)} %get-tuple-element.75), channel_id=1, source_target_pairs={{0,6},{2,4},{4,2},{6,0},{1,7},{3,5},{5,3},{7,1},{8,14},{10,12},{12... | collective-permute-start | bytes 589832 | tf_op jit(solution)/shard_map/ppermute | solution.py:309
  53.2 9.4 %collective-permute-start.22 = (bf16[96,384]{1,0:T(8,128)(2,1)S(1)}, bf16[96,384]{1,0:T(8,128)(2,1)S(1)}, u32[]{:S(2)}, u32[]{:S(2)}) collective-permute-start(bf16[96,384]{1,0:T(8,128)(2,1)S(1)} %get-tuple-element.87), channel_id=1, source_target_pairs={{0,6},{2,4},{4,2},{6,0},{1,7},{3,5},{5,3},{7,1},{8,14},{10,12},{12... | collective-permute-start | bytes 221192 | tf_op jit(solution)/shard_map/ppermute | solution.py:309
  53.6 9.1 %collective-permute-start.21 = (bf16[96,384]{1,0:T(8,128)(2,1)S(1)}, bf16[96,384]{1,0:T(8,128)(2,1)S(1)}, u32[]{:S(2)}, u32[]{:S(2)}) collective-permute-start(bf16[96,384]{1,0:T(8,128)(2,1)S(1)} %get-tuple-element.88), channel_id=1, source_target_pairs={{0,4},{2,6},{4,0},{6,2},{1,5},{3,7},{5,1},{7,3},{8,12},{10,14},{12... | collective-permute-start | bytes 221192 | tf_op jit(solution)/shard_map/ppermute | solution.py:309
  56.4 7.1 %collective-permute-start.20 = (bf16[96,384]{1,0:T(8,128)(2,1)S(1)}, bf16[96,384]{1,0:T(8,128)(2,1)S(1)}, u32[]{:S(2)}, u32[]{:S(2)}) collective-permute-start(bf16[96,384]{1,0:T(8,128)(2,1)S(1)} %get-tuple-element.89), channel_id=1, source_target_pairs={{0,2},{2,0},{4,6},{6,4},{1,3},{3,1},{5,7},{7,5},{8,10},{10,8},{12,... | collective-permute-start | bytes 221192 | tf_op jit(solution)/shard_map/ppermute | solution.py:309
  63.6 1.9 %copy-start = (bf16[2,384,128]{2,1,0:T(8,128)(2,1)S(1)}, bf16[2,384,128]{2,1,0:T(8,128)(2,1)}, u32[]{:S(2)}) copy-start(bf16[2,384,128]{2,1,0:T(8,128)(2,1)} %gate.1) | copy-start | bytes 589828
  63.6 1.9 %copy-start.1 = (bf16[2,384,128]{2,1,0:T(8,128)(2,1)S(1)}, bf16[2,384,128]{2,1,0:T(8,128)(2,1)}, u32[]{:S(2)}) copy-start(bf16[2,384,128]{2,1,0:T(8,128)(2,1)} %cot.1) | copy-start | bytes 589828
  63.6 1.8 %collective-permute-start.23 = (bf16[4,384,128]{2,1,0:T(8,128)(2,1)S(1)}, bf16[4,384,128]{2,1,0:T(8,128)(2,1)S(1)}, u32[]{:S(2)}, u32[]{:S(2)}) collective-permute-start(bf16[4,384,128]{2,1,0:T(8,128)(2,1)S(1)} %pad_maximum_fusion.1), channel_id=1, source_target_pairs={{0,1},{1,0},{2,3},{3,2},{4,5},{5,4},{6,7},{7,6},{8,9},{9,8},{10,11... | collective-permute-start | bytes 1179656 | tf_op jit(solution)/shard_map/ppermute | solution.py:309

commit v3 on v2

--- a/solution.py
+++ b/solution.py
@@ -10,7 +10,7 @@
 
 PAIR = 2
 NEAR_PARTS = 2
-ROWS_AT_ONCE = 16
+ROWS_AT_ONCE = 32
 VMEM = pltpu.VMEM
 PARAMS = pltpu.CompilerParams(vmem_limit_bytes=32 * 1024 * 1024)
 PRE_PARAMS = pltpu.CompilerParams(vmem_limit_bytes=60 * 1024 * 1024)
@@ -144,9 +144,10 @@
             rows = slice(at, at + ROWS_AT_ONCE)
             logits = s_now[r % 2, rows] * scaling + bias_wide[rows]
             expo = jnp.exp(logits - jnp.max(logits, axis=-1, keepdims=True))
-            probs = expo * (1.0 / jnp.sum(expo, axis=-1, keepdims=True))
             d_probs = p_now[r % 2, rows]
-            inner = jnp.sum(probs * d_probs, axis=-1, keepdims=True)
+            inverse = 1.0 / jnp.sum(expo, axis=-1, keepdims=True)
+            inner = jnp.sum(expo * d_probs, axis=-1, keepdims=True) * inverse
+            probs = expo * inverse
             d_logits = probs * (d_probs - inner)
             low_now[r % 2, rows] = probs.astype(jnp.bfloat16)
             d_low_now[r % 2, rows] = d_logits.astype(jnp.bfloat16)

time: 67.1 us -> 67.4 us (level)
  transfers between devices with their start and end apart: 24 -> 24, of which waited for: 14 -> 14; matrix products, arithmetic and copies ran while one was open for 1% -> 1% of each run, Pallas kernels for 18% -> 19%
where the time goes in v3:
time: 67.4 us; the launch traced here: 67.2 us
  waiting for transfers between devices  24.6 us (36%)
  starting transfers between devices  23.2 us (34%)
  Pallas kernels  17 us (25%)
  local copies, waits for them, and re-layouts  1.17 us (2%)
  between operations  0.9 us (1%)
    ppermute x24, waiting for transfers between devices, swap(): lax.ppermute(value, axes, [(i, i ^ s) for i in range(count)])  24.6 us
    ppermute x24, starting transfers between devices, swap(): lax.ppermute(value, axes, [(i, i ^ s) for i in range(count)])  23.2 us
    pallas_call x4, Pallas kernels, main(): pl.pallas_call(functools.partial(main_kernel, scaling, size, blocks, star...  11.8 us
    pallas_call x1, Pallas kernels, make_packs(): pl.pallas_call(pack_kernel, in_specs=[pl.BlockSpec(memory_space=pl.ANY)]...  2.87 us
    pallas_call x1, Pallas kernels, post(): pl.pallas_call(post_kernel, out_shape=[jax.ShapeDtypeStruct(gate.shape, j...  1.45 us
  transfers between devices with their start and end apart: 24, of which 14 were waited for; matrix products, arithmetic and copies ran while one was open for 1% of the time, Pallas kernels for 19%

profile of v3, /device:TPU:0, one launch (start us, length us, event | category | flops | bytes accessed | tf_op | source)
XLA Modules:
  0.0 67.2 jit_solution(16422688127230246519)
XLA Ops:
  0.6 1.0 %copy-done.3 = bf16[4,96,384]{2,1,0:T(8,128)(2,1)S(1)} copy-done((bf16[4,96,384]{2,1,0:T(8,128)(2,1)S(1)}, bf16[4,96,384]{2,1,0:T(8,128)(2,1)}, u32[]{:S(2)}) %copy-start.3) | copy-done | bytes 294936
  1.6 3.0 %collective-permute-start.3 = (bf16[96,384]{1,0:T(8,128)(2,1)S(1)}, bf16[96,384]{1,0:T(8,128)(2,1)S(1)}, u32[]{:S(2)}, u32[]{:S(2)}) collective-permute-start(bf16[96,384]{1,0:T(8,128)(2,1)S(1)} %get-tuple-element.51), channel_id=1, source_target_pairs={{0,2},{2,0},{4,6},{6,4},{1,3},{3,1},{5,7},{7,5},{8,10},{10,8},{12,... | collective-permute-start | bytes 221192 | tf_op jit(solution)/shard_map/ppermute | solution.py:310
  4.6 1.6 %collective-permute-start.4 = (bf16[96,384]{1,0:T(8,128)(2,1)S(1)}, bf16[96,384]{1,0:T(8,128)(2,1)S(1)}, u32[]{:S(2)}, u32[]{:S(2)}) collective-permute-start(bf16[96,384]{1,0:T(8,128)(2,1)S(1)} %get-tuple-element.52), channel_id=1, source_target_pairs={{0,4},{2,6},{4,0},{6,2},{1,5},{3,7},{5,1},{7,3},{8,12},{10,14},{12... | collective-permute-start | bytes 221192 | tf_op jit(solution)/shard_map/ppermute | solution.py:310
  6.2 2.9 %pack.1 = (bf16[2,384,128]{2,1,0:T(8,128)(2,1)}, bf16[2,384,128]{2,1,0:T(8,128)(2,1)}, bf16[2,384,128]{2,1,0:T(8,128)(2,1)}, bf16[384,128]{1,0:T(8,128)(2,1)}, bf16[384,128]{1,0:T(8,128)(2,1)}) custom-call(bf16[2,384,128]{2,1,0:T(8,128)(2,1)} %refs_0_.1, bf16[2,384,128]{2,1,0:T(8,128)(2,1)} %refs_1_.1, bf16[2,384,128]{2,1,0:T(8,128)(2,1)} %refs_2_.1, ...), custom_call_target="tpu_custom_call" | custom-call | tf_op jit(solution)/shard_map/pack/pallas_call | solution.py:67
  9.1 2.0 %collective-permute-start = (bf16[2,384,128]{2,1,0:T(8,128)(2,1)}, bf16[2,384,128]{2,1,0:T(8,128)(2,1)S(1)}, u32[]{:S(2)}, u32[]{:S(2)}) collective-permute-start(bf16[2,384,128]{2,1,0:T(8,128)(2,1)} %get-tuple-element.47), channel_id=1, source_target_pairs={{0,2},{2,0},{4,6},{6,4},{1,3},{3,1},{5,7},{7,5},{8,10},{10,8},{12,... | collective-permute-start | bytes 589832 | tf_op jit(solution)/shard_map/ppermute | solution.py:310
  11.1 1.6 %collective-permute-start.11 = (bf16[2,384,128]{2,1,0:T(8,128)(2,1)}, bf16[2,384,128]{2,1,0:T(8,128)(2,1)S(1)}, u32[]{:S(2)}, u32[]{:S(2)}) collective-permute-start(bf16[2,384,128]{2,1,0:T(8,128)(2,1)} %get-tuple-element.62), channel_id=1, source_target_pairs={{0,4},{2,6},{4,0},{6,2},{1,5},{3,7},{5,1},{7,3},{8,12},{10,14},{12... | collective-permute-start | bytes 589832 | tf_op jit(solution)/shard_map/ppermute | solution.py:310
  12.9 3.0 %collective-permute-start.6 = (bf16[4,96,384]{2,1,0:T(8,128)(2,1)S(1)}, bf16[4,96,384]{2,1,0:T(8,128)(2,1)S(1)}, u32[]{:S(2)}, u32[]{:S(2)}) collective-permute-start(bf16[4,96,384]{2,1,0:T(8,128)(2,1)S(1)} %maximum_select_fusion.refs_4_), channel_id=1, source_target_pairs={{0,8},{8,0},{1,9},{9,1},{2,10},{10,2},{3,11},{11,3},{4,12},{12,4},... | collective-permute-start | bytes 884744 | tf_op jit(solution)/shard_map/ppermute | solution.py:310
  16.5 1.1 %collective-permute-done.7 = bf16[2,96,384]{2,1,0:T(8,128)(2,1)S(1)} collective-permute-done((bf16[2,96,384]{2,1,0:T(8,128)(2,1)S(1)}, bf16[2,96,384]{2,1,0:T(8,128)(2,1)S(1)}, u32[]{:S(2)}, u32[]{:S(2)}) %collective-permute-start.7) | collective-permute-done | bytes 147488 | tf_op jit(solution)/shard_map/ppermute | solution.py:310
  18.2 0.7 collective-permute-done.1.refs_2_
  18.9 0.4 collective-permute-done.2.refs_3_
  19.3 2.8 %attention.4 = (f32[384,768]{1,0:T(8,128)S(1)}, bf16[768,64]{1,0:T(8,128)(2,1)S(1)}, bf16[768,64]{1,0:T(8,128)(2,1)S(1)}, f32[64,768]{1,0:T(8,128)S(1)}, f32[64,768]{1,0:T(8,128)S(1)}) custom-call(bf16[384,128]{1,0:T(8,128)(2,1)S(1)} %copy-done.2, bf16[384,128]{1,0:T(8,128)(2,1)S(1)} %get-tuple-element.104.refs_1_, ...), custom_call_target="tpu_custom_call" | custom-call | flops 1 | bytes 1 | tf_op jit(solution)/shard_map/attention/pallas_call | solution.py:227
  22.1 3.1 %collective-permute-done.11 = bf16[2,384,128]{2,1,0:T(8,128)(2,1)S(1)} collective-permute-done((bf16[2,384,128]{2,1,0:T(8,128)(2,1)}, bf16[2,384,128]{2,1,0:T(8,128)(2,1)S(1)}, u32[]{:S(2)}, u32[]{:S(2)}) %collective-permute-start.11) | collective-permute-done | bytes 196640 | tf_op jit(solution)/shard_map/ppermute | solution.py:310
  25.2 1.9 %collective-permute-done.12 = bf16[2,384,128]{2,1,0:T(8,128)(2,1)S(1)} collective-permute-done((bf16[2,384,128]{2,1,0:T(8,128)(2,1)}, bf16[2,384,128]{2,1,0:T(8,128)(2,1)S(1)}, u32[]{:S(2)}, u32[]{:S(2)}) %collective-permute-start.12) | collective-permute-done | bytes 196640 | tf_op jit(solution)/shard_map/ppermute | solution.py:310
  27.3 0.5 collective-permute-start.9
  28.0 1.0 %collective-permute-done.9.refs_5_ = bf16[4,96,384]{2,1,0:T(8,128)(2,1)S(1)} collective-permute-done((bf16[4,96,384]{2,1,0:T(8,128)(2,1)S(1)}, bf16[4,96,384]{2,1,0:T(8,128)(2,1)S(1)}, u32[]{:S(2)}, u32[]{:S(2)}) %collective-permute-start.9) | collective-permute-done | bytes 294944 | tf_op jit(solution)/shard_map/ppermute | solution.py:310
  29.0 3.0 %attention.5 = (f32[384,768]{1,0:T(8,128)S(1)}, bf16[384,128]{1,0:T(8,128)(2,1)S(1)}, bf16[384,128]{1,0:T(8,128)(2,1)S(1)}, bf16[2,384,128]{2,1,0:T(8,128)(2,1)S(1)}) custom-call(bf16[384,128]{1,0:T(8,128)(2,1)S(1)} %copy-done.2, bf16[384,128]{1,0:T(8,128)(2,1)S(1)} %get-tuple-element.104.refs_1_, bf16[384,128]{1,0:T(8,128)(2,1)S(1)} %collective-permute-done.1.refs_2_, ...), custom_call_target="tpu_custom_call" | custom-call | flops 1 | bytes 1 | tf_op jit(solution)/shard_map/attention/pallas_call | solution.py:227
  32.0 2.8 %attention.6 = (bf16[4,96,384]{2,1,0:T(8,128)(2,1)S(1)}, bf16[4,96,384]{2,1,0:T(8,128)(2,1)S(1)}, bf16[768,64]{1,0:T(8,128)(2,1)S(1)}, bf16[768,64]{1,0:T(8,128)...) custom-call(bf16[384,128]{1,0:T(8,128)(2,1)S(1)} %get-tuple-element.102.refs_0_, ...), custom_call_target="tpu_custom_call" | custom-call | flops 1 | bytes 1 | tf_op jit(solution)/shard_map/attention/pallas_call | solution.py:227
  34.9 0.4 collective-permute-start.15
  35.3 1.2 %collective-permute-done.15 = bf16[4,96,384]{2,1,0:T(8,128)(2,1)S(1)} collective-permute-done((bf16[4,96,384]{2,1,0:T(8,128)(2,1)S(1)}, bf16[4,96,384]{2,1,0:T(8,128)(2,1)S(1)}, u32[]{:S(2)}, u32[]{:S(2)}) %collective-permute-start.15) | collective-permute-done | bytes 294944 | tf_op jit(solution)/shard_map/ppermute | solution.py:310
  36.6 2.6 %collective-permute-start.18 = (bf16[4,96,384]{2,1,0:T(8,128)(2,1)S(1)}, bf16[4,96,384]{2,1,0:T(8,128)(2,1)S(1)}, u32[]{:S(2)}, u32[]{:S(2)}) collective-permute-start(bf16[4,96,384]{2,1,0:T(8,128)(2,1)S(1)} %add_convert_fusion.1), channel_id=1, source_target_pairs={{0,8},{8,0},{1,9},{9,1},{2,10},{10,2},{3,11},{11,3},{4,12},{12,4},... | collective-permute-start | bytes 884744 | tf_op jit(solution)/shard_map/ppermute | solution.py:310
  39.2 3.2 %attention.7 = (bf16[4,96,384]{2,1,0:T(8,128)(2,1)S(1)}, bf16[4,96,384]{2,1,0:T(8,128)(2,1)S(1)}, bf16[2,384,128]{2,1,0:T(8,128)(2,1)S(1)}, bf16[2,384,128]{2,1,0:T(8,128)(2,1)S(1)}) custom-call(bf16[384,128]{1,0:T(8,128)(2,1)S(1)} %get-tuple-element.102.refs_0_, bf16[384,128]{1,0:T(8,128)(2,1)S(1)} %get-tuple-element.100.refs_1_, ...), custom_call_target="tpu_custom_call" | custom-call | flops 1 | bytes 1 | tf_op jit(solution)/shard_map/attention/pallas_call | solution.py:227
  42.4 0.6 collective-permute-start.10
  43.0 2.8 %collective-permute-start.16 = (bf16[2,384,128]{2,1,0:T(8,128)(2,1)S(1)}, bf16[2,384,128]{2,1,0:T(8,128)(2,1)S(1)}, u32[]{:S(2)}, u32[]{:S(2)}) collective-permute-start(bf16[2,384,128]{2,1,0:T(8,128)(2,1)S(1)} %get-tuple-element.74), channel_id=1, source_target_pairs={{0,4},{2,6},{4,0},{6,2},{1,5},{3,7},{5,1},{7,3},{8,12},{10,14},{12... | collective-permute-start | bytes 589832 | tf_op jit(solution)/shard_map/ppermute | solution.py:310
  46.0 7.3 %collective-permute-done.18 = bf16[4,96,384]{2,1,0:T(8,128)(2,1)S(1)} collective-permute-done((bf16[4,96,384]{2,1,0:T(8,128)(2,1)S(1)}, bf16[4,96,384]{2,1,0:T(8,128)(2,1)S(1)}, u32[]{:S(2)}, u32[]{:S(2)}) %collective-permute-start.18) | collective-permute-done | bytes 294944 | tf_op jit(solution)/shard_map/ppermute | solution.py:310
  53.8 2.8 %collective-permute-start.21 = (bf16[96,384]{1,0:T(8,128)(2,1)S(1)}, bf16[96,384]{1,0:T(8,128)(2,1)S(1)}, u32[]{:S(2)}, u32[]{:S(2)}) collective-permute-start(bf16[96,384]{1,0:T(8,128)(2,1)S(1)} %get-tuple-element.88), channel_id=1, source_target_pairs={{0,4},{2,6},{4,0},{6,2},{1,5},{3,7},{5,1},{7,3},{8,12},{10,14},{12... | collective-permute-start | bytes 221192 | tf_op jit(solution)/shard_map/ppermute | solution.py:310
  56.6 0.4 collective-permute-start.20
  57.0 4.4 %collective-permute-done.17 = bf16[2,384,128]{2,1,0:T(8,128)(2,1)S(1)} collective-permute-done((bf16[2,384,128]{2,1,0:T(8,128)(2,1)S(1)}, bf16[2,384,128]{2,1,0:T(8,128)(2,1)S(1)}, u32[]{:S(2)}, u32[]{:S(2)}) %collective-permute-start.17) | collective-permute-done | bytes 196640 | tf_op jit(solution)/shard_map/ppermute | solution.py:310
  61.4 1.5 %collective-permute-done.22.refs_3_ = bf16[96,384]{1,0:T(8,128)(2,1)S(1)} collective-permute-done((bf16[96,384]{1,0:T(8,128)(2,1)S(1)}, bf16[96,384]{1,0:T(8,128)(2,1)S(1)}, u32[]{:S(2)}, u32[]{:S(2)}) %collective-permute-start.22) | collective-permute-done | bytes 73760 | tf_op jit(solution)/shard_map/ppermute | solution.py:310
  63.0 0.9 %collective-permute-done.20.refs_1_ = bf16[96,384]{1,0:T(8,128)(2,1)S(1)} collective-permute-done((bf16[96,384]{1,0:T(8,128)(2,1)S(1)}, bf16[96,384]{1,0:T(8,128)(2,1)S(1)}, u32[]{:S(2)}, u32[]{:S(2)}) %collective-permute-start.20) | collective-permute-done | bytes 73760 | tf_op jit(solution)/shard_map/ppermute | solution.py:310
  64.0 0.9 %bias_grad.1 = f32[4,96,384]{2,1,0:T(8,128)} custom-call(bf16[96,384]{1,0:T(8,128)(2,1)S(1)} %get-tuple-element.90.refs_0_, bf16[96,384]{1,0:T(8,128)(2,1)S(1)} %collective-permute-done.20.refs_1_, bf16[96,384]{1,0:T(8,128)(2,1)S(1)} %collective-permute-done.21.refs_2_, bf16[96,384]{1,0:T(8,128)(2,1)S(1)} %collective-permute-done.22.refs_3_), custom_call_target="tpu_custom_call" | custom-call | tf_op jit(solution)/shard_map/bias_grad/pallas_call | solution.py:290
  65.0 0.8 %collective-permute-done.23.swapped = bf16[4,384,128]{2,1,0:T(8,128)(2,1)S(1)} collective-permute-done((bf16[4,384,128]{2,1,0:T(8,128)(2,1)S(1)}, bf16[4,384,128]{2,1,0:T(8,128)(2,1)S(1)}, u32[]{:S(2)}, u32[]{:S(2)}) %collective-permute-start.23) | collective-permute-done | bytes 393248 | tf_op jit(solution)/shard_map/ppermute | solution.py:310
  65.8 1.5 %unpack.1 = (bf16[2,384,128]{2,1,0:T(8,128)(2,1)}, bf16[2,384,128]{2,1,0:T(8,128)(2,1)}, bf16[2,384,128]{2,1,0:T(8,128)(2,1)}, bf16[2,384,128]{2,1,0:T(8,128)(2,1)}) custom-call(bf16[2,384,128]{2,1,0:T(8,128)(2,1)S(1)} %copy-done, bf16[2,384,128]{2,1,0:T(8,128)(2,1)S(1)} %copy-done.1, bf16[4,384,128]{2,1,0:T(8,128)(2,1)S(1)} %pad_maximum_fusion.packs, ...), custom_call_target="tpu_custom_call" | custom-call | tf_op jit(solution)/shard_map/unpack/pallas_call | solution.py:274
  (52 shorter events, 2.8 us)
Async XLA Ops:
  0.6 1.0 %copy-start.3 = (bf16[4,96,384]{2,1,0:T(8,128)(2,1)S(1)}, bf16[4,96,384]{2,1,0:T(8,128)(2,1)}, u32[]{:S(2)}) copy-start(bf16[4,96,384]{2,1,0:T(8,128)(2,1)} %bias.1) | copy-start | bytes 884740
  1.6 11.1 %copy-start.4 = (s32[384]{0:T(512)S(1)}, s32[384]{0:T(512)}, u32[]{:S(2)}) copy-start(s32[384]{0:T(512)} %param.12) | copy-start | bytes 4612
  1.6 11.1 %collective-permute-start.3 = (bf16[96,384]{1,0:T(8,128)(2,1)S(1)}, bf16[96,384]{1,0:T(8,128)(2,1)S(1)}, u32[]{:S(2)}, u32[]{:S(2)}) collective-permute-start(bf16[96,384]{1,0:T(8,128)(2,1)S(1)} %get-tuple-element.51), channel_id=1, source_target_pairs={{0,2},{2,0},{4,6},{6,4},{1,3},{3,1},{5,7},{7,5},{8,10},{10,8},{12,... | collective-permute-start | bytes 221192 | tf_op jit(solution)/shard_map/ppermute | solution.py:310
  4.6 8.1 %collective-permute-start.4 = (bf16[96,384]{1,0:T(8,128)(2,1)S(1)}, bf16[96,384]{1,0:T(8,128)(2,1)S(1)}, u32[]{:S(2)}, u32[]{:S(2)}) collective-permute-start(bf16[96,384]{1,0:T(8,128)(2,1)S(1)} %get-tuple-element.52), channel_id=1, source_target_pairs={{0,4},{2,6},{4,0},{6,2},{1,5},{3,7},{5,1},{7,3},{8,12},{10,14},{12... | collective-permute-start | bytes 221192 | tf_op jit(solution)/shard_map/ppermute | solution.py:310
  6.2 6.6 %collective-permute-start.5 = (bf16[96,384]{1,0:T(8,128)(2,1)S(1)}, bf16[96,384]{1,0:T(8,128)(2,1)S(1)}, u32[]{:S(2)}, u32[]{:S(2)}) collective-permute-start(bf16[96,384]{1,0:T(8,128)(2,1)S(1)} %get-tuple-element.53), channel_id=1, source_target_pairs={{0,6},{2,4},{4,2},{6,0},{1,7},{3,5},{5,3},{7,1},{8,14},{10,12},{12... | collective-permute-start | bytes 221192 | tf_op jit(solution)/shard_map/ppermute | solution.py:310
  9.1 8.5 %copy-start.5 = (bf16[384,128]{1,0:T(8,128)(2,1)S(1)}, bf16[384,128]{1,0:T(8,128)(2,1)}, u32[]{:S(2)}) copy-start(bf16[384,128]{1,0:T(8,128)(2,1)} %get-tuple-element.49) | copy-start | bytes 294916
  9.1 10.2 %copy-start.2 = (bf16[384,128]{1,0:T(8,128)(2,1)S(1)}, bf16[384,128]{1,0:T(8,128)(2,1)}, u32[]{:S(2)}) copy-start(bf16[384,128]{1,0:T(8,128)(2,1)} %get-tuple-element.46.refs_0_) | copy-start | bytes 294916
  9.1 7.1 %collective-permute-start = (bf16[2,384,128]{2,1,0:T(8,128)(2,1)}, bf16[2,384,128]{2,1,0:T(8,128)(2,1)S(1)}, u32[]{:S(2)}, u32[]{:S(2)}) collective-permute-start(bf16[2,384,128]{2,1,0:T(8,128)(2,1)} %get-tuple-element.47), channel_id=1, source_target_pairs={{0,2},{2,0},{4,6},{6,4},{1,3},{3,1},{5,7},{7,5},{8,10},{10,8},{12,... | collective-permute-start | bytes 589832 | tf_op jit(solution)/shard_map/ppermute | solution.py:310
  11.1 14.2 %collective-permute-start.11 = (bf16[2,384,128]{2,1,0:T(8,128)(2,1)}, bf16[2,384,128]{2,1,0:T(8,128)(2,1)S(1)}, u32[]{:S(2)}, u32[]{:S(2)}) collective-permute-start(bf16[2,384,128]{2,1,0:T(8,128)(2,1)} %get-tuple-element.62), channel_id=1, source_target_pairs={{0,4},{2,6},{4,0},{6,2},{1,5},{3,7},{5,1},{7,3},{8,12},{10,14},{12... | collective-permute-start | bytes 589832 | tf_op jit(solution)/shard_map/ppermute | solution.py:310
  12.7 14.5 %collective-permute-start.12 = (bf16[2,384,128]{2,1,0:T(8,128)(2,1)}, bf16[2,384,128]{2,1,0:T(8,128)(2,1)S(1)}, u32[]{:S(2)}, u32[]{:S(2)}) collective-permute-start(bf16[2,384,128]{2,1,0:T(8,128)(2,1)} %get-tuple-element.63), channel_id=1, source_target_pairs={{0,6},{2,4},{4,2},{6,0},{1,7},{3,5},{5,3},{7,1},{8,14},{10,12},{12... | collective-permute-start | bytes 589832 | tf_op jit(solution)/shard_map/ppermute | solution.py:310
  12.9 14.4 %collective-permute-start.6 = (bf16[4,96,384]{2,1,0:T(8,128)(2,1)S(1)}, bf16[4,96,384]{2,1,0:T(8,128)(2,1)S(1)}, u32[]{:S(2)}, u32[]{:S(2)}) collective-permute-start(bf16[4,96,384]{2,1,0:T(8,128)(2,1)S(1)} %maximum_select_fusion.refs_4_), channel_id=1, source_target_pairs={{0,8},{8,0},{1,9},{9,1},{2,10},{10,2},{3,11},{11,3},{4,12},{12,4},... | collective-permute-start | bytes 884744 | tf_op jit(solution)/shard_map/ppermute | solution.py:310
  15.9 2.0 %collective-permute-start.8 = (bf16[2,96,384]{2,1,0:T(8,128)(2,1)S(1)}, bf16[2,96,384]{2,1,0:T(8,128)(2,1)S(1)}, u32[]{:S(2)}, u32[]{:S(2)}) collective-permute-start(bf16[2,96,384]{2,1,0:T(8,128)(2,1)S(1)} %get-tuple-element.91), channel_id=1, source_target_pairs={{0,1},{1,0},{2,3},{3,2},{4,5},{5,4},{6,7},{7,6},{8,9},{9,8},{10,11... | collective-permute-start | bytes 442376 | tf_op jit(solution)/shard_map/ppermute | solution.py:310
  16.2 1.4 %collective-permute-start.7 = (bf16[2,96,384]{2,1,0:T(8,128)(2,1)S(1)}, bf16[2,96,384]{2,1,0:T(8,128)(2,1)S(1)}, u32[]{:S(2)}, u32[]{:S(2)}) collective-permute-start(bf16[2,96,384]{2,1,0:T(8,128)(2,1)S(1)} %get-tuple-element.92), channel_id=1, source_target_pairs={{0,1},{1,0},{2,3},{3,2},{4,5},{5,4},{6,7},{7,6},{8,9},{9,8},{10,11... | collective-permute-start | bytes 442376 | tf_op jit(solution)/shard_map/ppermute | solution.py:310
  17.6 1.3 %collective-permute-start.1 = (bf16[384,128]{1,0:T(8,128)(2,1)S(1)}, bf16[384,128]{1,0:T(8,128)(2,1)S(1)}, u32[]{:S(2)}, u32[]{:S(2)}) collective-permute-start(bf16[384,128]{1,0:T(8,128)(2,1)S(1)} %copy-done.5), channel_id=1, source_target_pairs={{0,1},{1,0},{2,3},{3,2},{4,5},{5,4},{6,7},{7,6},{8,9},{9,8},{10,11... | collective-permute-start | bytes 294920 | tf_op jit(solution)/shard_map/ppermute | solution.py:310
  17.9 1.4 %collective-permute-start.2 = (bf16[384,128]{1,0:T(8,128)(2,1)S(1)}, bf16[384,128]{1,0:T(8,128)(2,1)S(1)}, u32[]{:S(2)}, u32[]{:S(2)}) collective-permute-start(bf16[384,128]{1,0:T(8,128)(2,1)S(1)} %get-tuple-element.103), channel_id=1, source_target_pairs={{0,1},{1,0},{2,3},{3,2},{4,5},{5,4},{6,7},{7,6},{8,9},{9,8},{10,11... | collective-permute-start | bytes 294920 | tf_op jit(solution)/shard_map/ppermute | solution.py:310
  27.2 4.8 %collective-permute-start.13 = (bf16[384,128]{1,0:T(8,128)(2,1)S(1)}, bf16[384,128]{1,0:T(8,128)(2,1)S(1)}, u32[]{:S(2)}, u32[]{:S(2)}) collective-permute-start(bf16[384,128]{1,0:T(8,128)(2,1)S(1)} %get-tuple-element.101), channel_id=1, source_target_pairs={{0,1},{1,0},{2,3},{3,2},{4,5},{5,4},{6,7},{7,6},{8,9},{9,8},{10,11... | collective-permute-start | bytes 294920 | tf_op jit(solution)/shard_map/ppermute | solution.py:310
  27.3 1.7 %collective-permute-start.9 = (bf16[4,96,384]{2,1,0:T(8,128)(2,1)S(1)}, bf16[4,96,384]{2,1,0:T(8,128)(2,1)S(1)}, u32[]{:S(2)}, u32[]{:S(2)}) collective-permute-start(bf16[4,96,384]{2,1,0:T(8,128)(2,1)S(1)} %collective-permute-done.6.refs_4_), channel_id=1, source_target_pairs={{0,1},{1,0},{2,3},{3,2},{4,5},{5,4},{6,7},{7,6},{8,9},{9,8},{10,11... | collective-permute-start | bytes 884744 | tf_op jit(solution)/shard_map/ppermute | solution.py:310
  27.8 4.2 %collective-permute-start.14 = (bf16[384,128]{1,0:T(8,128)(2,1)S(1)}, bf16[384,128]{1,0:T(8,128)(2,1)S(1)}, u32[]{:S(2)}, u32[]{:S(2)}) collective-permute-start(bf16[384,128]{1,0:T(8,128)(2,1)S(1)} %get-tuple-element.99), channel_id=1, source_target_pairs={{0,1},{1,0},{2,3},{3,2},{4,5},{5,4},{6,7},{7,6},{8,9},{9,8},{10,11... | collective-permute-start | bytes 294920 | tf_op jit(solution)/shard_map/ppermute | solution.py:310
  34.9 1.6 %collective-permute-start.15 = (bf16[4,96,384]{2,1,0:T(8,128)(2,1)S(1)}, bf16[4,96,384]{2,1,0:T(8,128)(2,1)S(1)}, u32[]{:S(2)}, u32[]{:S(2)}) collective-permute-start(bf16[4,96,384]{2,1,0:T(8,128)(2,1)S(1)} %get-tuple-element.68), channel_id=1, source_target_pairs={{0,1},{1,0},{2,3},{3,2},{4,5},{5,4},{6,7},{7,6},{8,9},{9,8},{10,11... | collective-permute-start | bytes 884744 | tf_op jit(solution)/shard_map/ppermute | solution.py:310
  36.6 16.7 %collective-permute-start.18 = (bf16[4,96,384]{2,1,0:T(8,128)(2,1)S(1)}, bf16[4,96,384]{2,1,0:T(8,128)(2,1)S(1)}, u32[]{:S(2)}, u32[]{:S(2)}) collective-permute-start(bf16[4,96,384]{2,1,0:T(8,128)(2,1)S(1)} %add_convert_fusion.1), channel_id=1, source_target_pairs={{0,8},{8,0},{1,9},{9,1},{2,10},{10,2},{3,11},{11,3},{4,12},{12,4},... | collective-permute-start | bytes 884744 | tf_op jit(solution)/shard_map/ppermute | solution.py:310
  42.3 11.0 %collective-permute-start.19 = (bf16[4,96,384]{2,1,0:T(8,128)(2,1)S(1)}, bf16[4,96,384]{2,1,0:T(8,128)(2,1)S(1)}, u32[]{:S(2)}, u32[]{:S(2)}) collective-permute-start(bf16[4,96,384]{2,1,0:T(8,128)(2,1)S(1)} %get-tuple-element.78), channel_id=1, source_target_pairs={{0,1},{1,0},{2,3},{3,2},{4,5},{5,4},{6,7},{7,6},{8,9},{9,8},{10,11... | collective-permute-start | bytes 884744 | tf_op jit(solution)/shard_map/ppermute | solution.py:310
  42.4 14.2 %collective-permute-start.10 = (bf16[2,384,128]{2,1,0:T(8,128)(2,1)S(1)}, bf16[2,384,128]{2,1,0:T(8,128)(2,1)S(1)}, u32[]{:S(2)}, u32[]{:S(2)}) collective-permute-start(bf16[2,384,128]{2,1,0:T(8,128)(2,1)S(1)} %get-tuple-element.61), channel_id=1, source_target_pairs={{0,2},{2,0},{4,6},{6,4},{1,3},{3,1},{5,7},{7,5},{8,10},{10,8},{12,... | collective-permute-start | bytes 589832 | tf_op jit(solution)/shard_map/ppermute | solution.py:310
  43.0 14.0 %collective-permute-start.16 = (bf16[2,384,128]{2,1,0:T(8,128)(2,1)S(1)}, bf16[2,384,128]{2,1,0:T(8,128)(2,1)S(1)}, u32[]{:S(2)}, u32[]{:S(2)}) collective-permute-start(bf16[2,384,128]{2,1,0:T(8,128)(2,1)S(1)} %get-tuple-element.74), channel_id=1, source_target_pairs={{0,4},{2,6},{4,0},{6,2},{1,5},{3,7},{5,1},{7,3},{8,12},{10,14},{12... | collective-permute-start | bytes 589832 | tf_op jit(solution)/shard_map/ppermute | solution.py:310
  45.8 15.5 %collective-permute-start.17 = (bf16[2,384,128]{2,1,0:T(8,128)(2,1)S(1)}, bf16[2,384,128]{2,1,0:T(8,128)(2,1)S(1)}, u32[]{:S(2)}, u32[]{:S(2)}) collective-permute-start(bf16[2,384,128]{2,1,0:T(8,128)(2,1)S(1)} %get-tuple-element.75), channel_id=1, source_target_pairs={{0,6},{2,4},{4,2},{6,0},{1,7},{3,5},{5,3},{7,1},{8,14},{10,12},{12... | collective-permute-start | bytes 589832 | tf_op jit(solution)/shard_map/ppermute | solution.py:310
  53.4 9.5 %collective-permute-start.22 = (bf16[96,384]{1,0:T(8,128)(2,1)S(1)}, bf16[96,384]{1,0:T(8,128)(2,1)S(1)}, u32[]{:S(2)}, u32[]{:S(2)}) collective-permute-start(bf16[96,384]{1,0:T(8,128)(2,1)S(1)} %get-tuple-element.87), channel_id=1, source_target_pairs={{0,6},{2,4},{4,2},{6,0},{1,7},{3,5},{5,3},{7,1},{8,14},{10,12},{12... | collective-permute-start | bytes 221192 | tf_op jit(solution)/shard_map/ppermute | solution.py:310
  53.8 9.2 %collective-permute-start.21 = (bf16[96,384]{1,0:T(8,128)(2,1)S(1)}, bf16[96,384]{1,0:T(8,128)(2,1)S(1)}, u32[]{:S(2)}, u32[]{:S(2)}) collective-permute-start(bf16[96,384]{1,0:T(8,128)(2,1)S(1)} %get-tuple-element.88), channel_id=1, source_target_pairs={{0,4},{2,6},{4,0},{6,2},{1,5},{3,7},{5,1},{7,3},{8,12},{10,14},{12... | collective-permute-start | bytes 221192 | tf_op jit(solution)/shard_map/ppermute | solution.py:310
  56.6 7.2 %collective-permute-start.20 = (bf16[96,384]{1,0:T(8,128)(2,1)S(1)}, bf16[96,384]{1,0:T(8,128)(2,1)S(1)}, u32[]{:S(2)}, u32[]{:S(2)}) collective-permute-start(bf16[96,384]{1,0:T(8,128)(2,1)S(1)} %get-tuple-element.89), channel_id=1, source_target_pairs={{0,2},{2,0},{4,6},{6,4},{1,3},{3,1},{5,7},{7,5},{8,10},{10,8},{12,... | collective-permute-start | bytes 221192 | tf_op jit(solution)/shard_map/ppermute | solution.py:310
  63.9 1.9 %copy-start = (bf16[2,384,128]{2,1,0:T(8,128)(2,1)S(1)}, bf16[2,384,128]{2,1,0:T(8,128)(2,1)}, u32[]{:S(2)}) copy-start(bf16[2,384,128]{2,1,0:T(8,128)(2,1)} %gate.1) | copy-start | bytes 589828
  63.9 1.9 %copy-start.1 = (bf16[2,384,128]{2,1,0:T(8,128)(2,1)S(1)}, bf16[2,384,128]{2,1,0:T(8,128)(2,1)}, u32[]{:S(2)}) copy-start(bf16[2,384,128]{2,1,0:T(8,128)(2,1)} %cot.1) | copy-start | bytes 589828
  64.0 1.8 %collective-permute-start.23 = (bf16[4,384,128]{2,1,0:T(8,128)(2,1)S(1)}, bf16[4,384,128]{2,1,0:T(8,128)(2,1)S(1)}, u32[]{:S(2)}, u32[]{:S(2)}) collective-permute-start(bf16[4,384,128]{2,1,0:T(8,128)(2,1)S(1)} %pad_maximum_fusion.1), channel_id=1, source_target_pairs={{0,1},{1,0},{2,3},{3,2},{4,5},{5,4},{6,7},{7,6},{8,9},{9,8},{10,11... | collective-permute-start | bytes 1179656 | tf_op jit(solution)/shard_map/ppermute | solution.py:310

commit v4 on v2

--- a/solution.py
+++ b/solution.py
@@ -10,6 +10,7 @@
 
 PAIR = 2
 NEAR_PARTS = 2
+SENT = (2, 3, 1)
 ROWS_AT_ONCE = 16
 VMEM = pltpu.VMEM
 PARAMS = pltpu.CompilerParams(vmem_limit_bytes=32 * 1024 * 1024)
@@ -257,9 +258,9 @@
     rows, half, channels = gate.shape
     size = channels // 4
     _, near, core = places()
-    for s in range(4):
-        held[near ^ s, core] = packs[s]
-        held[near ^ s, 1 - core] = swapped[s]
+    for i, s in enumerate((0, *SENT)):
+        held[near ^ s, core] = packs[i]
+        held[near ^ s, 1 - core] = swapped[i]
     for r in range(rows):
         full = []
         for j in range(4):
@@ -365,7 +366,7 @@
             sums[g] = (d_mine + wide(other_core(d_other))).astype(jnp.bfloat16)
         if a == 0:
             stay, pass_on, *earlier = earlier
-        returned += [near_swap(value, len(returned) + i + 1) for i, value in enumerate(earlier)]
+        returned += earlier
     d_sum = sums[0]
     if not relative:
         d_sum = d_sum.reshape(chips, own, half)[chip ^ jnp.arange(chips)]
@@ -374,6 +375,8 @@
             total = total + wide(far_swap(d_sum[4 * f : 4 * f + 4], f))
         d_sum = total.astype(jnp.bfloat16)
     pieces = [near_swap(d_sum[s], s) for s in range(4)]
+    returned = lax.optimization_barrier(tuple(returned))
+    returned = [near_swap(returned[s - 1], s) for s in SENT]
     returned = lax.optimization_barrier((*returned, *pieces))[:3]
     swapped = other_core(jnp.stack([pass_on] + [pack[1] for pack in returned]))
     packs = jnp.stack([stay] + [pack[0] for pack in returned])

time: 67.1 us -> 66.8 us (level)
  transfers between devices with their start and end apart: 24 -> 24, of which waited for: 14 -> 13; matrix products, arithmetic and copies ran while one was open for 1% -> 1% of each run, Pallas kernels for 18% -> 19%
where the time goes in v4:
time: 66.8 us; the launch traced here: 66.6 us
  waiting for transfers between devices  24.4 us (37%)
  starting transfers between devices  23.2 us (35%)
  Pallas kernels  16.6 us (25%)
  local copies, waits for them, and re-layouts  1.17 us (2%)
  between operations  0.9 us (1%)
    ppermute x24, waiting for transfers between devices, swap(): lax.ppermute(value, axes, [(i, i ^ s) for i in range(count)])  24.4 us
    ppermute x24, starting transfers between devices, swap(): lax.ppermute(value, axes, [(i, i ^ s) for i in range(count)])  23.2 us
    pallas_call x4, Pallas kernels, main(): pl.pallas_call(functools.partial(main_kernel, scaling, size, blocks, star...  11.4 us
    pallas_call x1, Pallas kernels, make_packs(): pl.pallas_call(pack_kernel, in_specs=[pl.BlockSpec(memory_space=pl.ANY)]...  2.87 us
    pallas_call x1, Pallas kernels, post(): pl.pallas_call(post_kernel, out_shape=[jax.ShapeDtypeStruct(gate.shape, j...  1.45 us
  transfers between devices with their start and end apart: 24, of which 13 were waited for; matrix products, arithmetic and copies ran while one was open for 1% of the time, Pallas kernels for 19%

profile of v4, /device:TPU:0, one launch (start us, length us, event | category | flops | bytes accessed | tf_op | source)
XLA Modules:
  0.0 66.6 jit_solution(2612465123088465507)
XLA Ops:
  0.6 1.0 %copy-done.3 = bf16[4,96,384]{2,1,0:T(8,128)(2,1)S(1)} copy-done((bf16[4,96,384]{2,1,0:T(8,128)(2,1)S(1)}, bf16[4,96,384]{2,1,0:T(8,128)(2,1)}, u32[]{:S(2)}) %copy-start.3) | copy-done | bytes 294936
  1.6 3.0 %collective-permute-start.3 = (bf16[96,384]{1,0:T(8,128)(2,1)S(1)}, bf16[96,384]{1,0:T(8,128)(2,1)S(1)}, u32[]{:S(2)}, u32[]{:S(2)}) collective-permute-start(bf16[96,384]{1,0:T(8,128)(2,1)S(1)} %get-tuple-element.54), channel_id=1, source_target_pairs={{0,2},{2,0},{4,6},{6,4},{1,3},{3,1},{5,7},{7,5},{8,10},{10,8},{12,... | collective-permute-start | bytes 221192 | tf_op jit(solution)/shard_map/ppermute | solution.py:310
  4.6 1.6 %collective-permute-start.4 = (bf16[96,384]{1,0:T(8,128)(2,1)S(1)}, bf16[96,384]{1,0:T(8,128)(2,1)S(1)}, u32[]{:S(2)}, u32[]{:S(2)}) collective-permute-start(bf16[96,384]{1,0:T(8,128)(2,1)S(1)} %get-tuple-element.55), channel_id=1, source_target_pairs={{0,4},{2,6},{4,0},{6,2},{1,5},{3,7},{5,1},{7,3},{8,12},{10,14},{12... | collective-permute-start | bytes 221192 | tf_op jit(solution)/shard_map/ppermute | solution.py:310
  6.2 2.9 %pack.1 = (bf16[2,384,128]{2,1,0:T(8,128)(2,1)}, bf16[2,384,128]{2,1,0:T(8,128)(2,1)}, bf16[2,384,128]{2,1,0:T(8,128)(2,1)}, bf16[384,128]{1,0:T(8,128)(2,1)}, bf16[384,128]{1,0:T(8,128)(2,1)}) custom-call(bf16[2,384,128]{2,1,0:T(8,128)(2,1)} %refs_0_.1, bf16[2,384,128]{2,1,0:T(8,128)(2,1)} %refs_1_.1, bf16[2,384,128]{2,1,0:T(8,128)(2,1)} %refs_2_.1, ...), custom_call_target="tpu_custom_call" | custom-call | tf_op jit(solution)/shard_map/pack/pallas_call | solution.py:68
  9.1 2.0 %collective-permute-start = (bf16[2,384,128]{2,1,0:T(8,128)(2,1)}, bf16[2,384,128]{2,1,0:T(8,128)(2,1)S(1)}, u32[]{:S(2)}, u32[]{:S(2)}) collective-permute-start(bf16[2,384,128]{2,1,0:T(8,128)(2,1)} %get-tuple-element.50), channel_id=1, source_target_pairs={{0,2},{2,0},{4,6},{6,4},{1,3},{3,1},{5,7},{7,5},{8,10},{10,8},{12,... | collective-permute-start | bytes 589832 | tf_op jit(solution)/shard_map/ppermute | solution.py:310
  11.1 1.6 %collective-permute-start.10 = (bf16[2,384,128]{2,1,0:T(8,128)(2,1)}, bf16[2,384,128]{2,1,0:T(8,128)(2,1)S(1)}, u32[]{:S(2)}, u32[]{:S(2)}) collective-permute-start(bf16[2,384,128]{2,1,0:T(8,128)(2,1)} %get-tuple-element.65), channel_id=1, source_target_pairs={{0,4},{2,6},{4,0},{6,2},{1,5},{3,7},{5,1},{7,3},{8,12},{10,14},{12... | collective-permute-start | bytes 589832 | tf_op jit(solution)/shard_map/ppermute | solution.py:310
  12.9 3.0 %collective-permute-start.6 = (bf16[4,96,384]{2,1,0:T(8,128)(2,1)S(1)}, bf16[4,96,384]{2,1,0:T(8,128)(2,1)S(1)}, u32[]{:S(2)}, u32[]{:S(2)}) collective-permute-start(bf16[4,96,384]{2,1,0:T(8,128)(2,1)S(1)} %maximum_select_fusion.refs_4_), channel_id=1, source_target_pairs={{0,8},{8,0},{1,9},{9,1},{2,10},{10,2},{3,11},{11,3},{4,12},{12,4},... | collective-permute-start | bytes 884744 | tf_op jit(solution)/shard_map/ppermute | solution.py:310
  16.5 1.1 %collective-permute-done.7 = bf16[2,96,384]{2,1,0:T(8,128)(2,1)S(1)} collective-permute-done((bf16[2,96,384]{2,1,0:T(8,128)(2,1)S(1)}, bf16[2,96,384]{2,1,0:T(8,128)(2,1)S(1)}, u32[]{:S(2)}, u32[]{:S(2)}) %collective-permute-start.7) | collective-permute-done | bytes 147488 | tf_op jit(solution)/shard_map/ppermute | solution.py:310
  18.2 0.7 %collective-permute-done.1.refs_2_ = bf16[384,128]{1,0:T(8,128)(2,1)S(1)} collective-permute-done((bf16[384,128]{1,0:T(8,128)(2,1)S(1)}, bf16[384,128]{1,0:T(8,128)(2,1)S(1)}, u32[]{:S(2)}, u32[]{:S(2)}) %collective-permute-start.1) | collective-permute-done | bytes 98336 | tf_op jit(solution)/shard_map/ppermute | solution.py:310
  19.3 2.7 %attention.4 = (f32[384,768]{1,0:T(8,128)S(1)}, bf16[768,64]{1,0:T(8,128)(2,1)S(1)}, bf16[768,64]{1,0:T(8,128)(2,1)S(1)}, f32[64,768]{1,0:T(8,128)S(1)}, f32[64,768]{1,0:T(8,128)S(1)}) custom-call(bf16[384,128]{1,0:T(8,128)(2,1)S(1)} %copy-done.2, bf16[384,128]{1,0:T(8,128)(2,1)S(1)} %get-tuple-element.110.refs_1_, ...), custom_call_target="tpu_custom_call" | custom-call | flops 1 | bytes 1 | tf_op jit(solution)/shard_map/attention/pallas_call | solution.py:227
  22.0 3.2 %collective-permute-done.10 = bf16[2,384,128]{2,1,0:T(8,128)(2,1)S(1)} collective-permute-done((bf16[2,384,128]{2,1,0:T(8,128)(2,1)}, bf16[2,384,128]{2,1,0:T(8,128)(2,1)S(1)}, u32[]{:S(2)}, u32[]{:S(2)}) %collective-permute-start.10) | collective-permute-done | bytes 196640 | tf_op jit(solution)/shard_map/ppermute | solution.py:310
  25.2 1.9 %collective-permute-done.11 = bf16[2,384,128]{2,1,0:T(8,128)(2,1)S(1)} collective-permute-done((bf16[2,384,128]{2,1,0:T(8,128)(2,1)}, bf16[2,384,128]{2,1,0:T(8,128)(2,1)S(1)}, u32[]{:S(2)}, u32[]{:S(2)}) %collective-permute-start.11) | collective-permute-done | bytes 196640 | tf_op jit(solution)/shard_map/ppermute | solution.py:310
  27.3 0.5 collective-permute-start.9
  28.0 1.0 %collective-permute-done.9.refs_5_ = bf16[4,96,384]{2,1,0:T(8,128)(2,1)S(1)} collective-permute-done((bf16[4,96,384]{2,1,0:T(8,128)(2,1)S(1)}, bf16[4,96,384]{2,1,0:T(8,128)(2,1)S(1)}, u32[]{:S(2)}, u32[]{:S(2)}) %collective-permute-start.9) | collective-permute-done | bytes 294944 | tf_op jit(solution)/shard_map/ppermute | solution.py:310
  29.0 2.8 %attention.5 = (f32[384,768]{1,0:T(8,128)S(1)}, bf16[384,128]{1,0:T(8,128)(2,1)S(1)}, bf16[384,128]{1,0:T(8,128)(2,1)S(1)}, bf16[2,384,128]{2,1,0:T(8,128)(2,1)S(1)}) custom-call(bf16[384,128]{1,0:T(8,128)(2,1)S(1)} %copy-done.2, bf16[384,128]{1,0:T(8,128)(2,1)S(1)} %get-tuple-element.110.refs_1_, bf16[384,128]{1,0:T(8,128)(2,1)S(1)} %collective-permute-done.1.refs_2_, ...), custom_call_target="tpu_custom_call" | custom-call | flops 1 | bytes 1 | tf_op jit(solution)/shard_map/attention/pallas_call | solution.py:227
  31.9 2.8 %attention.6 = (bf16[4,96,384]{2,1,0:T(8,128)(2,1)S(1)}, bf16[4,96,384]{2,1,0:T(8,128)(2,1)S(1)}, bf16[768,64]{1,0:T(8,128)(2,1)S(1)}, bf16[768,64]{1,0:T(8,128)...) custom-call(bf16[384,128]{1,0:T(8,128)(2,1)S(1)} %get-tuple-element.108.refs_0_, ...), custom_call_target="tpu_custom_call" | custom-call | flops 1 | bytes 1 | tf_op jit(solution)/shard_map/attention/pallas_call | solution.py:227
  34.6 0.4 collective-permute-start.14
  35.1 1.2 %collective-permute-done.14 = bf16[4,96,384]{2,1,0:T(8,128)(2,1)S(1)} collective-permute-done((bf16[4,96,384]{2,1,0:T(8,128)(2,1)S(1)}, bf16[4,96,384]{2,1,0:T(8,128)(2,1)S(1)}, u32[]{:S(2)}, u32[]{:S(2)}) %collective-permute-start.14) | collective-permute-done | bytes 294944 | tf_op jit(solution)/shard_map/ppermute | solution.py:310
  36.4 2.6 %collective-permute-start.18 = (bf16[4,96,384]{2,1,0:T(8,128)(2,1)S(1)}, bf16[4,96,384]{2,1,0:T(8,128)(2,1)S(1)}, u32[]{:S(2)}, u32[]{:S(2)}) collective-permute-start(bf16[4,96,384]{2,1,0:T(8,128)(2,1)S(1)} %add_convert_fusion.1), channel_id=1, source_target_pairs={{0,8},{8,0},{1,9},{9,1},{2,10},{10,2},{3,11},{11,3},{4,12},{12,4},... | collective-permute-start | bytes 884744 | tf_op jit(solution)/shard_map/ppermute | solution.py:310
  38.9 3.1 %attention.7 = (bf16[4,96,384]{2,1,0:T(8,128)(2,1)S(1)}, bf16[4,96,384]{2,1,0:T(8,128)(2,1)S(1)}, bf16[2,384,128]{2,1,0:T(8,128)(2,1)S(1)}, bf16[2,384,128]{2,1,0:T(8,128)(2,1)S(1)}) custom-call(bf16[384,128]{1,0:T(8,128)(2,1)S(1)} %get-tuple-element.108.refs_0_, bf16[384,128]{1,0:T(8,128)(2,1)S(1)} %get-tuple-element.106.refs_1_, ...), custom_call_target="tpu_custom_call" | custom-call | flops 1 | bytes 1 | tf_op jit(solution)/shard_map/attention/pallas_call | solution.py:227
  42.1 1.9 %collective-permute-start.15 = (bf16[2,384,128]{2,1,0:T(8,128)(2,1)S(1)}, bf16[2,384,128]{2,1,0:T(8,128)(2,1)S(1)}, u32[]{:S(2)}, u32[]{:S(2)}) collective-permute-start(bf16[2,384,128]{2,1,0:T(8,128)(2,1)S(1)} %get-tuple-element.79), channel_id=1, source_target_pairs={{0,4},{2,6},{4,0},{6,2},{1,5},{3,7},{5,1},{7,3},{8,12},{10,14},{12... | collective-permute-start | bytes 589832 | tf_op jit(solution)/shard_map/ppermute | solution.py:310
  44.0 1.0 %collective-permute-start.16 = (bf16[2,384,128]{2,1,0:T(8,128)(2,1)S(1)}, bf16[2,384,128]{2,1,0:T(8,128)(2,1)S(1)}, u32[]{:S(2)}, u32[]{:S(2)}) collective-permute-start(bf16[2,384,128]{2,1,0:T(8,128)(2,1)S(1)} %get-tuple-element.80), channel_id=1, source_target_pairs={{0,6},{2,4},{4,2},{6,0},{1,7},{3,5},{5,3},{7,1},{8,14},{10,12},{12... | collective-permute-start | bytes 589832 | tf_op jit(solution)/shard_map/ppermute | solution.py:310
  45.0 0.6 collective-permute-start.17
  45.7 7.4 %collective-permute-done.18 = bf16[4,96,384]{2,1,0:T(8,128)(2,1)S(1)} collective-permute-done((bf16[4,96,384]{2,1,0:T(8,128)(2,1)S(1)}, bf16[4,96,384]{2,1,0:T(8,128)(2,1)S(1)}, u32[]{:S(2)}, u32[]{:S(2)}) %collective-permute-start.18) | collective-permute-done | bytes 294944 | tf_op jit(solution)/shard_map/ppermute | solution.py:310
  53.6 2.8 %collective-permute-start.21 = (bf16[96,384]{1,0:T(8,128)(2,1)S(1)}, bf16[96,384]{1,0:T(8,128)(2,1)S(1)}, u32[]{:S(2)}, u32[]{:S(2)}) collective-permute-start(bf16[96,384]{1,0:T(8,128)(2,1)S(1)} %get-tuple-element.94), channel_id=1, source_target_pairs={{0,4},{2,6},{4,0},{6,2},{1,5},{3,7},{5,1},{7,3},{8,12},{10,14},{12... | collective-permute-start | bytes 221192 | tf_op jit(solution)/shard_map/ppermute | solution.py:310
  56.4 0.4 collective-permute-start.20
  56.8 3.7 %collective-permute-done.16 = bf16[2,384,128]{2,1,0:T(8,128)(2,1)S(1)} collective-permute-done((bf16[2,384,128]{2,1,0:T(8,128)(2,1)S(1)}, bf16[2,384,128]{2,1,0:T(8,128)(2,1)S(1)}, u32[]{:S(2)}, u32[]{:S(2)}) %collective-permute-start.16) | collective-permute-done | bytes 196640 | tf_op jit(solution)/shard_map/ppermute | solution.py:310
  60.4 1.5 %collective-permute-done.22.refs_3_ = bf16[96,384]{1,0:T(8,128)(2,1)S(1)} collective-permute-done((bf16[96,384]{1,0:T(8,128)(2,1)S(1)}, bf16[96,384]{1,0:T(8,128)(2,1)S(1)}, u32[]{:S(2)}, u32[]{:S(2)}) %collective-permute-start.22) | collective-permute-done | bytes 73760 | tf_op jit(solution)/shard_map/ppermute | solution.py:310
  62.0 1.3 %collective-permute-done.20.refs_1_ = bf16[96,384]{1,0:T(8,128)(2,1)S(1)} collective-permute-done((bf16[96,384]{1,0:T(8,128)(2,1)S(1)}, bf16[96,384]{1,0:T(8,128)(2,1)S(1)}, u32[]{:S(2)}, u32[]{:S(2)}) %collective-permute-start.20) | collective-permute-done | bytes 73760 | tf_op jit(solution)/shard_map/ppermute | solution.py:310
  63.5 0.9 %bias_grad.1 = f32[4,96,384]{2,1,0:T(8,128)} custom-call(bf16[96,384]{1,0:T(8,128)(2,1)S(1)} %get-tuple-element.96.refs_0_, bf16[96,384]{1,0:T(8,128)(2,1)S(1)} %collective-permute-done.20.refs_1_, bf16[96,384]{1,0:T(8,128)(2,1)S(1)} %collective-permute-done.21.refs_2_, bf16[96,384]{1,0:T(8,128)(2,1)S(1)} %collective-permute-done.22.refs_3_), custom_call_target="tpu_custom_call" | custom-call | tf_op jit(solution)/shard_map/bias_grad/pallas_call | solution.py:290
  64.4 0.8 %collective-permute-done.23.swapped = bf16[4,384,128]{2,1,0:T(8,128)(2,1)S(1)} collective-permute-done((bf16[4,384,128]{2,1,0:T(8,128)(2,1)S(1)}, bf16[4,384,128]{2,1,0:T(8,128)(2,1)S(1)}, u32[]{:S(2)}, u32[]{:S(2)}) %collective-permute-start.23) | collective-permute-done | bytes 393248 | tf_op jit(solution)/shard_map/ppermute | solution.py:310
  65.2 1.5 %unpack.1 = (bf16[2,384,128]{2,1,0:T(8,128)(2,1)}, bf16[2,384,128]{2,1,0:T(8,128)(2,1)}, bf16[2,384,128]{2,1,0:T(8,128)(2,1)}, bf16[2,384,128]{2,1,0:T(8,128)(2,1)}) custom-call(bf16[2,384,128]{2,1,0:T(8,128)(2,1)S(1)} %copy-done, bf16[2,384,128]{2,1,0:T(8,128)(2,1)S(1)} %copy-done.1, bf16[4,384,128]{2,1,0:T(8,128)(2,1)S(1)} %pad_maximum_fusion.packs, ...), custom_call_target="tpu_custom_call" | custom-call | tf_op jit(solution)/shard_map/unpack/pallas_call | solution.py:274
  (52 shorter events, 3.0 us)
Async XLA Ops:
  0.6 1.0 %copy-start.3 = (bf16[4,96,384]{2,1,0:T(8,128)(2,1)S(1)}, bf16[4,96,384]{2,1,0:T(8,128)(2,1)}, u32[]{:S(2)}) copy-start(bf16[4,96,384]{2,1,0:T(8,128)(2,1)} %bias.1) | copy-start | bytes 884740
  1.6 11.1 %copy-start.4 = (s32[384]{0:T(512)S(1)}, s32[384]{0:T(512)}, u32[]{:S(2)}) copy-start(s32[384]{0:T(512)} %param.12) | copy-start | bytes 4612
  1.6 11.1 %collective-permute-start.3 = (bf16[96,384]{1,0:T(8,128)(2,1)S(1)}, bf16[96,384]{1,0:T(8,128)(2,1)S(1)}, u32[]{:S(2)}, u32[]{:S(2)}) collective-permute-start(bf16[96,384]{1,0:T(8,128)(2,1)S(1)} %get-tuple-element.54), channel_id=1, source_target_pairs={{0,2},{2,0},{4,6},{6,4},{1,3},{3,1},{5,7},{7,5},{8,10},{10,8},{12,... | collective-permute-start | bytes 221192 | tf_op jit(solution)/shard_map/ppermute | solution.py:310
  4.6 8.1 %collective-permute-start.4 = (bf16[96,384]{1,0:T(8,128)(2,1)S(1)}, bf16[96,384]{1,0:T(8,128)(2,1)S(1)}, u32[]{:S(2)}, u32[]{:S(2)}) collective-permute-start(bf16[96,384]{1,0:T(8,128)(2,1)S(1)} %get-tuple-element.55), channel_id=1, source_target_pairs={{0,4},{2,6},{4,0},{6,2},{1,5},{3,7},{5,1},{7,3},{8,12},{10,14},{12... | collective-permute-start | bytes 221192 | tf_op jit(solution)/shard_map/ppermute | solution.py:310
  6.2 6.6 %collective-permute-start.5 = (bf16[96,384]{1,0:T(8,128)(2,1)S(1)}, bf16[96,384]{1,0:T(8,128)(2,1)S(1)}, u32[]{:S(2)}, u32[]{:S(2)}) collective-permute-start(bf16[96,384]{1,0:T(8,128)(2,1)S(1)} %get-tuple-element.56), channel_id=1, source_target_pairs={{0,6},{2,4},{4,2},{6,0},{1,7},{3,5},{5,3},{7,1},{8,14},{10,12},{12... | collective-permute-start | bytes 221192 | tf_op jit(solution)/shard_map/ppermute | solution.py:310
  9.1 8.5 %copy-start.5 = (bf16[384,128]{1,0:T(8,128)(2,1)S(1)}, bf16[384,128]{1,0:T(8,128)(2,1)}, u32[]{:S(2)}) copy-start(bf16[384,128]{1,0:T(8,128)(2,1)} %get-tuple-element.52) | copy-start | bytes 294916
  9.1 10.2 %copy-start.2 = (bf16[384,128]{1,0:T(8,128)(2,1)S(1)}, bf16[384,128]{1,0:T(8,128)(2,1)}, u32[]{:S(2)}) copy-start(bf16[384,128]{1,0:T(8,128)(2,1)} %get-tuple-element.49.refs_0_) | copy-start | bytes 294916
  9.1 7.1 %collective-permute-start = (bf16[2,384,128]{2,1,0:T(8,128)(2,1)}, bf16[2,384,128]{2,1,0:T(8,128)(2,1)S(1)}, u32[]{:S(2)}, u32[]{:S(2)}) collective-permute-start(bf16[2,384,128]{2,1,0:T(8,128)(2,1)} %get-tuple-element.50), channel_id=1, source_target_pairs={{0,2},{2,0},{4,6},{6,4},{1,3},{3,1},{5,7},{7,5},{8,10},{10,8},{12,... | collective-permute-start | bytes 589832 | tf_op jit(solution)/shard_map/ppermute | solution.py:310
  11.1 14.2 %collective-permute-start.10 = (bf16[2,384,128]{2,1,0:T(8,128)(2,1)}, bf16[2,384,128]{2,1,0:T(8,128)(2,1)S(1)}, u32[]{:S(2)}, u32[]{:S(2)}) collective-permute-start(bf16[2,384,128]{2,1,0:T(8,128)(2,1)} %get-tuple-element.65), channel_id=1, source_target_pairs={{0,4},{2,6},{4,0},{6,2},{1,5},{3,7},{5,1},{7,3},{8,12},{10,14},{12... | collective-permute-start | bytes 589832 | tf_op jit(solution)/shard_map/ppermute | solution.py:310
  12.7 14.5 %collective-permute-start.11 = (bf16[2,384,128]{2,1,0:T(8,128)(2,1)}, bf16[2,384,128]{2,1,0:T(8,128)(2,1)S(1)}, u32[]{:S(2)}, u32[]{:S(2)}) collective-permute-start(bf16[2,384,128]{2,1,0:T(8,128)(2,1)} %get-tuple-element.66), channel_id=1, source_target_pairs={{0,6},{2,4},{4,2},{6,0},{1,7},{3,5},{5,3},{7,1},{8,14},{10,12},{12... | collective-permute-start | bytes 589832 | tf_op jit(solution)/shard_map/ppermute | solution.py:310
  12.9 14.4 %collective-permute-start.6 = (bf16[4,96,384]{2,1,0:T(8,128)(2,1)S(1)}, bf16[4,96,384]{2,1,0:T(8,128)(2,1)S(1)}, u32[]{:S(2)}, u32[]{:S(2)}) collective-permute-start(bf16[4,96,384]{2,1,0:T(8,128)(2,1)S(1)} %maximum_select_fusion.refs_4_), channel_id=1, source_target_pairs={{0,8},{8,0},{1,9},{9,1},{2,10},{10,2},{3,11},{11,3},{4,12},{12,4},... | collective-permute-start | bytes 884744 | tf_op jit(solution)/shard_map/ppermute | solution.py:310
  15.9 2.0 %collective-permute-start.8 = (bf16[2,96,384]{2,1,0:T(8,128)(2,1)S(1)}, bf16[2,96,384]{2,1,0:T(8,128)(2,1)S(1)}, u32[]{:S(2)}, u32[]{:S(2)}) collective-permute-start(bf16[2,96,384]{2,1,0:T(8,128)(2,1)S(1)} %get-tuple-element.97), channel_id=1, source_target_pairs={{0,1},{1,0},{2,3},{3,2},{4,5},{5,4},{6,7},{7,6},{8,9},{9,8},{10,11... | collective-permute-start | bytes 442376 | tf_op jit(solution)/shard_map/ppermute | solution.py:310
  16.2 1.4 %collective-permute-start.7 = (bf16[2,96,384]{2,1,0:T(8,128)(2,1)S(1)}, bf16[2,96,384]{2,1,0:T(8,128)(2,1)S(1)}, u32[]{:S(2)}, u32[]{:S(2)}) collective-permute-start(bf16[2,96,384]{2,1,0:T(8,128)(2,1)S(1)} %get-tuple-element.98), channel_id=1, source_target_pairs={{0,1},{1,0},{2,3},{3,2},{4,5},{5,4},{6,7},{7,6},{8,9},{9,8},{10,11... | collective-permute-start | bytes 442376 | tf_op jit(solution)/shard_map/ppermute | solution.py:310
  17.6 1.3 %collective-permute-start.1 = (bf16[384,128]{1,0:T(8,128)(2,1)S(1)}, bf16[384,128]{1,0:T(8,128)(2,1)S(1)}, u32[]{:S(2)}, u32[]{:S(2)}) collective-permute-start(bf16[384,128]{1,0:T(8,128)(2,1)S(1)} %copy-done.5), channel_id=1, source_target_pairs={{0,1},{1,0},{2,3},{3,2},{4,5},{5,4},{6,7},{7,6},{8,9},{9,8},{10,11... | collective-permute-start | bytes 294920 | tf_op jit(solution)/shard_map/ppermute | solution.py:310
  17.9 1.4 %collective-permute-start.2 = (bf16[384,128]{1,0:T(8,128)(2,1)S(1)}, bf16[384,128]{1,0:T(8,128)(2,1)S(1)}, u32[]{:S(2)}, u32[]{:S(2)}) collective-permute-start(bf16[384,128]{1,0:T(8,128)(2,1)S(1)} %get-tuple-element.109), channel_id=1, source_target_pairs={{0,1},{1,0},{2,3},{3,2},{4,5},{5,4},{6,7},{7,6},{8,9},{9,8},{10,11... | collective-permute-start | bytes 294920 | tf_op jit(solution)/shard_map/ppermute | solution.py:310
  27.2 4.6 %collective-permute-start.12 = (bf16[384,128]{1,0:T(8,128)(2,1)S(1)}, bf16[384,128]{1,0:T(8,128)(2,1)S(1)}, u32[]{:S(2)}, u32[]{:S(2)}) collective-permute-start(bf16[384,128]{1,0:T(8,128)(2,1)S(1)} %get-tuple-element.107), channel_id=1, source_target_pairs={{0,1},{1,0},{2,3},{3,2},{4,5},{5,4},{6,7},{7,6},{8,9},{9,8},{10,11... | collective-permute-start | bytes 294920 | tf_op jit(solution)/shard_map/ppermute | solution.py:310
  27.3 1.7 %collective-permute-start.9 = (bf16[4,96,384]{2,1,0:T(8,128)(2,1)S(1)}, bf16[4,96,384]{2,1,0:T(8,128)(2,1)S(1)}, u32[]{:S(2)}, u32[]{:S(2)}) collective-permute-start(bf16[4,96,384]{2,1,0:T(8,128)(2,1)S(1)} %collective-permute-done.6.refs_4_), channel_id=1, source_target_pairs={{0,1},{1,0},{2,3},{3,2},{4,5},{5,4},{6,7},{7,6},{8,9},{9,8},{10,11... | collective-permute-start | bytes 884744 | tf_op jit(solution)/shard_map/ppermute | solution.py:310
  27.8 4.0 %collective-permute-start.13 = (bf16[384,128]{1,0:T(8,128)(2,1)S(1)}, bf16[384,128]{1,0:T(8,128)(2,1)S(1)}, u32[]{:S(2)}, u32[]{:S(2)}) collective-permute-start(bf16[384,128]{1,0:T(8,128)(2,1)S(1)} %get-tuple-element.105), channel_id=1, source_target_pairs={{0,1},{1,0},{2,3},{3,2},{4,5},{5,4},{6,7},{7,6},{8,9},{9,8},{10,11... | collective-permute-start | bytes 294920 | tf_op jit(solution)/shard_map/ppermute | solution.py:310
  34.6 1.7 %collective-permute-start.14 = (bf16[4,96,384]{2,1,0:T(8,128)(2,1)S(1)}, bf16[4,96,384]{2,1,0:T(8,128)(2,1)S(1)}, u32[]{:S(2)}, u32[]{:S(2)}) collective-permute-start(bf16[4,96,384]{2,1,0:T(8,128)(2,1)S(1)} %get-tuple-element.71), channel_id=1, source_target_pairs={{0,1},{1,0},{2,3},{3,2},{4,5},{5,4},{6,7},{7,6},{8,9},{9,8},{10,11... | collective-permute-start | bytes 884744 | tf_op jit(solution)/shard_map/ppermute | solution.py:310
  36.4 16.7 %collective-permute-start.18 = (bf16[4,96,384]{2,1,0:T(8,128)(2,1)S(1)}, bf16[4,96,384]{2,1,0:T(8,128)(2,1)S(1)}, u32[]{:S(2)}, u32[]{:S(2)}) collective-permute-start(bf16[4,96,384]{2,1,0:T(8,128)(2,1)S(1)} %add_convert_fusion.1), channel_id=1, source_target_pairs={{0,8},{8,0},{1,9},{9,1},{2,10},{10,2},{3,11},{11,3},{4,12},{12,4},... | collective-permute-start | bytes 884744 | tf_op jit(solution)/shard_map/ppermute | solution.py:310
  42.0 11.1 %collective-permute-start.19 = (bf16[4,96,384]{2,1,0:T(8,128)(2,1)S(1)}, bf16[4,96,384]{2,1,0:T(8,128)(2,1)S(1)}, u32[]{:S(2)}, u32[]{:S(2)}) collective-permute-start(bf16[4,96,384]{2,1,0:T(8,128)(2,1)S(1)} %get-tuple-element.84), channel_id=1, source_target_pairs={{0,1},{1,0},{2,3},{3,2},{4,5},{5,4},{6,7},{7,6},{8,9},{9,8},{10,11... | collective-permute-start | bytes 884744 | tf_op jit(solution)/shard_map/ppermute | solution.py:310
  42.1 14.3 %collective-permute-start.15 = (bf16[2,384,128]{2,1,0:T(8,128)(2,1)S(1)}, bf16[2,384,128]{2,1,0:T(8,128)(2,1)S(1)}, u32[]{:S(2)}, u32[]{:S(2)}) collective-permute-start(bf16[2,384,128]{2,1,0:T(8,128)(2,1)S(1)} %get-tuple-element.79), channel_id=1, source_target_pairs={{0,4},{2,6},{4,0},{6,2},{1,5},{3,7},{5,1},{7,3},{8,12},{10,14},{12... | collective-permute-start | bytes 589832 | tf_op jit(solution)/shard_map/ppermute | solution.py:310
  44.0 16.4 %collective-permute-start.16 = (bf16[2,384,128]{2,1,0:T(8,128)(2,1)S(1)}, bf16[2,384,128]{2,1,0:T(8,128)(2,1)S(1)}, u32[]{:S(2)}, u32[]{:S(2)}) collective-permute-start(bf16[2,384,128]{2,1,0:T(8,128)(2,1)S(1)} %get-tuple-element.80), channel_id=1, source_target_pairs={{0,6},{2,4},{4,2},{6,0},{1,7},{3,5},{5,3},{7,1},{8,14},{10,12},{12... | collective-permute-start | bytes 589832 | tf_op jit(solution)/shard_map/ppermute | solution.py:310
  45.0 15.4 %collective-permute-start.17 = (bf16[2,384,128]{2,1,0:T(8,128)(2,1)S(1)}, bf16[2,384,128]{2,1,0:T(8,128)(2,1)S(1)}, u32[]{:S(2)}, u32[]{:S(2)}) collective-permute-start(bf16[2,384,128]{2,1,0:T(8,128)(2,1)S(1)} %get-tuple-element.81), channel_id=1, source_target_pairs={{0,2},{2,0},{4,6},{6,4},{1,3},{3,1},{5,7},{7,5},{8,10},{10,8},{12,... | collective-permute-start | bytes 589832 | tf_op jit(solution)/shard_map/ppermute | solution.py:310
  53.2 8.7 %collective-permute-start.22 = (bf16[96,384]{1,0:T(8,128)(2,1)S(1)}, bf16[96,384]{1,0:T(8,128)(2,1)S(1)}, u32[]{:S(2)}, u32[]{:S(2)}) collective-permute-start(bf16[96,384]{1,0:T(8,128)(2,1)S(1)} %get-tuple-element.93), channel_id=1, source_target_pairs={{0,6},{2,4},{4,2},{6,0},{1,7},{3,5},{5,3},{7,1},{8,14},{10,12},{12... | collective-permute-start | bytes 221192 | tf_op jit(solution)/shard_map/ppermute | solution.py:310
  53.6 8.4 %collective-permute-start.21 = (bf16[96,384]{1,0:T(8,128)(2,1)S(1)}, bf16[96,384]{1,0:T(8,128)(2,1)S(1)}, u32[]{:S(2)}, u32[]{:S(2)}) collective-permute-start(bf16[96,384]{1,0:T(8,128)(2,1)S(1)} %get-tuple-element.94), channel_id=1, source_target_pairs={{0,4},{2,6},{4,0},{6,2},{1,5},{3,7},{5,1},{7,3},{8,12},{10,14},{12... | collective-permute-start | bytes 221192 | tf_op jit(solution)/shard_map/ppermute | solution.py:310
  56.4 6.9 %collective-permute-start.20 = (bf16[96,384]{1,0:T(8,128)(2,1)S(1)}, bf16[96,384]{1,0:T(8,128)(2,1)S(1)}, u32[]{:S(2)}, u32[]{:S(2)}) collective-permute-start(bf16[96,384]{1,0:T(8,128)(2,1)S(1)} %get-tuple-element.95), channel_id=1, source_target_pairs={{0,2},{2,0},{4,6},{6,4},{1,3},{3,1},{5,7},{7,5},{8,10},{10,8},{12,... | collective-permute-start | bytes 221192 | tf_op jit(solution)/shard_map/ppermute | solution.py:310
  63.3 1.9 %copy-start = (bf16[2,384,128]{2,1,0:T(8,128)(2,1)S(1)}, bf16[2,384,128]{2,1,0:T(8,128)(2,1)}, u32[]{:S(2)}) copy-start(bf16[2,384,128]{2,1,0:T(8,128)(2,1)} %gate.1) | copy-start | bytes 589828
  63.3 1.9 %copy-start.1 = (bf16[2,384,128]{2,1,0:T(8,128)(2,1)S(1)}, bf16[2,384,128]{2,1,0:T(8,128)(2,1)}, u32[]{:S(2)}) copy-start(bf16[2,384,128]{2,1,0:T(8,128)(2,1)} %cot.1) | copy-start | bytes 589828
  63.4 1.8 %collective-permute-start.23 = (bf16[4,384,128]{2,1,0:T(8,128)(2,1)S(1)}, bf16[4,384,128]{2,1,0:T(8,128)(2,1)S(1)}, u32[]{:S(2)}, u32[]{:S(2)}) collective-permute-start(bf16[4,384,128]{2,1,0:T(8,128)(2,1)S(1)} %pad_maximum_fusion.1), channel_id=1, source_target_pairs={{0,1},{1,0},{2,3},{3,2},{4,5},{5,4},{6,7},{7,6},{8,9},{9,8},{10,11... | collective-permute-start | bytes 1179656 | tf_op jit(solution)/shard_map/ppermute | solution.py:310

commit v5 on v4

--- a/solution.py
+++ b/solution.py
@@ -349,7 +349,7 @@
                 others[g] = other_core(groups[g])
             mine, closed, ended = groups[g], a == len(orders) - 1, g == order[-1]
             if closed and g != order[0]:
-                mine, last = lax.optimization_barrier((mine, sums[order[order.index(g) - 1]]))
+                mine, last, back = lax.optimization_barrier((mine, sums[order[order.index(g) - 1]], back))
                 sums[order[order.index(g) - 1]] = last
             out = main(
                 ours, swapped, mine, others[g], earlier, before[g], scaling, size, starts[g], relative, ended, closed, 1 - a
@@ -366,6 +366,7 @@
             sums[g] = (d_mine + wide(other_core(d_other))).astype(jnp.bfloat16)
         if a == 0:
             stay, pass_on, *earlier = earlier
+            back = other_core(pass_on)
         returned += earlier
     d_sum = sums[0]
     if not relative:
@@ -378,7 +379,8 @@
     returned = lax.optimization_barrier(tuple(returned))
     returned = [near_swap(returned[s - 1], s) for s in SENT]
     returned = lax.optimization_barrier((*returned, *pieces))[:3]
-    swapped = other_core(jnp.stack([pass_on] + [pack[1] for pack in returned]))
+    late = other_core(jnp.stack([pack[1] for pack in returned]))
+    swapped = jnp.concatenate([back[None], late])
     packs = jnp.stack([stay] + [pack[0] for pack in returned])
     return (*post(gate_logits, grad_out, packs, swapped), bias_out(pieces))
 

time: 66.8 us -> 66.7 us (level)
    ppermute x24 -> x25, waiting for transfers between devices: 24.4 us -> 24.2 us  [swap(): lax.ppermute(value, axes, [(i, i ^ s) for i in range(count)])]
    ppermute x24 -> x25, starting transfers between devices: 23.2 us -> 23.3 us  [swap(): lax.ppermute(value, axes, [(i, i ^ s) for i in range(count)])]
  transfers between devices with their start and end apart: 24 -> 25, of which waited for: 13 -> 14; matrix products, arithmetic and copies ran while one was open for 1% -> 1% of each run, Pallas kernels for 19% -> 19%
where the time goes in v5:
time: 66.7 us; the launch traced here: 66.5 us
  waiting for transfers between devices  24.2 us (36%)
  starting transfers between devices  23.3 us (35%)
  Pallas kernels  16.6 us (25%)
  local copies, waits for them, and re-layouts  1.17 us (2%)
  between operations  0.92 us (1%)
    ppermute x25, waiting for transfers between devices, swap(): lax.ppermute(value, axes, [(i, i ^ s) for i in range(count)])  24.2 us
    ppermute x25, starting transfers between devices, swap(): lax.ppermute(value, axes, [(i, i ^ s) for i in range(count)])  23.3 us
    pallas_call x4, Pallas kernels, main(): pl.pallas_call(functools.partial(main_kernel, scaling, size, blocks, star...  11.4 us
    pallas_call x1, Pallas kernels, make_packs(): pl.pallas_call(pack_kernel, in_specs=[pl.BlockSpec(memory_space=pl.ANY)]...  2.87 us
    pallas_call x1, Pallas kernels, post(): pl.pallas_call(post_kernel, out_shape=[jax.ShapeDtypeStruct(gate.shape, j...  1.46 us
  transfers between devices with their start and end apart: 25, of which 14 were waited for; matrix products, arithmetic and copies ran while one was open for 1% of the time, Pallas kernels for 19%

profile of v5, /device:TPU:0, one launch (start us, length us, event | category | flops | bytes accessed | tf_op | source)
XLA Modules:
  0.0 66.5 jit_solution(8665428179735901368)
XLA Ops:
  0.6 1.0 %copy-done.3 = bf16[4,96,384]{2,1,0:T(8,128)(2,1)S(1)} copy-done((bf16[4,96,384]{2,1,0:T(8,128)(2,1)S(1)}, bf16[4,96,384]{2,1,0:T(8,128)(2,1)}, u32[]{:S(2)}) %copy-start.3) | copy-done | bytes 294936
  1.6 3.0 %collective-permute-start.3 = (bf16[96,384]{1,0:T(8,128)(2,1)S(1)}, bf16[96,384]{1,0:T(8,128)(2,1)S(1)}, u32[]{:S(2)}, u32[]{:S(2)}) collective-permute-start(bf16[96,384]{1,0:T(8,128)(2,1)S(1)} %get-tuple-element.55), channel_id=1, source_target_pairs={{0,2},{2,0},{4,6},{6,4},{1,3},{3,1},{5,7},{7,5},{8,10},{10,8},{12,... | collective-permute-start | bytes 221192 | tf_op jit(solution)/shard_map/ppermute | solution.py:310
  4.6 1.6 %collective-permute-start.4 = (bf16[96,384]{1,0:T(8,128)(2,1)S(1)}, bf16[96,384]{1,0:T(8,128)(2,1)S(1)}, u32[]{:S(2)}, u32[]{:S(2)}) collective-permute-start(bf16[96,384]{1,0:T(8,128)(2,1)S(1)} %get-tuple-element.56), channel_id=1, source_target_pairs={{0,4},{2,6},{4,0},{6,2},{1,5},{3,7},{5,1},{7,3},{8,12},{10,14},{12... | collective-permute-start | bytes 221192 | tf_op jit(solution)/shard_map/ppermute | solution.py:310
  6.2 2.9 %pack.1 = (bf16[2,384,128]{2,1,0:T(8,128)(2,1)}, bf16[2,384,128]{2,1,0:T(8,128)(2,1)}, bf16[2,384,128]{2,1,0:T(8,128)(2,1)}, bf16[384,128]{1,0:T(8,128)(2,1)}, bf16[384,128]{1,0:T(8,128)(2,1)}) custom-call(bf16[2,384,128]{2,1,0:T(8,128)(2,1)} %refs_0_.1, bf16[2,384,128]{2,1,0:T(8,128)(2,1)} %refs_1_.1, bf16[2,384,128]{2,1,0:T(8,128)(2,1)} %refs_2_.1, ...), custom_call_target="tpu_custom_call" | custom-call | tf_op jit(solution)/shard_map/pack/pallas_call | solution.py:68
  9.1 2.0 %collective-permute-start = (bf16[2,384,128]{2,1,0:T(8,128)(2,1)}, bf16[2,384,128]{2,1,0:T(8,128)(2,1)S(1)}, u32[]{:S(2)}, u32[]{:S(2)}) collective-permute-start(bf16[2,384,128]{2,1,0:T(8,128)(2,1)} %get-tuple-element.51), channel_id=1, source_target_pairs={{0,2},{2,0},{4,6},{6,4},{1,3},{3,1},{5,7},{7,5},{8,10},{10,8},{12,... | collective-permute-start | bytes 589832 | tf_op jit(solution)/shard_map/ppermute | solution.py:310
  11.1 1.6 %collective-permute-start.10 = (bf16[2,384,128]{2,1,0:T(8,128)(2,1)}, bf16[2,384,128]{2,1,0:T(8,128)(2,1)S(1)}, u32[]{:S(2)}, u32[]{:S(2)}) collective-permute-start(bf16[2,384,128]{2,1,0:T(8,128)(2,1)} %get-tuple-element.66), channel_id=1, source_target_pairs={{0,4},{2,6},{4,0},{6,2},{1,5},{3,7},{5,1},{7,3},{8,12},{10,14},{12... | collective-permute-start | bytes 589832 | tf_op jit(solution)/shard_map/ppermute | solution.py:310
  12.9 3.0 %collective-permute-start.6 = (bf16[4,96,384]{2,1,0:T(8,128)(2,1)S(1)}, bf16[4,96,384]{2,1,0:T(8,128)(2,1)S(1)}, u32[]{:S(2)}, u32[]{:S(2)}) collective-permute-start(bf16[4,96,384]{2,1,0:T(8,128)(2,1)S(1)} %maximum_select_fusion.refs_4_), channel_id=1, source_target_pairs={{0,8},{8,0},{1,9},{9,1},{2,10},{10,2},{3,11},{11,3},{4,12},{12,4},... | collective-permute-start | bytes 884744 | tf_op jit(solution)/shard_map/ppermute | solution.py:310
  16.5 1.1 %collective-permute-done.7 = bf16[2,96,384]{2,1,0:T(8,128)(2,1)S(1)} collective-permute-done((bf16[2,96,384]{2,1,0:T(8,128)(2,1)S(1)}, bf16[2,96,384]{2,1,0:T(8,128)(2,1)S(1)}, u32[]{:S(2)}, u32[]{:S(2)}) %collective-permute-start.7) | collective-permute-done | bytes 147488 | tf_op jit(solution)/shard_map/ppermute | solution.py:310
  18.2 0.7 %collective-permute-done.1.refs_2_ = bf16[384,128]{1,0:T(8,128)(2,1)S(1)} collective-permute-done((bf16[384,128]{1,0:T(8,128)(2,1)S(1)}, bf16[384,128]{1,0:T(8,128)(2,1)S(1)}, u32[]{:S(2)}, u32[]{:S(2)}) %collective-permute-start.1) | collective-permute-done | bytes 98336 | tf_op jit(solution)/shard_map/ppermute | solution.py:310
  19.3 2.7 %attention.4 = (f32[384,768]{1,0:T(8,128)S(1)}, bf16[768,64]{1,0:T(8,128)(2,1)S(1)}, bf16[768,64]{1,0:T(8,128)(2,1)S(1)}, f32[64,768]{1,0:T(8,128)S(1)}, f32[64,768]{1,0:T(8,128)S(1)}) custom-call(bf16[384,128]{1,0:T(8,128)(2,1)S(1)} %copy-done.2, bf16[384,128]{1,0:T(8,128)(2,1)S(1)} %get-tuple-element.112.refs_1_, ...), custom_call_target="tpu_custom_call" | custom-call | flops 1 | bytes 1 | tf_op jit(solution)/shard_map/attention/pallas_call | solution.py:227
  22.0 3.2 %collective-permute-done.10 = bf16[2,384,128]{2,1,0:T(8,128)(2,1)S(1)} collective-permute-done((bf16[2,384,128]{2,1,0:T(8,128)(2,1)}, bf16[2,384,128]{2,1,0:T(8,128)(2,1)S(1)}, u32[]{:S(2)}, u32[]{:S(2)}) %collective-permute-start.10) | collective-permute-done | bytes 196640 | tf_op jit(solution)/shard_map/ppermute | solution.py:310
  25.2 1.9 %collective-permute-done.11 = bf16[2,384,128]{2,1,0:T(8,128)(2,1)S(1)} collective-permute-done((bf16[2,384,128]{2,1,0:T(8,128)(2,1)}, bf16[2,384,128]{2,1,0:T(8,128)(2,1)S(1)}, u32[]{:S(2)}, u32[]{:S(2)}) %collective-permute-start.11) | collective-permute-done | bytes 196640 | tf_op jit(solution)/shard_map/ppermute | solution.py:310
  27.3 0.5 collective-permute-start.9
  28.0 1.0 %collective-permute-done.9.refs_5_ = bf16[4,96,384]{2,1,0:T(8,128)(2,1)S(1)} collective-permute-done((bf16[4,96,384]{2,1,0:T(8,128)(2,1)S(1)}, bf16[4,96,384]{2,1,0:T(8,128)(2,1)S(1)}, u32[]{:S(2)}, u32[]{:S(2)}) %collective-permute-start.9) | collective-permute-done | bytes 294944 | tf_op jit(solution)/shard_map/ppermute | solution.py:310
  29.0 2.8 %attention.5 = (f32[384,768]{1,0:T(8,128)S(1)}, bf16[384,128]{1,0:T(8,128)(2,1)S(1)}, bf16[384,128]{1,0:T(8,128)(2,1)S(1)}, bf16[2,384,128]{2,1,0:T(8,128)(2,1)S(1)}) custom-call(bf16[384,128]{1,0:T(8,128)(2,1)S(1)} %copy-done.2, bf16[384,128]{1,0:T(8,128)(2,1)S(1)} %get-tuple-element.112.refs_1_, bf16[384,128]{1,0:T(8,128)(2,1)S(1)} %collective-permute-done.1.refs_2_, ...), custom_call_target="tpu_custom_call" | custom-call | flops 1 | bytes 1 | tf_op jit(solution)/shard_map/attention/pallas_call | solution.py:227
  31.9 2.8 %attention.6 = (bf16[4,96,384]{2,1,0:T(8,128)(2,1)S(1)}, bf16[4,96,384]{2,1,0:T(8,128)(2,1)S(1)}, bf16[768,64]{1,0:T(8,128)(2,1)S(1)}, bf16[768,64]{1,0:T(8,128)...) custom-call(bf16[384,128]{1,0:T(8,128)(2,1)S(1)} %get-tuple-element.110.refs_0_, ...), custom_call_target="tpu_custom_call" | custom-call | flops 1 | bytes 1 | tf_op jit(solution)/shard_map/attention/pallas_call | solution.py:227
  34.6 0.4 collective-permute-start.14
  35.2 1.1 %collective-permute-done.14 = bf16[4,96,384]{2,1,0:T(8,128)(2,1)S(1)} collective-permute-done((bf16[4,96,384]{2,1,0:T(8,128)(2,1)S(1)}, bf16[4,96,384]{2,1,0:T(8,128)(2,1)S(1)}, u32[]{:S(2)}, u32[]{:S(2)}) %collective-permute-start.14) | collective-permute-done | bytes 294944 | tf_op jit(solution)/shard_map/ppermute | solution.py:310
  36.4 2.5 %collective-permute-start.19 = (bf16[4,96,384]{2,1,0:T(8,128)(2,1)S(1)}, bf16[4,96,384]{2,1,0:T(8,128)(2,1)S(1)}, u32[]{:S(2)}, u32[]{:S(2)}) collective-permute-start(bf16[4,96,384]{2,1,0:T(8,128)(2,1)S(1)} %add_convert_fusion.1), channel_id=1, source_target_pairs={{0,8},{8,0},{1,9},{9,1},{2,10},{10,2},{3,11},{11,3},{4,12},{12,4},... | collective-permute-start | bytes 884744 | tf_op jit(solution)/shard_map/ppermute | solution.py:310
  39.0 3.1 %attention.7 = (bf16[4,96,384]{2,1,0:T(8,128)(2,1)S(1)}, bf16[4,96,384]{2,1,0:T(8,128)(2,1)S(1)}, bf16[2,384,128]{2,1,0:T(8,128)(2,1)S(1)}, bf16[2,384,128]{2,1,0:T(8,128)(2,1)S(1)}) custom-call(bf16[384,128]{1,0:T(8,128)(2,1)S(1)} %get-tuple-element.110.refs_0_, bf16[384,128]{1,0:T(8,128)(2,1)S(1)} %get-tuple-element.108.refs_1_, ...), custom_call_target="tpu_custom_call" | custom-call | flops 1 | bytes 1 | tf_op jit(solution)/shard_map/attention/pallas_call | solution.py:227
  42.1 1.9 %collective-permute-start.16 = (bf16[2,384,128]{2,1,0:T(8,128)(2,1)S(1)}, bf16[2,384,128]{2,1,0:T(8,128)(2,1)S(1)}, u32[]{:S(2)}, u32[]{:S(2)}) collective-permute-start(bf16[2,384,128]{2,1,0:T(8,128)(2,1)S(1)} %get-tuple-element.81), channel_id=1, source_target_pairs={{0,4},{2,6},{4,0},{6,2},{1,5},{3,7},{5,1},{7,3},{8,12},{10,14},{12... | collective-permute-start | bytes 589832 | tf_op jit(solution)/shard_map/ppermute | solution.py:310
  44.0 1.0 %collective-permute-start.17 = (bf16[2,384,128]{2,1,0:T(8,128)(2,1)S(1)}, bf16[2,384,128]{2,1,0:T(8,128)(2,1)S(1)}, u32[]{:S(2)}, u32[]{:S(2)}) collective-permute-start(bf16[2,384,128]{2,1,0:T(8,128)(2,1)S(1)} %get-tuple-element.82), channel_id=1, source_target_pairs={{0,6},{2,4},{4,2},{6,0},{1,7},{3,5},{5,3},{7,1},{8,14},{10,12},{12... | collective-permute-start | bytes 589832 | tf_op jit(solution)/shard_map/ppermute | solution.py:310
  45.1 0.6 collective-permute-start.18
  45.7 7.4 %collective-permute-done.19 = bf16[4,96,384]{2,1,0:T(8,128)(2,1)S(1)} collective-permute-done((bf16[4,96,384]{2,1,0:T(8,128)(2,1)S(1)}, bf16[4,96,384]{2,1,0:T(8,128)(2,1)S(1)}, u32[]{:S(2)}, u32[]{:S(2)}) %collective-permute-start.19) | collective-permute-done | bytes 294944 | tf_op jit(solution)/shard_map/ppermute | solution.py:310
  53.6 2.8 %collective-permute-start.22 = (bf16[96,384]{1,0:T(8,128)(2,1)S(1)}, bf16[96,384]{1,0:T(8,128)(2,1)S(1)}, u32[]{:S(2)}, u32[]{:S(2)}) collective-permute-start(bf16[96,384]{1,0:T(8,128)(2,1)S(1)} %get-tuple-element.96), channel_id=1, source_target_pairs={{0,4},{2,6},{4,0},{6,2},{1,5},{3,7},{5,1},{7,3},{8,12},{10,14},{12... | collective-permute-start | bytes 221192 | tf_op jit(solution)/shard_map/ppermute | solution.py:310
  56.4 0.4 collective-permute-start.21
  56.8 3.7 %collective-permute-done.17 = bf16[2,384,128]{2,1,0:T(8,128)(2,1)S(1)} collective-permute-done((bf16[2,384,128]{2,1,0:T(8,128)(2,1)S(1)}, bf16[2,384,128]{2,1,0:T(8,128)(2,1)S(1)}, u32[]{:S(2)}, u32[]{:S(2)}) %collective-permute-start.17) | collective-permute-done | bytes 196640 | tf_op jit(solution)/shard_map/ppermute | solution.py:310
  60.5 1.5 %collective-permute-done.23.refs_3_ = bf16[96,384]{1,0:T(8,128)(2,1)S(1)} collective-permute-done((bf16[96,384]{1,0:T(8,128)(2,1)S(1)}, bf16[96,384]{1,0:T(8,128)(2,1)S(1)}, u32[]{:S(2)}, u32[]{:S(2)}) %collective-permute-start.23) | collective-permute-done | bytes 73760 | tf_op jit(solution)/shard_map/ppermute | solution.py:310
  62.0 1.3 %collective-permute-done.21.refs_1_ = bf16[96,384]{1,0:T(8,128)(2,1)S(1)} collective-permute-done((bf16[96,384]{1,0:T(8,128)(2,1)S(1)}, bf16[96,384]{1,0:T(8,128)(2,1)S(1)}, u32[]{:S(2)}, u32[]{:S(2)}) %collective-permute-start.21) | collective-permute-done | bytes 73760 | tf_op jit(solution)/shard_map/ppermute | solution.py:310
  63.5 0.9 %bias_grad.1 = f32[4,96,384]{2,1,0:T(8,128)} custom-call(bf16[96,384]{1,0:T(8,128)(2,1)S(1)} %get-tuple-element.98.refs_0_, bf16[96,384]{1,0:T(8,128)(2,1)S(1)} %collective-permute-done.21.refs_1_, bf16[96,384]{1,0:T(8,128)(2,1)S(1)} %collective-permute-done.22.refs_2_, bf16[96,384]{1,0:T(8,128)(2,1)S(1)} %collective-permute-done.23.refs_3_), custom_call_target="tpu_custom_call" | custom-call | tf_op jit(solution)/shard_map/bias_grad/pallas_call | solution.py:290
  64.4 0.6 collective-permute-done.24
  65.1 1.5 %unpack.1 = (bf16[2,384,128]{2,1,0:T(8,128)(2,1)}, bf16[2,384,128]{2,1,0:T(8,128)(2,1)}, bf16[2,384,128]{2,1,0:T(8,128)(2,1)}, bf16[2,384,128]{2,1,0:T(8,128)(2,1)}) custom-call(bf16[2,384,128]{2,1,0:T(8,128)(2,1)S(1)} %copy-done, bf16[2,384,128]{2,1,0:T(8,128)(2,1)S(1)} %copy-done.1, bf16[4,384,128]{2,1,0:T(8,128)(2,1)S(1)} %pad_maximum_fusion.packs, ...), custom_call_target="tpu_custom_call" | custom-call | tf_op jit(solution)/shard_map/unpack/pallas_call | solution.py:274
  (55 shorter events, 3.2 us)
Async XLA Ops:
  0.6 1.0 %copy-start.3 = (bf16[4,96,384]{2,1,0:T(8,128)(2,1)S(1)}, bf16[4,96,384]{2,1,0:T(8,128)(2,1)}, u32[]{:S(2)}) copy-start(bf16[4,96,384]{2,1,0:T(8,128)(2,1)} %bias.1) | copy-start | bytes 884740
  1.6 11.1 %copy-start.4 = (s32[384]{0:T(512)S(1)}, s32[384]{0:T(512)}, u32[]{:S(2)}) copy-start(s32[384]{0:T(512)} %param.12) | copy-start | bytes 4612
  1.6 11.1 %collective-permute-start.3 = (bf16[96,384]{1,0:T(8,128)(2,1)S(1)}, bf16[96,384]{1,0:T(8,128)(2,1)S(1)}, u32[]{:S(2)}, u32[]{:S(2)}) collective-permute-start(bf16[96,384]{1,0:T(8,128)(2,1)S(1)} %get-tuple-element.55), channel_id=1, source_target_pairs={{0,2},{2,0},{4,6},{6,4},{1,3},{3,1},{5,7},{7,5},{8,10},{10,8},{12,... | collective-permute-start | bytes 221192 | tf_op jit(solution)/shard_map/ppermute | solution.py:310
  4.6 8.1 %collective-permute-start.4 = (bf16[96,384]{1,0:T(8,128)(2,1)S(1)}, bf16[96,384]{1,0:T(8,128)(2,1)S(1)}, u32[]{:S(2)}, u32[]{:S(2)}) collective-permute-start(bf16[96,384]{1,0:T(8,128)(2,1)S(1)} %get-tuple-element.56), channel_id=1, source_target_pairs={{0,4},{2,6},{4,0},{6,2},{1,5},{3,7},{5,1},{7,3},{8,12},{10,14},{12... | collective-permute-start | bytes 221192 | tf_op jit(solution)/shard_map/ppermute | solution.py:310
  6.2 6.6 %collective-permute-start.5 = (bf16[96,384]{1,0:T(8,128)(2,1)S(1)}, bf16[96,384]{1,0:T(8,128)(2,1)S(1)}, u32[]{:S(2)}, u32[]{:S(2)}) collective-permute-start(bf16[96,384]{1,0:T(8,128)(2,1)S(1)} %get-tuple-element.57), channel_id=1, source_target_pairs={{0,6},{2,4},{4,2},{6,0},{1,7},{3,5},{5,3},{7,1},{8,14},{10,12},{12... | collective-permute-start | bytes 221192 | tf_op jit(solution)/shard_map/ppermute | solution.py:310
  9.1 8.5 %copy-start.5 = (bf16[384,128]{1,0:T(8,128)(2,1)S(1)}, bf16[384,128]{1,0:T(8,128)(2,1)}, u32[]{:S(2)}) copy-start(bf16[384,128]{1,0:T(8,128)(2,1)} %get-tuple-element.53) | copy-start | bytes 294916
  9.1 10.2 %copy-start.2 = (bf16[384,128]{1,0:T(8,128)(2,1)S(1)}, bf16[384,128]{1,0:T(8,128)(2,1)}, u32[]{:S(2)}) copy-start(bf16[384,128]{1,0:T(8,128)(2,1)} %get-tuple-element.50.refs_0_) | copy-start | bytes 294916
  9.1 7.1 %collective-permute-start = (bf16[2,384,128]{2,1,0:T(8,128)(2,1)}, bf16[2,384,128]{2,1,0:T(8,128)(2,1)S(1)}, u32[]{:S(2)}, u32[]{:S(2)}) collective-permute-start(bf16[2,384,128]{2,1,0:T(8,128)(2,1)} %get-tuple-element.51), channel_id=1, source_target_pairs={{0,2},{2,0},{4,6},{6,4},{1,3},{3,1},{5,7},{7,5},{8,10},{10,8},{12,... | collective-permute-start | bytes 589832 | tf_op jit(solution)/shard_map/ppermute | solution.py:310
  11.1 14.2 %collective-permute-start.10 = (bf16[2,384,128]{2,1,0:T(8,128)(2,1)}, bf16[2,384,128]{2,1,0:T(8,128)(2,1)S(1)}, u32[]{:S(2)}, u32[]{:S(2)}) collective-permute-start(bf16[2,384,128]{2,1,0:T(8,128)(2,1)} %get-tuple-element.66), channel_id=1, source_target_pairs={{0,4},{2,6},{4,0},{6,2},{1,5},{3,7},{5,1},{7,3},{8,12},{10,14},{12... | collective-permute-start | bytes 589832 | tf_op jit(solution)/shard_map/ppermute | solution.py:310
  12.7 14.5 %collective-permute-start.11 = (bf16[2,384,128]{2,1,0:T(8,128)(2,1)}, bf16[2,384,128]{2,1,0:T(8,128)(2,1)S(1)}, u32[]{:S(2)}, u32[]{:S(2)}) collective-permute-start(bf16[2,384,128]{2,1,0:T(8,128)(2,1)} %get-tuple-element.67), channel_id=1, source_target_pairs={{0,6},{2,4},{4,2},{6,0},{1,7},{3,5},{5,3},{7,1},{8,14},{10,12},{12... | collective-permute-start | bytes 589832 | tf_op jit(solution)/shard_map/ppermute | solution.py:310
  12.9 14.4 %collective-permute-start.6 = (bf16[4,96,384]{2,1,0:T(8,128)(2,1)S(1)}, bf16[4,96,384]{2,1,0:T(8,128)(2,1)S(1)}, u32[]{:S(2)}, u32[]{:S(2)}) collective-permute-start(bf16[4,96,384]{2,1,0:T(8,128)(2,1)S(1)} %maximum_select_fusion.refs_4_), channel_id=1, source_target_pairs={{0,8},{8,0},{1,9},{9,1},{2,10},{10,2},{3,11},{11,3},{4,12},{12,4},... | collective-permute-start | bytes 884744 | tf_op jit(solution)/shard_map/ppermute | solution.py:310
  15.9 2.0 %collective-permute-start.8 = (bf16[2,96,384]{2,1,0:T(8,128)(2,1)S(1)}, bf16[2,96,384]{2,1,0:T(8,128)(2,1)S(1)}, u32[]{:S(2)}, u32[]{:S(2)}) collective-permute-start(bf16[2,96,384]{2,1,0:T(8,128)(2,1)S(1)} %get-tuple-element.99), channel_id=1, source_target_pairs={{0,1},{1,0},{2,3},{3,2},{4,5},{5,4},{6,7},{7,6},{8,9},{9,8},{10,11... | collective-permute-start | bytes 442376 | tf_op jit(solution)/shard_map/ppermute | solution.py:310
  16.2 1.4 %collective-permute-start.7 = (bf16[2,96,384]{2,1,0:T(8,128)(2,1)S(1)}, bf16[2,96,384]{2,1,0:T(8,128)(2,1)S(1)}, u32[]{:S(2)}, u32[]{:S(2)}) collective-permute-start(bf16[2,96,384]{2,1,0:T(8,128)(2,1)S(1)} %get-tuple-element.100), channel_id=1, source_target_pairs={{0,1},{1,0},{2,3},{3,2},{4,5},{5,4},{6,7},{7,6},{8,9},{9,8},{10,11... | collective-permute-start | bytes 442376 | tf_op jit(solution)/shard_map/ppermute | solution.py:310
  17.6 1.3 %collective-permute-start.1 = (bf16[384,128]{1,0:T(8,128)(2,1)S(1)}, bf16[384,128]{1,0:T(8,128)(2,1)S(1)}, u32[]{:S(2)}, u32[]{:S(2)}) collective-permute-start(bf16[384,128]{1,0:T(8,128)(2,1)S(1)} %copy-done.5), channel_id=1, source_target_pairs={{0,1},{1,0},{2,3},{3,2},{4,5},{5,4},{6,7},{7,6},{8,9},{9,8},{10,11... | collective-permute-start | bytes 294920 | tf_op jit(solution)/shard_map/ppermute | solution.py:310
  17.9 1.4 %collective-permute-start.2 = (bf16[384,128]{1,0:T(8,128)(2,1)S(1)}, bf16[384,128]{1,0:T(8,128)(2,1)S(1)}, u32[]{:S(2)}, u32[]{:S(2)}) collective-permute-start(bf16[384,128]{1,0:T(8,128)(2,1)S(1)} %get-tuple-element.111), channel_id=1, source_target_pairs={{0,1},{1,0},{2,3},{3,2},{4,5},{5,4},{6,7},{7,6},{8,9},{9,8},{10,11... | collective-permute-start | bytes 294920 | tf_op jit(solution)/shard_map/ppermute | solution.py:310
  27.2 4.6 %collective-permute-start.12 = (bf16[384,128]{1,0:T(8,128)(2,1)S(1)}, bf16[384,128]{1,0:T(8,128)(2,1)S(1)}, u32[]{:S(2)}, u32[]{:S(2)}) collective-permute-start(bf16[384,128]{1,0:T(8,128)(2,1)S(1)} %get-tuple-element.109), channel_id=1, source_target_pairs={{0,1},{1,0},{2,3},{3,2},{4,5},{5,4},{6,7},{7,6},{8,9},{9,8},{10,11... | collective-permute-start | bytes 294920 | tf_op jit(solution)/shard_map/ppermute | solution.py:310
  27.3 1.7 %collective-permute-start.9 = (bf16[4,96,384]{2,1,0:T(8,128)(2,1)S(1)}, bf16[4,96,384]{2,1,0:T(8,128)(2,1)S(1)}, u32[]{:S(2)}, u32[]{:S(2)}) collective-permute-start(bf16[4,96,384]{2,1,0:T(8,128)(2,1)S(1)} %collective-permute-done.6.refs_4_), channel_id=1, source_target_pairs={{0,1},{1,0},{2,3},{3,2},{4,5},{5,4},{6,7},{7,6},{8,9},{9,8},{10,11... | collective-permute-start | bytes 884744 | tf_op jit(solution)/shard_map/ppermute | solution.py:310
  27.8 4.0 %collective-permute-start.13 = (bf16[384,128]{1,0:T(8,128)(2,1)S(1)}, bf16[384,128]{1,0:T(8,128)(2,1)S(1)}, u32[]{:S(2)}, u32[]{:S(2)}) collective-permute-start(bf16[384,128]{1,0:T(8,128)(2,1)S(1)} %get-tuple-element.107), channel_id=1, source_target_pairs={{0,1},{1,0},{2,3},{3,2},{4,5},{5,4},{6,7},{7,6},{8,9},{9,8},{10,11... | collective-permute-start | bytes 294920 | tf_op jit(solution)/shard_map/ppermute | solution.py:310
  34.6 1.7 %collective-permute-start.14 = (bf16[4,96,384]{2,1,0:T(8,128)(2,1)S(1)}, bf16[4,96,384]{2,1,0:T(8,128)(2,1)S(1)}, u32[]{:S(2)}, u32[]{:S(2)}) collective-permute-start(bf16[4,96,384]{2,1,0:T(8,128)(2,1)S(1)} %get-tuple-element.72), channel_id=1, source_target_pairs={{0,1},{1,0},{2,3},{3,2},{4,5},{5,4},{6,7},{7,6},{8,9},{9,8},{10,11... | collective-permute-start | bytes 884744 | tf_op jit(solution)/shard_map/ppermute | solution.py:310
  35.1 1.3 %collective-permute-start.15 = (bf16[384,128]{1,0:T(8,128)(2,1)S(1)}, bf16[384,128]{1,0:T(8,128)(2,1)S(1)}, u32[]{:S(2)}, u32[]{:S(2)}) collective-permute-start(bf16[384,128]{1,0:T(8,128)(2,1)S(1)} %get-tuple-element.73), channel_id=1, source_target_pairs={{0,1},{1,0},{2,3},{3,2},{4,5},{5,4},{6,7},{7,6},{8,9},{9,8},{10,11... | collective-permute-start | bytes 294920 | tf_op jit(solution)/shard_map/ppermute | solution.py:310
  36.4 16.6 %collective-permute-start.19 = (bf16[4,96,384]{2,1,0:T(8,128)(2,1)S(1)}, bf16[4,96,384]{2,1,0:T(8,128)(2,1)S(1)}, u32[]{:S(2)}, u32[]{:S(2)}) collective-permute-start(bf16[4,96,384]{2,1,0:T(8,128)(2,1)S(1)} %add_convert_fusion.1), channel_id=1, source_target_pairs={{0,8},{8,0},{1,9},{9,1},{2,10},{10,2},{3,11},{11,3},{4,12},{12,4},... | collective-permute-start | bytes 884744 | tf_op jit(solution)/shard_map/ppermute | solution.py:310
  42.0 11.1 %collective-permute-start.20 = (bf16[4,96,384]{2,1,0:T(8,128)(2,1)S(1)}, bf16[4,96,384]{2,1,0:T(8,128)(2,1)S(1)}, u32[]{:S(2)}, u32[]{:S(2)}) collective-permute-start(bf16[4,96,384]{2,1,0:T(8,128)(2,1)S(1)} %get-tuple-element.86), channel_id=1, source_target_pairs={{0,1},{1,0},{2,3},{3,2},{4,5},{5,4},{6,7},{7,6},{8,9},{9,8},{10,11... | collective-permute-start | bytes 884744 | tf_op jit(solution)/shard_map/ppermute | solution.py:310
  42.1 14.3 %collective-permute-start.16 = (bf16[2,384,128]{2,1,0:T(8,128)(2,1)S(1)}, bf16[2,384,128]{2,1,0:T(8,128)(2,1)S(1)}, u32[]{:S(2)}, u32[]{:S(2)}) collective-permute-start(bf16[2,384,128]{2,1,0:T(8,128)(2,1)S(1)} %get-tuple-element.81), channel_id=1, source_target_pairs={{0,4},{2,6},{4,0},{6,2},{1,5},{3,7},{5,1},{7,3},{8,12},{10,14},{12... | collective-permute-start | bytes 589832 | tf_op jit(solution)/shard_map/ppermute | solution.py:310
  44.0 16.4 %collective-permute-start.17 = (bf16[2,384,128]{2,1,0:T(8,128)(2,1)S(1)}, bf16[2,384,128]{2,1,0:T(8,128)(2,1)S(1)}, u32[]{:S(2)}, u32[]{:S(2)}) collective-permute-start(bf16[2,384,128]{2,1,0:T(8,128)(2,1)S(1)} %get-tuple-element.82), channel_id=1, source_target_pairs={{0,6},{2,4},{4,2},{6,0},{1,7},{3,5},{5,3},{7,1},{8,14},{10,12},{12... | collective-permute-start | bytes 589832 | tf_op jit(solution)/shard_map/ppermute | solution.py:310
  45.1 15.4 %collective-permute-start.18 = (bf16[2,384,128]{2,1,0:T(8,128)(2,1)S(1)}, bf16[2,384,128]{2,1,0:T(8,128)(2,1)S(1)}, u32[]{:S(2)}, u32[]{:S(2)}) collective-permute-start(bf16[2,384,128]{2,1,0:T(8,128)(2,1)S(1)} %get-tuple-element.83), channel_id=1, source_target_pairs={{0,2},{2,0},{4,6},{6,4},{1,3},{3,1},{5,7},{7,5},{8,10},{10,8},{12,... | collective-permute-start | bytes 589832 | tf_op jit(solution)/shard_map/ppermute | solution.py:310
  53.2 8.7 %collective-permute-start.23 = (bf16[96,384]{1,0:T(8,128)(2,1)S(1)}, bf16[96,384]{1,0:T(8,128)(2,1)S(1)}, u32[]{:S(2)}, u32[]{:S(2)}) collective-permute-start(bf16[96,384]{1,0:T(8,128)(2,1)S(1)} %get-tuple-element.95), channel_id=1, source_target_pairs={{0,6},{2,4},{4,2},{6,0},{1,7},{3,5},{5,3},{7,1},{8,14},{10,12},{12... | collective-permute-start | bytes 221192 | tf_op jit(solution)/shard_map/ppermute | solution.py:310
  53.6 8.4 %collective-permute-start.22 = (bf16[96,384]{1,0:T(8,128)(2,1)S(1)}, bf16[96,384]{1,0:T(8,128)(2,1)S(1)}, u32[]{:S(2)}, u32[]{:S(2)}) collective-permute-start(bf16[96,384]{1,0:T(8,128)(2,1)S(1)} %get-tuple-element.96), channel_id=1, source_target_pairs={{0,4},{2,6},{4,0},{6,2},{1,5},{3,7},{5,1},{7,3},{8,12},{10,14},{12... | collective-permute-start | bytes 221192 | tf_op jit(solution)/shard_map/ppermute | solution.py:310
  56.4 6.9 %collective-permute-start.21 = (bf16[96,384]{1,0:T(8,128)(2,1)S(1)}, bf16[96,384]{1,0:T(8,128)(2,1)S(1)}, u32[]{:S(2)}, u32[]{:S(2)}) collective-permute-start(bf16[96,384]{1,0:T(8,128)(2,1)S(1)} %get-tuple-element.97), channel_id=1, source_target_pairs={{0,2},{2,0},{4,6},{6,4},{1,3},{3,1},{5,7},{7,5},{8,10},{10,8},{12,... | collective-permute-start | bytes 221192 | tf_op jit(solution)/shard_map/ppermute | solution.py:310
  63.4 1.7 %copy-start = (bf16[2,384,128]{2,1,0:T(8,128)(2,1)S(1)}, bf16[2,384,128]{2,1,0:T(8,128)(2,1)}, u32[]{:S(2)}) copy-start(bf16[2,384,128]{2,1,0:T(8,128)(2,1)} %gate.1) | copy-start | bytes 589828
  63.4 1.7 %copy-start.1 = (bf16[2,384,128]{2,1,0:T(8,128)(2,1)S(1)}, bf16[2,384,128]{2,1,0:T(8,128)(2,1)}, u32[]{:S(2)}) copy-start(bf16[2,384,128]{2,1,0:T(8,128)(2,1)} %cot.1) | copy-start | bytes 589828
  63.4 1.6 %collective-permute-start.24 = (bf16[3,384,128]{2,1,0:T(8,128)(2,1)S(1)}, bf16[3,384,128]{2,1,0:T(8,128)(2,1)S(1)}, u32[]{:S(2)}, u32[]{:S(2)}) collective-permute-start(bf16[3,384,128]{2,1,0:T(8,128)(2,1)S(1)} %pad_maximum_fusion.2), channel_id=1, source_target_pairs={{0,1},{1,0},{2,3},{3,2},{4,5},{5,4},{6,7},{7,6},{8,9},{9,8},{10,11... | collective-permute-start | bytes 884744 | tf_op jit(solution)/shard_map/ppermute | solution.py:310
